TPU v7x, 32 devices: a whole 2x2x4 slice. The times are simulated.
32 devices in a mesh: context: 8 (over y, x, core), tensor: 4 (over z).
Axes of the slice: x: 2, y: 2, z: 4, core: 2. Of those that a mesh axis runs over, the one named last changes fastest.
Arguments:
- queries: bfloat16 [16384, 8192], P('context', 'tensor'), may hold values from -6 to 6
- key_rows: bfloat16 [16384, 8192], P('context', 'tensor'), may hold values from -6 to 6
- value_rows: bfloat16 [16384, 8192], P('context', 'tensor'), may hold values from -200 to 200
- short_filter: float32 [7, 512], P(None, 'tensor'), may hold values from -2 to 2
- medium_filter: bfloat16 [128, 512], P(None, 'tensor'), may hold values from -0.5 to 0.5
- decays: float32 [512, 16], P('tensor'), may hold values from 0 to 1, as said below
- residue: float32 [512, 16], P('tensor'), may hold values from -1.5 to 1.5
- skip_gain: float32 [8192], P('tensor'), may hold values from -1 to 1
- norm_gain: float32 [8192], P('tensor'), may hold values from 0.5 to 1.5
Outputs:
- mixer_out: bfloat16 [16384, 8192], P('context', 'tensor')
Inputs may be any that keep to these rules, and one draw needn't show every extreme that they name: decays lie between 1 / 81920 and 1 / 32.
All inputs are finite; a program needn't handle non-finite values.
Results may differ from a plain program's by a relative error of at most 0.0065.
Values may be sent and summed in bfloat16 or wider, within the bound.
No kernel may reach another device: no remote copies, remote signals or barrier semaphores. Data moves between devices by JAX's collectives and lax.ppermute only.
A program may use at most 192 MiB of HBM per device.

v0:
```python
import math

import jax
import jax.numpy as jnp
from jax import lax
from jax.sharding import PartitionSpec as P

D = 8192
GROUP_CH = 16


HIGH = lax.Precision.HIGHEST


def passed_along(value, axis, steps):
    count = lax.axis_size(axis)
    first, last = (max(0, -steps), min(count, count - steps))
    return lax.ppermute(value, axis, [(source, source + steps) for source in range(first, last)])


def short_conv(gated, prior, short_filter):
    width = short_filter.shape[0]
    rows = gated.shape[0]
    joined = jnp.concatenate([prior, gated], axis=0)
    spread = jnp.repeat(short_filter, GROUP_CH, axis=1)
    total = jnp.zeros_like(gated)
    for delay in range(width):
        begin = width - 1 - delay
        total = total + spread[delay][None, :] * joined[begin : begin + rows]
    return total


def medium_conv(first, prior, medium_filter):
    width, groups = medium_filter.shape
    rows, chans = first.shape
    lead = jnp.concatenate([jnp.zeros((1, chans), first.dtype), prior, first], axis=0).T
    blocks = lead.reshape(groups, GROUP_CH, rows // width + 1, width)
    windows = jnp.concatenate([blocks[:, :, :-1], blocks[:, :, 1:]], axis=3)
    inner = jnp.arange(2 * width)[:, None]
    outer = jnp.arange(width)[None, :]
    offset = outer + width - inner
    onehot = (offset[:, :, None] == jnp.arange(width)[None, None, :]).astype(jnp.bfloat16)
    toeplitz = jnp.einsum(
        "jit,tg->gji", onehot, medium_filter, preferred_element_type=jnp.float32
    ).astype(jnp.bfloat16)
    result = jnp.einsum("gkbj,gji->gkbi", windows, toeplitz, preferred_element_type=jnp.float32)
    return result.reshape(chans, rows)


def block_sums(signal, decays, width):
    steps = jnp.arange(width, dtype=jnp.float32)
    tail = jnp.exp(-decays[:, :, None] * (width - 1 - steps)[None, None, :])
    return jnp.einsum("gkbi,gmi->gkbm", signal, tail, precision=HIGH)


def apply_modes(signal, sums, decays, amplitude):
    groups, inner, count, width = signal.shape
    block_index = jnp.arange(count, dtype=jnp.float32)
    block_gap = block_index[:, None] - 1.0 - block_index[None, :]
    carry = jnp.where(
        block_gap[None, None] >= 0.0,
        jnp.exp(-decays[:, :, None, None] * (jnp.maximum(block_gap, 0.0) * width)[None, None]),
        0.0,
    )
    before = jnp.einsum("gmxy,gkym->gkxm", carry, sums, precision=HIGH)
    steps = jnp.arange(width, dtype=jnp.float32)
    leading = amplitude[:, :, None] * jnp.exp(-decays[:, :, None] * (steps + 1.0)[None, None, :])
    earlier_part = jnp.einsum("gkxm,gmi->gkxi", before, leading, precision=HIGH)
    distance = steps[None, :] - steps[:, None]
    clipped = jnp.maximum(distance, 0.0)
    kernel = jnp.zeros((groups, width, width), jnp.float32)
    for mode in range(decays.shape[1]):
        kernel = kernel + amplitude[:, mode, None, None] * jnp.exp(
            -decays[:, mode, None, None] * clipped[None]
        )
    kernel = jnp.where(distance[None] >= 0.0, kernel, 0.0)
    within = jnp.einsum("gkbj,gji->gkbi", signal, kernel, precision=HIGH)
    return within + earlier_part


def local(
    queries,
    key_rows,
    value_rows,
    short_filter,
    medium_filter,
    decays,
    residue,
    skip_gain,
    norm_gain,
):
    rows, chans = queries.shape
    short_width = short_filter.shape[0]
    medium_width = medium_filter.shape[0]
    kv_prior = passed_along(
        (key_rows[rows - short_width + 1 :], value_rows[rows - short_width + 1 :]), "context", 1
    )
    gated = key_rows.astype(jnp.float32) * value_rows.astype(jnp.float32)
    gated_prior = kv_prior[0].astype(jnp.float32) * kv_prior[1].astype(jnp.float32)
    short = short_conv(gated, gated_prior, short_filter)
    first = (queries.astype(jnp.float32) * short).astype(jnp.bfloat16)
    first_prior = passed_along(first[rows - medium_width + 1 :], "context", 1)
    medium_t = medium_conv(first, first_prior, medium_filter)
    second_t = (key_rows.T.astype(jnp.float32) * medium_t).astype(jnp.bfloat16)
    amplitude = residue * jnp.sqrt(-jnp.expm1(-2.0 * decays))
    spread_t = lax.all_to_all(second_t, "context", split_axis=0, concat_axis=1, tiled=True)
    share, length = spread_t.shape
    groups = share // GROUP_CH
    begin = lax.axis_index("context") * groups
    local_decays = lax.dynamic_slice_in_dim(decays, begin, groups, 0)
    local_amplitude = lax.dynamic_slice_in_dim(amplitude, begin, groups, 0)
    width = math.gcd(length, 256)
    signal = spread_t.astype(jnp.float32).reshape(groups, GROUP_CH, length // width, width)
    sums = block_sums(signal, local_decays, width)
    result = apply_modes(signal, sums, local_decays, local_amplitude).reshape(share, length)
    conv_t = lax.all_to_all(
        result.astype(jnp.bfloat16), "context", split_axis=1, concat_axis=0, tiled=True
    )
    conv = conv_t.T.astype(jnp.float32)
    second = second_t.T.astype(jnp.float32)
    mixed = value_rows.astype(jnp.float32) * (conv + skip_gain[None, :] * second)
    energy = lax.psum(jnp.sum(mixed * mixed, axis=1), "tensor")
    scale = lax.rsqrt(energy / D + 1e-06)
    return (mixed * scale[:, None] * norm_gain[None, :]).astype(jnp.bfloat16)


def solution(mesh):
    return jax.shard_map(
        local,
        mesh=mesh,
        in_specs=(
            P("context", "tensor"),
            P("context", "tensor"),
            P("context", "tensor"),
            P(None, "tensor"),
            P(None, "tensor"),
            P("tensor", None),
            P("tensor", None),
            P("tensor"),
            P("tensor"),
        ),
        out_specs=P("context", "tensor"),
        check_vma=False,
    )
```

profile of v0, /device:TPU:0, one launch (start us, length us, event | category | flops | bytes accessed | tf_op | source)
XLA Modules:
  0.0 623.7 jit_solution(8991005513683465911)
XLA Ops:
  8.5 12.3 %convert_multiply_fusion = f32[2048,2048]{1,0:T(8,128)} fusion(bf16[2048,2048]{1,0:T(8,128)(2,1)} %param.10, bf16[2048,2048]{1,0:T(8,128)(2,1)} %param.11), kind=kLoop, calls=%fused_computation.5 | loop fusion | flops 12582912 | bytes 33554432 | tf_op jit(solution)/shard_map/mul | solution.py:98
  22.0 43.9 %fusion.7 = bf16[2048,2048]{1,0:T(8,128)(2,1)} fusion(f32[6,2048]{1,0:T(8,128)S(1)} %convert_multiply_fusion.2, f32[2048,2048]{1,0:T(8,128)} %convert_multiply_fusion, bf16[2048,2048]{1,0:T(8,128)(2,1)} %param.9, f32[2048]{0:T(1024)S(1)} %broadcast_in_dim.106, f32[2048]{0:T(1024)S(1)} %broadcast_in_dim.104, f32[2048]{0:T(1024)S(1)} %broadcast_in_dim.102, ...), kind=kLoop, calls=%fused_computation.15 | loop fusion | flops 92274688 | bytes 33660928 | tf_op jit(solution)/shard_map/convert_element_type | solution.py:101
  77.7 12.0 %copy.36 = bf16[128,256,128,1]{2,1,3,0:T(8,128)(2,1)} copy(bf16[128,256,128,1]{0,2,1,3:T(8,128)(2,1)} %convert_bitcast_fusion.1) | data formatting | bytes 16777216 | tf_op jit(solution)/shard_map/convert_element_type | solution.py:45
  89.7 39.1 %concatenate.10 = bf16[2176,2048]{1,0:T(8,128)(2,1)} concatenate(bf16[1,2048]{1,0:T(2,128)(2,1)S(1)} %broadcast_in_dim.92, bf16[127,2048]{1,0:T(8,128)(2,1)S(1)} %collective-permute-done.2, bf16[2048,2048]{1,0:T(8,128)(2,1)} %fusion.7), dimensions={0} | concatenate | bytes 17825792 | tf_op jit(solution)/shard_map/concatenate | solution.py:36
  128.8 11.7 %copy.24 = bf16[2048,2176]{1,0:T(8,128)(2,1)} copy(bf16[2048,2176]{0,1:T(8,128)(2,1)} %bitcast.132) | data formatting | bytes 17825792 | tf_op jit(solution)/shard_map/transpose | solution.py:36
  140.5 16.3 %reshape.303 = bf16[128,16,17,128]{3,2,1,0:T(8,128)(2,1)} reshape(bf16[2048,2176]{1,0:T(8,128)(2,1)} %copy.24) | data formatting | bytes 17825792 | tf_op jit(solution)/shard_map/reshape | solution.py:37
  156.8 14.0 %fusion.180 = (bf16[128,16,16,128]{3,2,1,0:T(8,128)(2,1)}, bf16[128,16,16,128]{3,2,1,0:T(8,128)(2,1)}) fusion(bf16[128,16,17,128]{3,2,1,0:T(8,128)(2,1)} %reshape.303), kind=kLoop, calls=%fused_computation.245 | loop fusion | bytes 33554432 | tf_op jit(solution)/shard_map/slice | solution.py:38
  170.8 14.0 %fusion.21 = f32[128,16,16,128]{3,2,1,0:T(8,128)} fusion(bf16[128,256,128,1]{2,1,3,0:T(8,128)(2,1)} %copy.36, bf16[128,16,16,128]{3,2,1,0:T(8,128)(2,1)} %get-tuple-element.6, bf16[128,16,16,128]{3,2,1,0:T(8,128)(2,1)} %get-tuple-element.5), kind=kOutput, calls=%fused_computation.34 | convolution fusion | flops 2181038080 | bytes 41943040 | tf_op jit(solution)/shard_map/gkbj,gji->gkbi/dot_general | solution.py:46
  184.8 15.7 %copy.50 = f32[256,8,16,128]{3,1,2,0:T(8,128)} copy(f32[256,8,16,128]{3,2,1,0:T(8,128)} %bitcast.134) | data formatting | bytes 33554432
  200.5 17.6 %copy.26 = f32[2048,2048]{0,1:T(8,128)} copy(f32[2048,2048]{1,0:T(8,128)} %bitcast.130) | data formatting | bytes 33554432 | tf_op jit(solution)/shard_map/reshape | solution.py:47
  218.1 12.0 %fusion.1 = bf16[2048,2048]{0,1:T(8,128)(2,1)} fusion(f32[2048,2048]{0,1:T(8,128)} %copy.26, bf16[2048,2048]{1,0:T(8,128)(2,1)} %param.10), kind=kLoop, calls=%fused_computation.9 | loop fusion | flops 12582912 | bytes 33554432 | tf_op jit(solution)/shard_map/convert_element_type | solution.py:104
  230.1 12.3 %copy.27 = bf16[2048,2048]{1,0:T(8,128)(2,1)} copy(bf16[2048,2048]{0,1:T(8,128)(2,1)} %fusion.1) | data formatting | bytes 16777216 | tf_op jit(solution)/shard_map/convert_element_type | solution.py:104
  248.4 93.3 %all-to-all-done = bf16[8,256,2048]{2,1,0:T(8,128)(2,1)} async-done(((bf16[8,256,2048]{2,1,0:T(8,128)(2,1)}), bf16[8,256,2048]{2,1,0:T(8,128)(2,1)}, u32[]{:S(2)}, u32[]{:S(2)}) %all-to-all-start) | async-done | bytes 8388640 | tf_op jit(solution)/shard_map/all_to_all | solution.py:106
  353.0 13.5 %reshape.305 = bf16[16,16,64,256]{3,2,1,0:T(8,128)(2,1)} reshape(bf16[256,8,2048]{2,1,0:T(8,128)(2,1)} %copy.28) | data formatting | bytes 16777216 | tf_op jit(solution)/shard_map/reshape | solution.py:113
  366.5 13.5 %fusion.144 = f32[16,16,64,16]{2,3,1,0:T(8,128)S(1)} fusion(bf16[16,16,64,256]{3,2,1,0:T(8,128)(2,1)} %reshape.305, f32[256]{0:T(256)S(1)} %iota_subtract_fusion.3, f32[16,16]{1,0:T(8,128)S(1)} %copy.29), kind=kOutput, calls=%fused_computation.158 | convolution fusion | flops 805371904 | bytes 9439232 | tf_op jit(solution)/shard_map/gkbi,gmi->gkbm/dot_general | solution.py:53
  380.1 13.6 %fusion.138 = f32[16,16,64,16]{2,1,3,0:T(8,128)S(1)} fusion(f32[64,64]{1,0:T(8,128)S(1)} %maximum_multiply_fusion, f32[16,16]{1,0:T(8,128)S(1)} %copy.29, pred[64,64]{1,0:T(8,128)(4,1)S(1)} %fusion.159, f32[16,16,64,16]{2,3,1,0:T(8,128)S(1)} %fusion.144), kind=kOutput, calls=%fused_computation.156 | convolution fusion | flops 203423744 | bytes 2118656 | tf_op jit(solution)/shard_map/gmxy,gkym->gkxm/dot_general | solution.py:65
  393.7 19.8 %fusion.31 = f32[16,16,64,256]{3,2,1,0:T(8,128)S(1)} fusion(bf16[16,16,64,256]{3,2,1,0:T(8,128)(2,1)S(1)} %copy-done.2, f32[16]{0:T(128)S(1)} %get-tuple-element.40, f32[16]{0:T(128)S(1)} %get-tuple-element.10, f32[16]{0:T(128)S(1)} %get-tuple-element.26, f32[16]{0:T(128)S(1)} %get-tuple-element.11, f32[16]{0:T(128)S(1)} %get-tuple-element.27, ...), kind=kOutput, calls=%fused_computation.49 | convolution fusion | flops 12935233536 | bytes 25495552 | tf_op jit(solution)/shard_map/gkbj,gji->gkbi/dot_general | solution.py:77
  413.4 16.8 %add_convert_fusion = bf16[16,16,64,256]{3,2,1,0:T(8,128)(2,1)} fusion(f32[16,16,64,256]{3,2,1,0:T(8,128)S(1)} %fusion.31, f32[16,16,64,16]{2,1,3,0:T(8,128)S(1)} %fusion.138, f32[256]{0:T(256)S(1)} %iota_add_fusion, f32[16,16]{1,0:T(8,128)S(1)} %copy.32, f32[16,16]{1,0:T(8,128)S(1)} %copy.29), kind=kOutput, calls=%fused_computation.40 | convolution fusion | flops 813826048 | bytes 26217472 | tf_op jit(solution)/shard_map/gkxm,gmi->gkxi/dot_general | solution.py:68
  430.2 13.5 %convert_element_type.72 = bf16[256,8,2048]{2,1,0:T(8,128)(2,1)} reshape(bf16[16,16,64,256]{3,2,1,0:T(8,128)(2,1)} %add_convert_fusion) | data formatting | bytes 16777216 | tf_op jit(solution)/shard_map/convert_element_type | solution.py:117
  455.0 100.0 %all_to_all.26 = bf16[256,8,2048]{2,0,1:T(8,128)(2,1)} all-to-all(bf16[256,8,2048]{2,0,1:T(8,128)(2,1)} %copy.34), channel_id=1, replica_groups=mesh['context'=8,'tensor'=4] {'context'}, dimensions={1} | all-to-all | bytes 16777216 | tf_op jit(solution)/shard_map/all_to_all | solution.py:116
  566.2 17.7 %copy.35 = f32[2048,2048]{0,1:T(8,128)} copy(f32[2048,2048]{1,0:T(8,128)} %bitcast.131) | data formatting | bytes 33554432 | tf_op jit(solution)/shard_map/convert_element_type | solution.py:119
  583.9 12.1 %multiply_reduce_fusion = f32[2048]{0:T(1024)S(1)} fusion(f32[2048,2048]{0,1:T(8,128)} %copy.35, bf16[2048,2048]{0,1:T(8,128)(2,1)} %fusion.1, f32[2048]{0:T(1024)S(1)} %copy-done.4, bf16[2048,2048]{1,0:T(8,128)(2,1)} %param.11), kind=kLoop, calls=%fused_computation.39 | loop fusion | flops 29358080 | bytes 33570816 | tf_op jit(solution)/shard_map/reduce_sum | solution.py:122
  596.0 12.1 %psum.7 = f32[2048]{0:T(1024)S(1)} all-reduce(f32[2048]{0:T(1024)S(1)} %multiply_reduce_fusion), channel_id=1, replica_groups=mesh['context'=8,'tensor'=4] {'tensor'}, use_global_device_ids=true, to_apply=%region_1.2 | all-reduce | flops 2048 | bytes 16384 | tf_op jit(solution)/shard_map/psum | solution.py:122
  608.1 15.3 %multiply_convert_fusion = bf16[2048,2048]{1,0:T(8,128)(2,1)} fusion(f32[2048]{0:T(1024)S(1)} %copy-done.6, f32[2048]{0:T(1024)S(1)} %add_rsqrt_fusion, f32[2048,2048]{0,1:T(8,128)} %copy.35, bf16[2048,2048]{0,1:T(8,128)(2,1)} %fusion.1, f32[2048]{0:T(1024)S(1)} %copy-done.4, bf16[2048,2048]{1,0:T(8,128)(2,1)} %param.11), kind=kLoop, calls=%fused_computation.38 | loop fusion | flops 33554432 | bytes 41967616 | tf_op jit(solution)/shard_map/convert_element_type | solution.py:124
  (62 shorter events, 61.1 us)
Async XLA Ops:
  0.0 69.2 %copy-start = (bf16[128,128]{1,0:T(8,128)(2,1)S(1)}, bf16[128,128]{1,0:T(8,128)(2,1)}, u32[]{:S(2)}) copy-start(bf16[128,128]{1,0:T(8,128)(2,1)} %param.13) | copy-start | bytes 98308
  0.8 21.2 %collective-permute-start = (bf16[6,2048]{1,0:T(8,128)(2,1)S(1)}, bf16[6,2048]{1,0:T(8,128)(2,1)S(1)}, u32[]{:S(2)}, u32[]{:S(2)}) collective-permute-start(bf16[6,2048]{1,0:T(8,128)(2,1)S(1)} %slice.182), channel_id=1, source_target_pairs={{0,4},{4,8},{8,12},{12,16},{16,20},{20,24},{24,28},{1,5},{5,9},{9,... | collective-permute-start | bytes 73736 | tf_op jit(solution)/shard_map/ppermute | solution.py:18
  3.9 16.9 %copy-start.7 = (f32[7,128]{1,0:T(8,128)S(1)}, f32[7,128]{1,0:T(8,128)}, u32[]{:S(2)}) copy-start(f32[7,128]{1,0:T(8,128)} %param.12) | copy-start | bytes 10756
  3.9 18.1 %collective-permute-start.1 = (bf16[6,2048]{1,0:T(8,128)(2,1)S(1)}, bf16[6,2048]{1,0:T(8,128)(2,1)S(1)}, u32[]{:S(2)}, u32[]{:S(2)}) collective-permute-start(bf16[6,2048]{1,0:T(8,128)(2,1)S(1)} %slice.183), channel_id=1, source_target_pairs={{0,4},{4,8},{8,12},{12,16},{16,20},{20,24},{24,28},{1,5},{5,9},{9,... | collective-permute-start | bytes 73736 | tf_op jit(solution)/shard_map/ppermute | solution.py:18
  67.1 22.6 %collective-permute-start.2 = (bf16[127,2048]{1,0:T(8,128)(2,1)S(1)}, bf16[127,2048]{1,0:T(8,128)(2,1)S(1)}, u32[]{:S(2)}, u32[]{:S(2)}) collective-permute-start(bf16[127,2048]{1,0:T(8,128)(2,1)S(1)} %slice.245), channel_id=1, source_target_pairs={{0,4},{4,8},{8,12},{12,16},{16,20},{20,24},{24,28},{1,5},{5,9},{9,... | collective-permute-start | bytes 1560584 | tf_op jit(solution)/shard_map/ppermute | solution.py:18
  242.4 5.3 copy-start.3
  242.4 5.3 copy-start.5
  242.4 99.4 %all-to-all-start = ((bf16[8,256,2048]{2,1,0:T(8,128)(2,1)}), bf16[8,256,2048]{2,1,0:T(8,128)(2,1)}, u32[]{:S(2)}, u32[]{:S(2)}) async-start(bf16[8,256,2048]{2,1,0:T(8,128)(2,1)} %bitcast.133), calls=%async_computation | async-start | bytes 16777216 | tf_op jit(solution)/shard_map/all_to_all | solution.py:106
  366.5 27.1 %copy-start.2 = (bf16[16,16,64,256]{3,2,1,0:T(8,128)(2,1)S(1)}, bf16[16,16,64,256]{3,2,1,0:T(8,128)(2,1)}, u32[]{:S(2)}) copy-start(bf16[16,16,64,256]{3,2,1,0:T(8,128)(2,1)} %reshape.305) | copy-start | bytes 25165828
  566.2 17.7 %copy-start.4 = (f32[2048]{0:T(1024)S(1)}, f32[2048]{0:T(1024)}, u32[]{:S(2)}) copy-start(f32[2048]{0:T(1024)} %param.16) | copy-start | bytes 24580
  583.9 24.2 %copy-start.6 = (f32[2048]{0:T(1024)S(1)}, f32[2048]{0:T(1024)}, u32[]{:S(2)}) copy-start(f32[2048]{0:T(1024)} %param.17) | copy-start | bytes 24580
  608.1 15.3 %copy-start.1 = (bf16[128,128]{1,0:T(8,128)(2,1)S(1)}, bf16[128,128]{1,0:T(8,128)(2,1)}, u32[]{:S(2)}) copy-start(bf16[128,128]{1,0:T(8,128)(2,1)} %param.13) | copy-start | bytes 98308
where the time goes:
time: 632 us; the launch traced here: 624 us
  local copies, waits for them, and re-layouts  210 us (33%)
  blocking collectives  112 us (18%)
  other arithmetic  107 us (17%)
  waiting for transfers between devices  93.3 us (15%)
  matrix products  86.1 us (14%)
  starting transfers between devices  14.3 us (2%)
    all_to_all x1, blocking collectives, local(): lax.all_to_all(result.astype(jnp.bfloat16), 'context', split_axis=1, conc...  100 us
    all_to_all x1, waiting for transfers between devices, local(): lax.all_to_all(second_t, 'context', split_axis=0, concat_axis=1, tiled=True)  93.3 us
    convert_element_type x1, other arithmetic, local(): first = (queries.astype(jnp.float32) * short).astype(jnp.bfloat16)  43.9 us
    concatenate x1, local copies, waits for them, and re-layouts, medium_conv(): jnp.concatenate([jnp.zeros((1, chans), first.dtype), prior, first], axis=0)  39.1 us
    convert_element_type x2, local copies, waits for them, and re-layouts, local(): result.astype(jnp.bfloat16)  24.8 us
    dot_general x1, matrix products, apply_modes(): within = jnp.einsum('gkbj,gji->gkbi', signal, kernel, precision=HIGH)  19.8 us
    convert_element_type x1, local copies, waits for them, and re-layouts, local(): conv = conv_t.T.astype(jnp.float32)  17.7 us
    reshape x1, local copies, waits for them, and re-layouts, medium_conv(): return result.reshape(chans, rows)  17.6 us
  transfers between devices with their start and end apart: 4, of which 1 were waited for; matrix products, arithmetic and copies ran while one was open for 6% of the time, Pallas kernels for 0%

commit v1 on v0

v1 whole, which is shorter than its diff:
```python
import functools

import jax
import jax.numpy as jnp
from jax import lax
from jax.experimental import pallas as pl
from jax.experimental.pallas import tpu as pltpu
from jax.sharding import PartitionSpec as P

GROUP_CH = 16
LANES = 128
PACK = LANES // GROUP_CH
WIDE = 256
F32 = jnp.float32
BF16 = jnp.bfloat16


def split2(value):
    high = value.astype(BF16)
    return high, (value - high.astype(F32)).astype(BF16)


def passed_along(value, axis, steps):
    count = lax.axis_size(axis)
    return lax.ppermute(value, axis, [(source, source + steps) for source in range(count - steps)])


def mix_kernel(q, k, v, halo, short_taps, medium_taps, profile, tail_high, tail_low, lead_high,
               lead_low, block_decay, skip, y_out, state_out, gated, first_t, key_t, y_t, ends):
    rows = q.shape[0]
    modes = tail_high.shape[0] // PACK
    gated[0:8, :] = halo[LANES:LANES + 8, :].astype(F32) + halo[LANES + 8:LANES + 16, :].astype(F32)
    first_t[:, 0:LANES] = halo[0:LANES, :].T
    for begin in range(0, rows, WIDE):
        part = pl.ds(begin, WIDE)
        gated[pl.ds(begin + 8, WIDE), :] = k[part, :].astype(F32) * v[part, :].astype(F32)
    taps = short_taps[...]
    for begin in range(0, rows, WIDE):
        part = pl.ds(begin, WIDE)
        total = taps[0:1, :] * gated[pl.ds(begin + 8, WIDE), :]
        for delay in range(1, 7):
            total = total + taps[delay:delay + 1, :] * gated[pl.ds(begin + 8 - delay, WIDE), :]
        first = (q[part, :].astype(F32) * total).astype(BF16)
        first_t[:, begin + LANES:begin + LANES + WIDE] = first.T
        key_t[:, begin:begin + WIDE] = k[part, :].T
    skip_t = jnp.broadcast_to(skip[...], (LANES, LANES)).T
    row_i = lax.broadcasted_iota(jnp.int32, (LANES, LANES), 0)
    col_i = lax.broadcasted_iota(jnp.int32, (LANES, LANES), 1)
    causal = col_i >= row_i
    zero = jnp.zeros((LANES, LANES), BF16)
    halves = rows // LANES
    blocks = rows // WIDE
    lane = lax.broadcasted_iota(jnp.int32, (rows // WIDE * GROUP_CH, LANES), 1)
    pad = jnp.zeros((LANES - 6 * modes, WIDE), BF16)
    pad_lead = jnp.zeros((LANES - 3 * modes, WIDE), BF16)
    for g in range(PACK):
        chans = pl.ds(g * GROUP_CH, GROUP_CH)
        mode_rows = pl.ds(g * modes, modes)
        turned = pltpu.roll(jnp.broadcast_to(medium_taps[g:g + 1, :].astype(F32), (LANES, LANES)),
                            0, 1, stride=1, stride_axis=0)
        medium_w = jnp.concatenate(
            [jnp.where(causal, 0.0, turned), jnp.where(causal, turned, 0.0)], axis=0).astype(BF16)
        window = jnp.concatenate(
            [first_t[chans, b * LANES:(b + 2) * LANES] for b in range(halves)], axis=0)
        medium = jnp.dot(window, medium_w, preferred_element_type=F32)
        key = jnp.concatenate(
            [key_t[chans, b * LANES:(b + 1) * LANES] for b in range(halves)], axis=0)
        second = (key.astype(F32) * medium).astype(BF16)
        second = jnp.concatenate(
            [jnp.concatenate([second[2 * b * GROUP_CH:(2 * b + 1) * GROUP_CH],
                              second[(2 * b + 1) * GROUP_CH:(2 * b + 2) * GROUP_CH]], axis=1)
             for b in range(blocks)], axis=0)
        tails = jnp.concatenate([tail_high[mode_rows, :]] * 3 + [tail_low[mode_rows, :]] * 3 + [pad], axis=0)
        sums = lax.dot_general(second, tails, (((1,), (1,)), ((), ())), preferred_element_type=F32)
        sums = sums + pltpu.roll(sums, LANES - 3 * modes, 1)
        decay = block_decay[g:g + 1, :]
        state = jnp.zeros((GROUP_CH, LANES), F32)
        states = []
        for b in range(blocks):
            states.append(state)
            state = decay * state + sums[b * GROUP_CH:(b + 1) * GROUP_CH, :]
        ends[chans, :] = state
        high, low = split2(jnp.concatenate(states, axis=0))
        carried = jnp.where((lane >= modes) & (lane < 2 * modes), low, high)
        carried = jnp.where(lane < 3 * modes, carried, jnp.zeros_like(carried))
        leads = jnp.concatenate(
            [lead_high[mode_rows, :], lead_high[mode_rows, :], lead_low[mode_rows, :], pad_lead], axis=0)
        turned = pltpu.roll(jnp.broadcast_to(profile[g:g + 1, :], (LANES, WIDE)), 0, 1, stride=1, stride_axis=0)
        near = jnp.where(causal, turned[:, :LANES], 0.0).astype(BF16)
        long_w = jnp.concatenate(
            [jnp.concatenate([near, turned[:, LANES:].astype(BF16)], axis=1),
             jnp.concatenate([zero, near], axis=1)], axis=0)
        y = jnp.dot(second, long_w, preferred_element_type=F32)
        y = y + jnp.dot(carried, leads, preferred_element_type=F32)
        gain = skip_t[g * GROUP_CH:(g + 1) * GROUP_CH, :]
        gain = jnp.concatenate([jnp.concatenate([gain, gain], axis=1)] * blocks, axis=0)
        y = (y + gain * second.astype(F32)).astype(BF16)
        for b in range(blocks):
            y_t[chans, b * WIDE:(b + 1) * WIDE] = y[b * GROUP_CH:(b + 1) * GROUP_CH, :]
    for begin in range(0, rows, WIDE):
        y_out[pl.ds(begin, WIDE), :] = y_t[:, begin:begin + WIDE].T
    state_out[...] = ends[...].T[:modes, :]


def mix(q, k, v, halo, short_taps, medium_taps, profile, tails, leads, block_decay, skip):
    rows, chans = q.shape
    modes = tails[0].shape[0] * GROUP_CH // chans
    grid = (chans // LANES,)
    column = lambda height: pl.BlockSpec((height, LANES), lambda i: (0, i))
    down = lambda height, width: pl.BlockSpec((height, width), lambda i: (i, 0))
    return pl.pallas_call(
        mix_kernel,
        grid=grid,
        out_shape=(jax.ShapeDtypeStruct((rows, chans), BF16), jax.ShapeDtypeStruct((modes, chans), F32)),
        in_specs=[column(rows)] * 3 + [
            column(halo.shape[0]), column(8), down(PACK, LANES), down(PACK, WIDE),
            down(PACK * modes, WIDE), down(PACK * modes, WIDE), down(PACK * modes, WIDE),
            down(PACK * modes, WIDE), down(PACK, LANES), column(1)],
        out_specs=(column(rows), column(modes)),
        scratch_shapes=[
            pltpu.VMEM((rows + 8, LANES), F32),
            pltpu.VMEM((LANES, rows + LANES), BF16),
            pltpu.VMEM((LANES, rows), BF16),
            pltpu.VMEM((LANES, rows), BF16),
            pltpu.VMEM((LANES, LANES), F32),
        ],
        compiler_params=pltpu.CompilerParams(vmem_limit_bytes=40 << 20),
        cost_estimate=pl.CostEstimate(flops=8 * rows * chans * WIDE, bytes_accessed=8 * rows * chans, transcendentals=0),
        name="mix",
    )(q, k, v, halo, short_taps, medium_taps, profile, *tails, *leads, block_decay, skip)


def join_kernel(y, v, states, weights, decay_row, state_amp, mixed_out, energy_out, energy):
    rows = y.shape[0]
    modes = state_amp.shape[0]
    step = pl.program_id(0)
    count = states.shape[0]
    entry = jnp.zeros((modes, LANES), F32)
    for source in range(count):
        entry = entry + weights[source] * states[source]
    entry = entry * state_amp[...]
    lane = lax.broadcasted_iota(jnp.int32, (modes, LANES), 1) // GROUP_CH
    spread = jnp.concatenate([jnp.where(lane == g, entry, 0.0) for g in range(PACK)], axis=0)
    entry_w = jnp.concatenate(split2(spread), axis=0)
    rate = decay_row[...]
    time = lax.broadcasted_iota(jnp.int32, (LANES, LANES), 0).astype(F32) + 1.0
    lead = jnp.exp(-rate * time)
    fade = jnp.exp(-rate * float(LANES))
    for begin in range(0, rows, LANES):
        part = pl.ds(begin, LANES)
        lead16 = lead.astype(BF16)
        carried = jnp.dot(jnp.concatenate([lead16, lead16], axis=1), entry_w, preferred_element_type=F32)
        mixed = v[part, :].astype(F32) * (y[part, :].astype(F32) + carried)
        mixed_out[part, :] = mixed.astype(BF16)
        square = mixed * mixed

        @pl.when(step == 0)
        def _():
            energy[part, :] = square

        @pl.when(step > 0)
        def _():
            energy[part, :] += square

        lead = lead * fade

    @pl.when(step == pl.num_programs(0) - 1)
    def _():
        for begin in range(0, rows, LANES):
            energy_out[:, begin:begin + LANES] = jnp.sum(energy[pl.ds(begin, LANES), :].T, axis=0, keepdims=True)


def join(y, v, states, weights, decay_row, state_amp):
    rows, chans = y.shape
    count, modes, _ = states.shape
    column = lambda height: pl.BlockSpec((height, LANES), lambda i: (0, i))
    deep = pl.BlockSpec((count, modes, LANES), lambda i: (0, 0, i))
    return pl.pallas_call(
        join_kernel,
        grid=(chans // LANES,),
        out_shape=(jax.ShapeDtypeStruct((rows, chans), BF16), jax.ShapeDtypeStruct((1, rows), F32)),
        in_specs=[column(rows), column(rows), deep, deep, column(1), column(modes)],
        out_specs=(column(rows), pl.BlockSpec((1, rows), lambda i: (0, 0))),
        scratch_shapes=[pltpu.VMEM((rows, LANES), F32)],
        compiler_params=pltpu.CompilerParams(vmem_limit_bytes=40 << 20),
        cost_estimate=pl.CostEstimate(flops=2 * rows * chans * WIDE, bytes_accessed=6 * rows * chans, transcendentals=0),
        name="join",
    )(y, v, states, weights, decay_row, state_amp)


def local(queries, key_rows, value_rows, short_filter, medium_filter, decays, residue, skip_gain,
          norm_gain, width):
    rows, chans = queries.shape
    groups, modes = decays.shape
    taps = short_filter.shape[0]
    short_taps = jnp.pad(jnp.repeat(short_filter, GROUP_CH, axis=1), ((0, 8 - taps), (0, 0)))
    near = rows - LANES
    gated = key_rows[near - 8:].astype(F32) * value_rows[near - 8:].astype(F32)
    total = jnp.zeros((LANES, chans), F32)
    for delay in range(taps):
        total = total + short_taps[delay][None, :] * gated[8 - delay:8 - delay + LANES]
    first = (queries[near:].astype(F32) * total).astype(BF16)
    halo = passed_along(jnp.concatenate([first, *split2(gated[LANES:])], axis=0), "context", 1)

    amplitude = residue * jnp.sqrt(-jnp.expm1(-2.0 * decays))
    time = jnp.arange(WIDE, dtype=F32)
    fade = jnp.exp(-decays[:, :, None] * time[None, None, :])
    profile = jnp.sum(amplitude[:, :, None] * fade, axis=1)
    tails = split2(jnp.exp(-decays[:, :, None] * (WIDE - 1 - time)[None, None, :]).reshape(groups * modes, WIDE))
    leads = split2((amplitude[:, :, None] * jnp.exp(-decays[:, :, None] * (time + 1.0)[None, None, :])).reshape(groups * modes, WIDE))
    block_decay = jnp.pad(jnp.tile(jnp.exp(-decays * WIDE), (1, 3)), ((0, 0), (0, LANES - 3 * modes)))
    y, state = mix(queries, key_rows, value_rows, halo, short_taps, medium_filter.T, profile, tails,
                   leads, block_decay, skip_gain[None, :])
    states = lax.all_gather(state, "context")
    count = lax.axis_size("context")
    gap = (lax.axis_index("context") - 1 - jnp.arange(count)).astype(F32)
    rate = jnp.repeat(decays.T, GROUP_CH, axis=1)
    weights = jnp.where(gap[:, None, None] >= 0.0,
                        jnp.exp(-rate[None] * (jnp.maximum(gap, 0.0) * rows)[:, None, None]), 0.0)
    state_amp = jnp.repeat(amplitude.T, GROUP_CH, axis=1)
    mixed, energy = join(y, value_rows, states, weights, decays.reshape(1, groups * modes), state_amp)
    energy = lax.psum(energy, "tensor")
    scale = lax.rsqrt(energy[0] / width + 1e-06)
    return (mixed.astype(F32) * scale[:, None] * norm_gain[None, :]).astype(BF16)


def solution(mesh):
    def whole(*args):
        return jax.shard_map(
            functools.partial(local, width=args[0].shape[1]),
            mesh=mesh,
            in_specs=(
                P("context", "tensor"),
                P("context", "tensor"),
                P("context", "tensor"),
                P(None, "tensor"),
                P(None, "tensor"),
                P("tensor", None),
                P("tensor", None),
                P("tensor"),
                P("tensor"),
            ),
            out_specs=P("context", "tensor"),
            check_vma=False,
        )(*args)

    return whole
```

time: 632 us -> 193 us (0.31); the launches traced: 624 us -> 192 us
  local copies, waits for them, and re-layouts: 210 us -> 13.3 us
  Pallas kernels: 0 us -> 107 us
  blocking collectives: 112 us -> 11.8 us
  other arithmetic: 107 us -> 14.2 us
  matrix products: 86.1 us -> 0 us
  waiting for transfers between devices: 93.3 us -> 29.9 us
  between operations: 0.51 us -> 13.7 us
  starting transfers between devices: 14.3 us -> 2.4 us
    pallas_call x0 -> x2, Pallas kernels: none -> 107 us  [the longest x1 57.9 us: mix(): pl.pallas_call(mix_kernel, grid=grid, out_shape=(jax.ShapeDtypeStruct((ro...]
    all_to_all x1 -> x0, blocking collectives: 100 us -> none  [local(): lax.all_to_all(result.astype(jnp.bfloat16), 'context', split_axis=1, conc...]
    all_to_all x1 -> x0, waiting for transfers between devices: 93.3 us -> none  [local(): lax.all_to_all(second_t, 'context', split_axis=0, concat_axis=1, tiled=True)]
    dot_general x6 -> x0, matrix products: 86.1 us -> none  [the longest x1 19.8 us: apply_modes(): within = jnp.einsum('gkbj,gji->gkbi', signal, kernel, precision=HIGH)]
    convert_element_type x4, other arithmetic: 82.4 us -> 11.7 us  [the longest x1 8.74 us: local(): (mixed.astype(F32) * scale[:, None] * norm_gain[None, :]).astype(BF16)]
    convert_element_type x5 -> x0, local copies, waits for them, and re-layouts: 66.7 us -> none  [the longest x2 24.8 us: local(): result.astype(jnp.bfloat16)]
    reshape x3, local copies, waits for them, and re-layouts: 47.5 us -> 0.97 us  [the longest x1 0.63 us: local(): state_amp = jnp.repeat(amplitude.T, GROUP_CH, axis=1)]
    concatenate x1 -> x0, local copies, waits for them, and re-layouts: 39.1 us -> none  [medium_conv(): jnp.concatenate([jnp.zeros((1, chans), first.dtype), prior, first], axis=0)]
  transfers between devices with their start and end apart: 4 -> 2, of which waited for: 1 -> 1; matrix products, arithmetic and copies ran while one was open for 6% -> 3% of each run, Pallas kernels for 0% -> 0%
where the time goes in v1:
time: 193 us; the launch traced here: 192 us
  Pallas kernels  107 us (55%)
  waiting for transfers between devices  29.9 us (15%)
  other arithmetic  14.2 us (7%)
  between operations  13.7 us (7%)
  local copies, waits for them, and re-layouts  13.3 us (7%)
  blocking collectives  11.8 us (6%)
  starting transfers between devices  2.4 us (1%)
    pallas_call x1, Pallas kernels, mix(): pl.pallas_call(mix_kernel, grid=grid, out_shape=(jax.ShapeDtypeStruct((ro...  57.9 us
    pallas_call x1, Pallas kernels, join(): pl.pallas_call(join_kernel, grid=(chans // LANES,), out_shape=(jax.ShapeD...  49.3 us
    all_gather x1, waiting for transfers between devices, local(): states = lax.all_gather(state, 'context')  29.8 us
    psum x1, blocking collectives, local(): energy = lax.psum(energy, 'tensor')  11.8 us
    convert_element_type x1, other arithmetic, local(): (mixed.astype(F32) * scale[:, None] * norm_gain[None, :]).astype(BF16)  8.74 us
    unnamed x20, local copies, waits for them, and re-layouts  8.26 us
  transfers between devices with their start and end apart: 2, of which 1 were waited for; matrix products, arithmetic and copies ran while one was open for 3% of the time, Pallas kernels for 0%

profile of v1, /device:TPU:0, one launch (start us, length us, event | category | flops | bytes accessed | tf_op | source)
XLA Modules:
  0.0 192.4 jit_solution(8310136101480254850)
XLA Ops:
  6.5 0.9 slice_bitcast_fusion.6
  8.7 1.4 convert_multiply_fusion
  10.1 2.0 %fusion.4 = bf16[128,2048]{1,0:T(8,128)(2,1)S(1)} fusion(f32[136,2048]{1,0:T(8,128)S(1)} %convert_multiply_fusion, f32[2048]{0:T(1024)S(1)} %broadcast_in_dim.77, f32[2048]{0:T(1024)S(1)} %broadcast_in_dim.75, f32[2048]{0:T(1024)S(1)} %broadcast_in_dim.73, f32[2048]{0:T(1024)S(1)} %broadcast_in_dim.71, f32[2048]{0:T(1024)S(1)} %broadcast_in_dim.69, ...), kind=kLoop, calls=%fused_computation.12 | loop fusion | flops 4194304 | bytes 8445952 | tf_op jit(solution)/shard_map/convert_element_type | solution.py:202
  12.1 2.4 %collective-permute-start = (bf16[144,2048]{1,0:T(8,128)(2,1)S(1)}, bf16[144,2048]{1,0:T(8,128)(2,1)S(1)}, u32[]{:S(2)}, u32[]{:S(2)}) collective-permute-start(bf16[144,2048]{1,0:T(8,128)(2,1)S(1)} %pad_maximum_fusion), channel_id=1, source_target_pairs={{0,4},{4,8},{8,12},{12,16},{16,20},{20,24},{24,28},{1,5},{5,9},{9,... | collective-permute-start | bytes 1769480 | tf_op jit(solution)/shard_map/ppermute | solution.py:25
  14.6 0.1 copy.24
  14.8 0.8 multiply_reduce_fusion.profile
  15.8 0.1 copy.22
  16.0 0.2 broadcast_in_dim.78
  16.2 0.3 reshape.89
  16.5 0.9 subtract_convert_fusion
  17.5 57.9 %mix.1 = (bf16[2048,2048]{1,0:T(8,128)(2,1)S(1)}, f32[16,2048]{1,0:T(8,128)}) custom-call(bf16[2048,2048]{1,0:T(8,128)(2,1)} %q.1, bf16[2048,2048]{1,0:T(8,128)(2,1)} %k.1, bf16[2048,2048]{1,0:T(8,128)(2,1)} %v.3, bf16[144,2048]{1,0:T(8,128)(2,1)S(1)} %collective-permute-done.halo, f32[8,2048]{1,0:T(8,128)S(1)} %pad.8.short_taps, ...), custom_call_target="tpu_custom_call" | custom-call | flops 8589934592 | bytes 33554432 | tf_op jit(solution)/shard_map/mix/pallas_call | solution.py:111
  75.4 3.4 %copy-done.1 = bf16[2048,2048]{1,0:T(8,128)(2,1)} copy-done((bf16[2048,2048]{1,0:T(8,128)(2,1)}, bf16[2048,2048]{1,0:T(8,128)(2,1)S(1)}, u32[]{:S(2)}) %copy-start.1) | copy-done | bytes 8388632
  78.8 0.1 copy.28
  79.0 0.3 broadcast_in_dim.81
  79.3 0.6 neg.26
  79.9 0.3 broadcast_in_dim.83
  80.3 0.6 reshape.91.state_amp
  80.9 0.2 exponential_select_fusion.weights
  81.1 29.8 %all-gather.3.cloned.1.call-done = f32[128,2048]{1,0:T(8,128)} async-done(((f32[16,2048]{1,0:T(8,128)}), f32[128,2048]{1,0:T(8,128)}) %all-gather.3.cloned.1.call-update) | async-done | bytes 1048592 | tf_op jit(solution)/shard_map/all_gather | solution.py:214
  111.0 1.2 copy-done.2
  112.2 49.3 %join.1 = (bf16[2048,2048]{1,0:T(8,128)(2,1)S(1)}, f32[1,2048]{1,0:T(1,128)S(1)}) custom-call(bf16[2048,2048]{1,0:T(8,128)(2,1)} %copy-done.1, bf16[2048,2048]{1,0:T(8,128)(2,1)} %v.3, f32[8,16,2048]{2,1,0:T(8,128)S(1)} %bitcast.22, f32[8,16,2048]{2,1,0:T(8,128)S(1)} %exponential_select_fusion.weights, f32[1,2048]{1,0:T(1,128)S(1)} %reshape.90.decay_row, ...), custom_call_target="tpu_custom_call" | custom-call | flops 2147483648 | bytes 25165824 | tf_op jit(solution)/shard_map/join/pallas_call | solution.py:178
  161.5 3.4 %copy-done = bf16[2048,2048]{1,0:T(8,128)(2,1)} copy-done((bf16[2048,2048]{1,0:T(8,128)(2,1)}, bf16[2048,2048]{1,0:T(8,128)(2,1)S(1)}, u32[]{:S(2)}) %copy-start) | copy-done | bytes 8388632
  164.9 11.8 %psum.7 = f32[1,2048]{1,0:T(1,128)S(1)} all-reduce(f32[1,2048]{1,0:T(1,128)S(1)} %get-tuple-element.12), channel_id=1, replica_groups=mesh['context'=8,'tensor'=4] {'tensor'}, use_global_device_ids=true, to_apply=%region_1.2 | all-reduce | flops 2048 | bytes 16384 | tf_op jit(solution)/shard_map/psum | solution.py:222
  176.8 8.7 %multiply_convert_fusion = bf16[2048,2048]{1,0:T(8,128)(2,1)} fusion(bf16[2048,2048]{1,0:T(8,128)(2,1)} %copy-done, f32[2048]{0:T(1024)S(1)} %copy-done.7, f32[2048]{0:T(1024)S(1)} %bitcast.27), kind=kLoop, calls=%fused_computation | loop fusion | flops 16777216 | bytes 16793600 | tf_op jit(solution)/shard_map/convert_element_type | solution.py:224
  (47 shorter events, 1.8 us)
Async XLA Ops:
  6.5 104.4 %all-gather.3.cloned.1.call-start = ((), (), s32[]{:S(2)}) async-start(), calls=%async_computation | async-start | bytes 1179648 | tf_op jit(solution)/shard_map/all_gather | solution.py:214
  10.0 4.5 %copy-start.5 = (f32[128,16]{0,1:T(8,128)S(1)}, f32[128,16]{0,1:T(8,128)}, u32[]{:S(2)}) copy-start(f32[128,16]{0,1:T(8,128)} %param.14) | copy-start | bytes 24580
  10.1 4.5 %copy-start.8 = (f32[128,16]{0,1:T(8,128)S(1)}, f32[128,16]{0,1:T(8,128)}, u32[]{:S(2)}) copy-start(f32[128,16]{0,1:T(8,128)} %param.15) | copy-start | bytes 24580
  12.1 3.7 %copy-start.4 = (bf16[128,128]{1,0:T(8,128)(2,1)S(1)}, bf16[128,128]{1,0:T(8,128)(2,1)}, u32[]{:S(2)}) copy-start(bf16[128,128]{1,0:T(8,128)(2,1)} %param.13) | copy-start | bytes 98308
  12.1 3.9 %copy-start.6 = (f32[7,128]{1,0:T(8,128)S(1)}, f32[7,128]{1,0:T(8,128)}, u32[]{:S(2)}) copy-start(f32[7,128]{1,0:T(8,128)} %param.12) | copy-start | bytes 10756
  12.1 5.3 %collective-permute-start = (bf16[144,2048]{1,0:T(8,128)(2,1)S(1)}, bf16[144,2048]{1,0:T(8,128)(2,1)S(1)}, u32[]{:S(2)}, u32[]{:S(2)}) collective-permute-start(bf16[144,2048]{1,0:T(8,128)(2,1)S(1)} %pad_maximum_fusion), channel_id=1, source_target_pairs={{0,4},{4,8},{8,12},{12,16},{16,20},{20,24},{24,28},{1,5},{5,9},{9,... | collective-permute-start | bytes 1769480 | tf_op jit(solution)/shard_map/ppermute | solution.py:25
  16.5 1.0 copy-start.3
  75.4 3.4 %copy-start.1 = (bf16[2048,2048]{1,0:T(8,128)(2,1)}, bf16[2048,2048]{1,0:T(8,128)(2,1)S(1)}, u32[]{:S(2)}) copy-start(bf16[2048,2048]{1,0:T(8,128)(2,1)S(1)} %get-tuple-element.9.y) | copy-start | bytes 25165828
  111.0 1.2 copy-start.2
  112.2 64.6 %copy-start.7 = (f32[2048]{0:T(1024)S(1)}, f32[2048]{0:T(1024)}, u32[]{:S(2)}) copy-start(f32[2048]{0:T(1024)} %param.17) | copy-start | bytes 24580
  161.5 3.4 %copy-start = (bf16[2048,2048]{1,0:T(8,128)(2,1)}, bf16[2048,2048]{1,0:T(8,128)(2,1)S(1)}, u32[]{:S(2)}) copy-start(bf16[2048,2048]{1,0:T(8,128)(2,1)S(1)} %get-tuple-element.11) | copy-start | bytes 25165828
Sparse Core Ops, SparseCore 0:
  78.9 32.0 all-gather.2

commit v2 on v1

v2 whole, which is shorter than its diff:
```python
import functools
import math

import jax
import jax.numpy as jnp
from jax import lax
from jax.experimental import pallas as pl
from jax.experimental.pallas import tpu as pltpu
from jax.sharding import PartitionSpec as P

GROUP_CH = 16
LANES = 128
PACK = LANES // GROUP_CH
WIDE = 256
MODES = 16
SHORT = 7
RATE, AMP, SKIP = SHORT, SHORT + 1, SHORT + 2
STRIP = 256
JOIN_STRIP = 256
MIX_VMEM = 20 << 20
JOIN_VMEM = 20 << 20
F32 = jnp.float32
BF16 = jnp.bfloat16


def split2(value):
    high = value.astype(BF16)
    return high, (value - high.astype(F32)).astype(BF16)


def passed_along(value, axis, steps):
    count = lax.axis_size(axis)
    return lax.ppermute(value, axis, [(source, source + steps) for source in range(count - steps)])


def edge_kernel(q, k, v, taps, halo_out, gated):
    rows = q.shape[0]
    begin = rows - LANES
    kv = k[begin - 16:, :].astype(F32) * v[begin - 16:, :].astype(F32)
    gated[...] = kv
    total = taps[0:1, :] * gated[16:, :]
    for delay in range(1, SHORT):
        total = total + taps[delay:delay + 1, :] * gated[pl.ds(16 - delay, LANES), :]
    halo_out[0:LANES, :] = (q[begin:, :].astype(F32) * total).astype(BF16)
    last = kv[LANES + 8:, :]
    high = last.astype(BF16).astype(F32)
    halo_out[LANES:LANES + 16, :] = jnp.concatenate([high, last - high], axis=0).astype(BF16)


def edge(q, k, v, params):
    rows, chans = q.shape
    wide = math.gcd(chans, 512)
    tall = math.gcd(rows, 256)
    last = pl.BlockSpec((tall, wide), lambda i: (rows // tall - 1, i))
    column = lambda height: pl.BlockSpec((height, wide), lambda i: (0, i))
    return pl.pallas_call(
        edge_kernel,
        grid=(chans // wide,),
        out_shape=jax.ShapeDtypeStruct((LANES + 16, chans), BF16),
        in_specs=[last] * 3 + [column(params.shape[0])],
        out_specs=column(LANES + 16),
        scratch_shapes=[pltpu.VMEM((LANES + 16, wide), F32)],
        compiler_params=pltpu.CompilerParams(vmem_limit_bytes=16 << 20),
        name="edge",
    )(q, k, v, params)


def mix_kernel(q, k, v, halo, params, medium_taps, y_out, state_out, gated, first_t, key_t, y_t, seconds):
    rows = q.shape[0]
    blocks = rows // WIDE
    row_i = lax.broadcasted_iota(jnp.int32, (LANES, LANES), 0)
    col_i = lax.broadcasted_iota(jnp.int32, (LANES, LANES), 1)
    causal = col_i >= row_i
    zero = jnp.zeros((LANES, LANES), BF16)
    time_down = lax.broadcasted_iota(jnp.int32, (WIDE, LANES), 0).astype(F32)
    time_along = lax.broadcasted_iota(jnp.int32, (LANES, WIDE), 1).astype(F32)
    lane_group = lax.broadcasted_iota(jnp.int32, (WIDE, LANES), 1) // MODES

    def strip(s, nothing):
        here = pl.ds(pl.multiple_of(s * LANES, LANES), LANES)
        taps = params[:, here]
        gated[0:8, :] = halo[LANES:LANES + 8, here].astype(F32) + halo[LANES + 8:LANES + 16, here].astype(F32)
        first_t[:, 0:LANES] = halo[0:LANES, here].T
        for begin in range(0, rows, LANES):
            part = pl.ds(begin, LANES)
            keys = k[part, here]
            fresh = keys.astype(F32) * v[part, here].astype(F32)
            gated[pl.ds(begin + 8, LANES), :] = fresh
            total = taps[0:1, :] * fresh
            for delay in range(1, SHORT):
                total = total + taps[delay:delay + 1, :] * gated[pl.ds(begin + 8 - delay, LANES), :]
            first = (q[part, here].astype(F32) * total).astype(BF16)
            first_t[:, begin + LANES:begin + 2 * LANES] = first.T
            key_t[:, begin:begin + LANES] = keys.T

        for g in range(PACK):
            chans = pl.ds(g * GROUP_CH, GROUP_CH)
            turned = jnp.broadcast_to(medium_taps[pl.ds(s * PACK + g, 1), :], (LANES, LANES))
            turned = pltpu.roll(turned, 0, 1, stride=1, stride_axis=0)
            medium_w = jnp.concatenate(
                [jnp.where(causal, 0.0, turned), jnp.where(causal, turned, 0.0)], axis=0).astype(BF16)
            window = jnp.concatenate(
                [first_t[chans, b * LANES:(b + 2) * LANES] for b in range(rows // LANES)], axis=0)
            medium = jnp.dot(window, medium_w, preferred_element_type=F32)
            key = jnp.concatenate(
                [key_t[chans, b * LANES:(b + 1) * LANES] for b in range(rows // LANES)], axis=0)
            second = (key.astype(F32) * medium).astype(BF16)
            for b in range(rows // LANES):
                seconds[(b // 2) * GROUP_CH:(b // 2 + 1) * GROUP_CH,
                        g * WIDE + (b % 2) * LANES:g * WIDE + (b % 2 + 1) * LANES] = (
                    second[b * GROUP_CH:(b + 1) * GROUP_CH])

        rate = taps[RATE:RATE + 1, :]
        tails = jnp.exp(-rate * (WIDE - 1.0 - time_down)).astype(BF16)
        tails_w = jnp.concatenate([jnp.where(lane_group == g, tails, jnp.zeros_like(tails)) for g in range(PACK)], axis=0)
        sums = jnp.dot(seconds[...], tails_w, preferred_element_type=F32)
        decay = jnp.exp(-rate * float(WIDE))
        state = jnp.zeros((GROUP_CH, LANES), F32)
        states = []
        for b in range(blocks):
            states.append(state)
            state = decay * state + sums[b * GROUP_CH:(b + 1) * GROUP_CH, :]
        state_out[:, here] = state.astype(BF16)
        carried = jnp.concatenate(split2(jnp.concatenate(states, axis=0)), axis=1)

        down = lambda row: jnp.broadcast_to(taps[row:row + 1, :], (LANES, LANES)).T
        rate_t, amp_t, skip_t = down(RATE), down(AMP), down(SKIP)
        both = lambda half: jnp.concatenate([half, half], axis=1)
        power = both(amp_t) * jnp.exp(-both(rate_t) * time_along)
        lead = (power * jnp.exp(-both(rate_t))).astype(BF16)
        for g in range(PACK):
            chans = pl.ds(g * GROUP_CH, GROUP_CH)
            mine = slice(g * MODES, (g + 1) * MODES)
            profile = jnp.sum(power[mine], axis=0, keepdims=True)
            turned = pltpu.roll(jnp.broadcast_to(profile, (LANES, WIDE)), 0, 1, stride=1, stride_axis=0)
            near = jnp.where(causal, turned[:, :LANES], 0.0).astype(BF16)
            pieces = [jnp.concatenate([near, turned[:, LANES:].astype(BF16)], axis=1),
                      jnp.concatenate([zero, near], axis=1)]
            lead_g = [lead[mine]]
            if g > 0:
                lead_g = [jnp.zeros((g * MODES, WIDE), BF16)] + lead_g
            if g < PACK - 1:
                lead_g = lead_g + [jnp.zeros(((PACK - 1 - g) * MODES, WIDE), BF16)]
            second = seconds[:, g * WIDE:(g + 1) * WIDE]
            y = jnp.dot(jnp.concatenate([second, carried], axis=1),
                        jnp.concatenate(pieces + lead_g + lead_g, axis=0), preferred_element_type=F32)
            gain = both(skip_t[g * GROUP_CH:(g + 1) * GROUP_CH, :])
            gain = jnp.concatenate([gain] * blocks, axis=0)
            y = (y + gain * second.astype(F32)).astype(BF16)
            for b in range(blocks):
                y_t[chans, b * WIDE:(b + 1) * WIDE] = y[b * GROUP_CH:(b + 1) * GROUP_CH, :]
        for begin in range(0, rows, LANES):
            y_out[pl.ds(begin, LANES), here] = y_t[:, begin:begin + LANES].T
        return nothing

    lax.fori_loop(0, q.shape[1] // LANES, strip, 0)


def mix(q, k, v, halo, params, medium_taps):
    rows, chans = q.shape
    wide = math.gcd(chans, STRIP)
    column = lambda height: pl.BlockSpec((height, wide), lambda i: (0, i))
    return pl.pallas_call(
        mix_kernel,
        grid=(chans // wide,),
        out_shape=(jax.ShapeDtypeStruct((rows, chans), BF16), jax.ShapeDtypeStruct((GROUP_CH, chans), BF16)),
        in_specs=[column(rows)] * 3 + [column(halo.shape[0]), column(params.shape[0]),
                                       pl.BlockSpec((wide // GROUP_CH, LANES), lambda i: (i, 0))],
        out_specs=(column(rows), column(GROUP_CH)),
        scratch_shapes=[
            pltpu.VMEM((rows + 8, LANES), F32),
            pltpu.VMEM((LANES, rows + LANES), BF16),
            pltpu.VMEM((LANES, rows), BF16),
            pltpu.VMEM((LANES, rows), BF16),
            pltpu.VMEM((LANES, PACK * WIDE), BF16),
        ],
        compiler_params=pltpu.CompilerParams(vmem_limit_bytes=MIX_VMEM),
        cost_estimate=pl.CostEstimate(flops=8 * rows * chans * WIDE, bytes_accessed=8 * rows * chans, transcendentals=0),
        name="mix",
    )(q, k, v, halo, params, medium_taps)


def join_kernel(y, v, states, weights, params, mixed_out, energy_out, energy):
    rows, wide = y.shape
    step = pl.program_id(0)

    @pl.when(step == 0)
    def _():
        energy[...] = jnp.zeros_like(energy)

    row_i = lax.broadcasted_iota(jnp.int32, (LANES, LANES), 0)
    col_i = lax.broadcasted_iota(jnp.int32, (LANES, LANES), 1)
    own = row_i // GROUP_CH == col_i // MODES
    time = row_i.astype(F32) + 1.0
    entry = jnp.zeros((GROUP_CH, wide), F32)
    for source in range(states.shape[0]):
        entry = entry + weights[source:source + 1, :] * states[source].astype(F32)
    entries, leads = [], []
    for s in range(wide // LANES):
        here = slice(s * LANES, (s + 1) * LANES)
        spread = jnp.where(own, jnp.concatenate([entry[:, here]] * PACK, axis=0), 0.0)
        entries.append(jnp.concatenate(split2(spread), axis=1))
        leads.append(jnp.exp(-params[RATE:RATE + 1, here] * time))
    for b in range(rows // LANES):
        part = pl.ds(b * LANES, LANES)
        total = energy[part, :]
        for s in range(wide // LANES):
            here = slice(s * LANES, (s + 1) * LANES)
            lead = (leads[s] * jnp.exp(-params[RATE:RATE + 1, here] * float(b * LANES))).astype(BF16)
            carried = lax.dot_general(jnp.concatenate([lead, lead], axis=1), entries[s],
                                      (((1,), (1,)), ((), ())), preferred_element_type=F32)
            mixed = v[part, here].astype(F32) * (y[part, here].astype(F32) + carried)
            mixed_out[part, here] = mixed.astype(BF16)
            total = total + mixed * mixed
        energy[part, :] = total

    @pl.when(step == pl.num_programs(0) - 1)
    def _():
        for begin in range(0, rows, LANES):
            energy_out[:, begin:begin + LANES] = jnp.sum(energy[pl.ds(begin, LANES), :].T, axis=0, keepdims=True)


def join(y, v, states, weights, params):
    rows, chans = y.shape
    wide = math.gcd(chans, JOIN_STRIP)
    column = lambda height: pl.BlockSpec((height, wide), lambda i: (0, i))
    return pl.pallas_call(
        join_kernel,
        grid=(chans // wide,),
        out_shape=(jax.ShapeDtypeStruct((rows, chans), BF16), jax.ShapeDtypeStruct((1, rows), F32)),
        in_specs=[column(rows), column(rows), pl.BlockSpec((states.shape[0], GROUP_CH, wide), lambda i: (0, 0, i)),
                  column(weights.shape[0]), column(params.shape[0])],
        out_specs=(column(rows), pl.BlockSpec((1, rows), lambda i: (0, 0))),
        scratch_shapes=[pltpu.VMEM((rows, LANES), F32)],
        compiler_params=pltpu.CompilerParams(vmem_limit_bytes=JOIN_VMEM),
        cost_estimate=pl.CostEstimate(flops=2 * rows * chans * WIDE, bytes_accessed=6 * rows * chans, transcendentals=0),
        name="join",
    )(y, v, states, weights, params)


def local(queries, key_rows, value_rows, short_filter, medium_filter, decays, residue, skip_gain,
          norm_gain, width):
    rows, chans = queries.shape
    amplitude = residue * jnp.sqrt(-jnp.expm1(-2.0 * decays))
    params = jnp.concatenate([
        jnp.repeat(short_filter, GROUP_CH, axis=1),
        decays.reshape(1, chans), amplitude.reshape(1, chans), skip_gain[None, :],
        jnp.zeros((16 - SHORT - 3, chans), F32)], axis=0)
    halo = passed_along(edge(queries, key_rows, value_rows, params), "context", 1)
    y, state = mix(queries, key_rows, value_rows, halo, params, medium_filter.T.astype(F32))
    states = lax.all_gather(state, "context")
    count = lax.axis_size("context")
    gap = (lax.axis_index("context") - 1 - jnp.arange(count)).astype(F32)[:, None]
    weights = jnp.where(gap >= 0.0, params[AMP:AMP + 1] * jnp.exp(-params[RATE:RATE + 1] * (jnp.maximum(gap, 0.0) * rows)), 0.0)
    mixed, energy = join(y, value_rows, states, weights, params)
    energy = lax.psum(energy, "tensor")
    scale = lax.rsqrt(energy[0] / width + 1e-06)
    return (mixed.astype(F32) * scale[:, None] * norm_gain[None, :]).astype(BF16)


def solution(mesh):
    def whole(*args):
        return jax.shard_map(
            functools.partial(local, width=args[0].shape[1]),
            mesh=mesh,
            in_specs=(
                P("context", "tensor"),
                P("context", "tensor"),
                P("context", "tensor"),
                P(None, "tensor"),
                P(None, "tensor"),
                P("tensor", None),
                P("tensor", None),
                P("tensor"),
                P("tensor"),
            ),
            out_specs=P("context", "tensor"),
            check_vma=False,
        )(*args)

    return whole
```

time: 193 us -> 123 us (0.64)
  Pallas kernels: 107 us -> 51 us
  waiting for transfers between devices: 29.9 us -> 1.04 us
  blocking collectives: 11.8 us -> 31.5 us
  local copies, waits for them, and re-layouts: 13.3 us -> 27 us
  between operations: 13.7 us -> 0.16 us
  other arithmetic: 14.2 us -> 9.6 us
    pallas_call x2 -> x3, Pallas kernels: 107 us -> 51 us  [the longest x1 38.2 us: mix(): pl.pallas_call(mix_kernel, grid=(chans // wide,), out_shape=(jax.ShapeDty...]
    all_gather x1 -> x0, waiting for transfers between devices: 29.8 us -> none  [local(): states = lax.all_gather(state, 'context')]
    all_gather x0 -> x1, blocking collectives: none -> 19.4 us  [local(): states = lax.all_gather(state, 'context')]
    unnamed x20 -> x22, local copies, waits for them, and re-layouts: 8.26 us -> 24.6 us
    convert_element_type x3 -> x1, other arithmetic: 2.94 us -> 0.01 us  [local(): medium_filter.T.astype(F32)]
  transfers between devices with their start and end apart: 2 -> 1, of which waited for: 1 -> 1; matrix products, arithmetic and copies ran while one was open for 3% -> 0% of each run, Pallas kernels for 0% -> 0%
where the time goes in v2:
time: 123 us
  Pallas kernels  51 us (41%)
  blocking collectives  31.5 us (26%)
  local copies, waits for them, and re-layouts  27 us (22%)
  other arithmetic  9.6 us (8%)
  starting transfers between devices  2.39 us (2%)
    pallas_call x1, Pallas kernels, mix(): pl.pallas_call(mix_kernel, grid=(chans // wide,), out_shape=(jax.ShapeDty...  38.2 us
    unnamed x22, local copies, waits for them, and re-layouts  24.6 us
    all_gather x1, blocking collectives, local(): states = lax.all_gather(state, 'context')  19.4 us
    psum x1, blocking collectives, local(): energy = lax.psum(energy, 'tensor')  12.1 us
    pallas_call x1, Pallas kernels, join(): pl.pallas_call(join_kernel, grid=(chans // wide,), out_shape=(jax.ShapeDt...  10.8 us
    convert_element_type x1, other arithmetic, local(): (mixed.astype(F32) * scale[:, None] * norm_gain[None, :]).astype(BF16)  8.74 us
  transfers between devices with their start and end apart: 1, of which 1 were waited for; matrix products, arithmetic and copies ran while one was open for 0% of the time, Pallas kernels for 0%

profile of v2, /device:TPU:0, one launch (start us, length us, event | category | flops | bytes accessed | tf_op | source)
XLA Modules:
  0.0 122.7 jit_solution(2404301581786282615)
XLA Ops:
  0.0 0.8 copy.13
  0.8 0.7 fusion
  1.5 0.1 copy.14
  1.6 0.1 reshape.46
  1.8 0.9 broadcast_in_dim.24
  2.7 0.3 reshape.44
  3.0 0.8 concatenate.3.taps.params
  3.7 3.4 %copy-done = bf16[2048,2048]{1,0:T(8,128)(2,1)S(1)} copy-done((bf16[2048,2048]{1,0:T(8,128)(2,1)S(1)}, bf16[2048,2048]{1,0:T(8,128)(2,1)}, u32[]{:S(2)}) %copy-start) | copy-done | bytes 8388632
  7.1 3.4 %copy-done.3 = bf16[2048,2048]{1,0:T(8,128)(2,1)S(1)} copy-done((bf16[2048,2048]{1,0:T(8,128)(2,1)S(1)}, bf16[2048,2048]{1,0:T(8,128)(2,1)}, u32[]{:S(2)}) %copy-start.3) | copy-done | bytes 8388632
  10.5 3.4 %copy-done.5 = bf16[2048,2048]{1,0:T(8,128)(2,1)S(1)} copy-done((bf16[2048,2048]{1,0:T(8,128)(2,1)S(1)}, bf16[2048,2048]{1,0:T(8,128)(2,1)}, u32[]{:S(2)}) %copy-start.5) | copy-done | bytes 8388632
  13.9 1.9 %edge.1 = bf16[144,2048]{1,0:T(8,128)(2,1)S(1)} custom-call(bf16[2048,2048]{1,0:T(8,128)(2,1)S(1)} %copy-done.3, bf16[2048,2048]{1,0:T(8,128)(2,1)S(1)} %copy-done.5, bf16[2048,2048]{1,0:T(8,128)(2,1)S(1)} %copy-done, f32[16,2048]{1,0:T(8,128)S(1)} %concatenate.3.taps.params), custom_call_target="tpu_custom_call" | custom-call | tf_op jit(solution)/shard_map/edge/pallas_call | solution.py:56
  15.8 2.4 %collective-permute-start = (bf16[144,2048]{1,0:T(8,128)(2,1)S(1)}, bf16[144,2048]{1,0:T(8,128)(2,1)S(1)}, u32[]{:S(2)}, u32[]{:S(2)}) collective-permute-start(bf16[144,2048]{1,0:T(8,128)(2,1)S(1)} %edge.1), channel_id=1, source_target_pairs={{0,4},{4,8},{8,12},{12,16},{16,20},{20,24},{24,28},{1,5},{5,9},{9,... | collective-permute-start | bytes 1769480 | tf_op jit(solution)/shard_map/ppermute | solution.py:33
  18.2 0.1 copy.15
  18.4 0.1 copy.17
  18.7 1.0 collective-permute-done.halo
  19.8 3.4 %copy-done.1 = bf16[2048,2048]{1,0:T(8,128)(2,1)S(1)} copy-done((bf16[2048,2048]{1,0:T(8,128)(2,1)S(1)}, bf16[2048,2048]{1,0:T(8,128)(2,1)}, u32[]{:S(2)}) %copy-start.1) | copy-done | bytes 8388632
  23.2 3.4 %copy-done.4 = bf16[2048,2048]{1,0:T(8,128)(2,1)S(1)} copy-done((bf16[2048,2048]{1,0:T(8,128)(2,1)S(1)}, bf16[2048,2048]{1,0:T(8,128)(2,1)}, u32[]{:S(2)}) %copy-start.4) | copy-done | bytes 8388632
  26.5 3.4 %copy-done.6 = bf16[2048,2048]{1,0:T(8,128)(2,1)S(1)} copy-done((bf16[2048,2048]{1,0:T(8,128)(2,1)S(1)}, bf16[2048,2048]{1,0:T(8,128)(2,1)}, u32[]{:S(2)}) %copy-start.6) | copy-done | bytes 8388632
  29.9 38.2 %mix.1 = (bf16[2048,2048]{1,0:T(8,128)(2,1)S(1)}, bf16[16,2048]{1,0:T(8,128)(2,1)S(1)}) custom-call(bf16[2048,2048]{1,0:T(8,128)(2,1)S(1)} %copy-done.4, bf16[2048,2048]{1,0:T(8,128)(2,1)S(1)} %copy-done.6, bf16[2048,2048]{1,0:T(8,128)(2,1)S(1)} %copy-done.1, bf16[144,2048]{1,0:T(8,128)(2,1)S(1)} %collective-permute-done.halo, ...), custom_call_target="tpu_custom_call" | custom-call | flops 8589934592 | bytes 33554432 | tf_op jit(solution)/shard_map/mix/pallas_call | solution.py:163
  68.1 19.4 %all-gather = bf16[128,2048]{1,0:T(8,128)(2,1)S(1)} all-gather(bf16[16,2048]{1,0:T(8,128)(2,1)S(1)} %get-tuple-element.10), channel_id=2, replica_groups=mesh['context'=8,'tensor'=4] {'context'}, dimensions={0}, use_global_device_ids=true | all-gather | bytes 589824 | tf_op jit(solution)/shard_map/all_gather | solution.py:251
  87.6 10.8 %join.1 = (bf16[2048,2048]{1,0:T(8,128)(2,1)S(1)}, f32[1,2048]{1,0:T(1,128)S(1)}) custom-call(bf16[2048,2048]{1,0:T(8,128)(2,1)S(1)} %get-tuple-element.9.y, bf16[2048,2048]{1,0:T(8,128)(2,1)S(1)} %copy-done.2, bf16[8,16,2048]{2,1,0:T(8,128)(2,1)S(1)} %bitcast.5, f32[8,2048]{1,0:T(8,128)S(1)} %multiply_select_fusion.weights, ...), custom_call_target="tpu_custom_call" | custom-call | flops 2147483648 | bytes 25165824 | tf_op jit(solution)/shard_map/join/pallas_call | solution.py:227
  98.5 3.4 %copy-done.7 = bf16[2048,2048]{1,0:T(8,128)(2,1)} copy-done((bf16[2048,2048]{1,0:T(8,128)(2,1)}, bf16[2048,2048]{1,0:T(8,128)(2,1)S(1)}, u32[]{:S(2)}) %copy-start.7) | copy-done | bytes 8388632
  101.8 12.1 %psum.7 = f32[1,2048]{1,0:T(1,128)S(1)} all-reduce(f32[1,2048]{1,0:T(1,128)S(1)} %get-tuple-element.12), channel_id=1, replica_groups=mesh['context'=8,'tensor'=4] {'tensor'}, use_global_device_ids=true, to_apply=%region_0.1 | all-reduce | flops 2048 | bytes 16384 | tf_op jit(solution)/shard_map/psum | solution.py:256
  114.0 8.7 %multiply_convert_fusion = bf16[2048,2048]{1,0:T(8,128)(2,1)} fusion(bf16[2048,2048]{1,0:T(8,128)(2,1)} %copy-done.7, f32[2048]{0:T(1024)S(1)} %copy-done.9, f32[2048]{0:T(1024)S(1)} %bitcast.6), kind=kLoop, calls=%fused_computation | loop fusion | flops 16777216 | bytes 16793600 | tf_op jit(solution)/shard_map/convert_element_type | solution.py:258
  (22 shorter events, 0.4 us)
Async XLA Ops:
  3.7 3.4 %copy-start = (bf16[2048,2048]{1,0:T(8,128)(2,1)S(1)}, bf16[2048,2048]{1,0:T(8,128)(2,1)}, u32[]{:S(2)}) copy-start(bf16[2048,2048]{1,0:T(8,128)(2,1)} %v.5) | copy-start | bytes 25165828
  7.1 3.4 %copy-start.3 = (bf16[2048,2048]{1,0:T(8,128)(2,1)S(1)}, bf16[2048,2048]{1,0:T(8,128)(2,1)}, u32[]{:S(2)}) copy-start(bf16[2048,2048]{1,0:T(8,128)(2,1)} %q.3) | copy-start | bytes 25165828
  10.5 3.4 %copy-start.5 = (bf16[2048,2048]{1,0:T(8,128)(2,1)S(1)}, bf16[2048,2048]{1,0:T(8,128)(2,1)}, u32[]{:S(2)}) copy-start(bf16[2048,2048]{1,0:T(8,128)(2,1)} %k.3) | copy-start | bytes 25165828
  13.9 4.3 %copy-start.8 = (bf16[128,128]{1,0:T(8,128)(2,1)S(1)}, bf16[128,128]{1,0:T(8,128)(2,1)}, u32[]{:S(2)}) copy-start(bf16[128,128]{1,0:T(8,128)(2,1)} %param.13) | copy-start | bytes 98308
  15.8 4.0 %collective-permute-start = (bf16[144,2048]{1,0:T(8,128)(2,1)S(1)}, bf16[144,2048]{1,0:T(8,128)(2,1)S(1)}, u32[]{:S(2)}, u32[]{:S(2)}) collective-permute-start(bf16[144,2048]{1,0:T(8,128)(2,1)S(1)} %edge.1), channel_id=1, source_target_pairs={{0,4},{4,8},{8,12},{12,16},{16,20},{20,24},{24,28},{1,5},{5,9},{9,... | collective-permute-start | bytes 1769480 | tf_op jit(solution)/shard_map/ppermute | solution.py:33
  19.8 3.4 %copy-start.1 = (bf16[2048,2048]{1,0:T(8,128)(2,1)S(1)}, bf16[2048,2048]{1,0:T(8,128)(2,1)}, u32[]{:S(2)}) copy-start(bf16[2048,2048]{1,0:T(8,128)(2,1)} %v.5) | copy-start | bytes 25165828
  23.2 3.4 %copy-start.4 = (bf16[2048,2048]{1,0:T(8,128)(2,1)S(1)}, bf16[2048,2048]{1,0:T(8,128)(2,1)}, u32[]{:S(2)}) copy-start(bf16[2048,2048]{1,0:T(8,128)(2,1)} %q.3) | copy-start | bytes 25165828
  26.5 3.4 %copy-start.6 = (bf16[2048,2048]{1,0:T(8,128)(2,1)S(1)}, bf16[2048,2048]{1,0:T(8,128)(2,1)}, u32[]{:S(2)}) copy-start(bf16[2048,2048]{1,0:T(8,128)(2,1)} %k.3) | copy-start | bytes 25165828
  29.9 57.7 %copy-start.2 = (bf16[2048,2048]{1,0:T(8,128)(2,1)S(1)}, bf16[2048,2048]{1,0:T(8,128)(2,1)}, u32[]{:S(2)}) copy-start(bf16[2048,2048]{1,0:T(8,128)(2,1)} %v.5) | copy-start | bytes 25165828
  87.6 26.4 %copy-start.9 = (f32[2048]{0:T(1024)S(1)}, f32[2048]{0:T(1024)}, u32[]{:S(2)}) copy-start(f32[2048]{0:T(1024)} %param.17) | copy-start | bytes 24580
  98.4 3.4 %copy-start.7 = (bf16[2048,2048]{1,0:T(8,128)(2,1)}, bf16[2048,2048]{1,0:T(8,128)(2,1)S(1)}, u32[]{:S(2)}) copy-start(bf16[2048,2048]{1,0:T(8,128)(2,1)S(1)} %get-tuple-element.11) | copy-start | bytes 25165828

commit v3 on v2

v3 whole, which is shorter than its diff:
```python
import functools
import math

import jax
import jax.numpy as jnp
from jax import lax
from jax.experimental import pallas as pl
from jax.experimental.pallas import tpu as pltpu
from jax.sharding import PartitionSpec as P

GROUP_CH = 16
LANES = 128
PACK = LANES // GROUP_CH
WIDE = 256
MODES = 16
SHORT = 7
RATE, AMP, SKIP = SHORT, SHORT + 1, SHORT + 2
EARLY = 0
JOIN_STRIP = 256
MIX_VMEM = 60 << 20
JOIN_VMEM = 60 << 20
F32 = jnp.float32
BF16 = jnp.bfloat16


def split2(value):
    high = value.astype(BF16)
    return high, (value - high.astype(F32)).astype(BF16)


def passed_along(value, axis, steps):
    count = lax.axis_size(axis)
    return lax.ppermute(value, axis, [(source, source + steps) for source in range(count - steps)])


def edge_kernel(q, k, v, taps, halo_out, gated):
    rows = q.shape[0]
    begin = rows - LANES
    kv = k[begin - 16:, :].astype(F32) * v[begin - 16:, :].astype(F32)
    gated[...] = kv
    total = taps[0:1, :] * gated[16:, :]
    for delay in range(1, SHORT):
        total = total + taps[delay:delay + 1, :] * gated[pl.ds(16 - delay, LANES), :]
    halo_out[0:LANES, :] = (q[begin:, :].astype(F32) * total).astype(BF16)
    last = kv[LANES + 8:, :]
    high = last.astype(BF16).astype(F32)
    halo_out[LANES:LANES + 16, :] = jnp.concatenate([high, last - high], axis=0).astype(BF16)


def edge(q, k, v, params):
    rows, chans = q.shape
    wide = math.gcd(chans, 512)
    tall = math.gcd(rows, 256)
    last = pl.BlockSpec((tall, wide), lambda i: (rows // tall - 1, i))
    column = lambda height: pl.BlockSpec((height, wide), lambda i: (0, i))
    return pl.pallas_call(
        edge_kernel,
        grid=(chans // wide,),
        out_shape=jax.ShapeDtypeStruct((LANES + 16, chans), BF16),
        in_specs=[last] * 3 + [column(params.shape[0])],
        out_specs=column(LANES + 16),
        scratch_shapes=[pltpu.VMEM((LANES + 16, wide), F32)],
        compiler_params=pltpu.CompilerParams(vmem_limit_bytes=MIX_VMEM),
        name="edge",
    )(q, k, v, params)


def mix_kernel(q, k, v, halo, params, late_params, medium_taps, y_out, state_out, gated, y_t, seconds,
               first_a, key_a, first_b, key_b):
    parity = pl.program_id(0) % 2

    @pl.when(parity == 0)
    def _():
        mix_strip(q, k, v, halo, params, late_params, medium_taps, y_out, state_out, gated, y_t, seconds,
                  (first_a, key_a), (first_b, key_b))

    @pl.when(parity == 1)
    def _():
        mix_strip(q, k, v, halo, params, late_params, medium_taps, y_out, state_out, gated, y_t, seconds,
                  (first_b, key_b), (first_a, key_a))


def mix_strip(q, k, v, halo, params, late_params, medium_taps, y_out, state_out, gated, y_t, seconds,
              fresh_refs, ready_refs):
    rows = q.shape[0]
    blocks = rows // WIDE
    halves = rows // LANES
    next_first, next_key = fresh_refs
    first_t, key_t = ready_refs
    row_i = lax.broadcasted_iota(jnp.int32, (LANES, LANES), 0)
    col_i = lax.broadcasted_iota(jnp.int32, (LANES, LANES), 1)
    causal = col_i >= row_i
    zero = jnp.zeros((LANES, LANES), BF16)
    time_down = lax.broadcasted_iota(jnp.int32, (WIDE, LANES), 0).astype(F32)
    time_along = lax.broadcasted_iota(jnp.int32, (LANES, WIDE), 1).astype(F32)
    lane_group = lax.broadcasted_iota(jnp.int32, (WIDE, LANES), 1) // MODES
    taps = params[...]
    late = late_params[...]

    def gate_first(b):
        begin = b * LANES
        part = pl.ds(begin, LANES)
        keys = k[part, :]
        fresh = keys.astype(F32) * v[part, :].astype(F32)
        gated[pl.ds(begin + 8, LANES), :] = fresh
        total = taps[0:1, :] * fresh
        for delay in range(1, SHORT):
            total = total + taps[delay:delay + 1, :] * gated[pl.ds(begin + 8 - delay, LANES), :]
        first = (q[part, :].astype(F32) * total).astype(BF16)
        next_first[:, begin + LANES:begin + 2 * LANES] = first.T
        next_key[:, begin:begin + LANES] = keys.T

    def medium_of(g):
        chans = pl.ds(g * GROUP_CH, GROUP_CH)
        turned = jnp.broadcast_to(medium_taps[g:g + 1, :], (LANES, LANES))
        turned = pltpu.roll(turned, 0, 1, stride=1, stride_axis=0)
        medium_w = jnp.concatenate(
            [jnp.where(causal, 0.0, turned), jnp.where(causal, turned, 0.0)], axis=0).astype(BF16)
        window = jnp.concatenate([first_t[chans, b * LANES:(b + 2) * LANES] for b in range(halves)], axis=0)
        medium = jnp.dot(window, medium_w, preferred_element_type=F32)
        key = jnp.concatenate([key_t[chans, b * LANES:(b + 1) * LANES] for b in range(halves)], axis=0)
        second = (key.astype(F32) * medium).astype(BF16)
        for b in range(halves):
            seconds[(b // 2) * GROUP_CH:(b // 2 + 1) * GROUP_CH,
                    g * WIDE + (b % 2) * LANES:g * WIDE + (b % 2 + 1) * LANES] = (
                second[b * GROUP_CH:(b + 1) * GROUP_CH])

    gated[0:8, :] = halo[LANES:LANES + 8, :].astype(F32) + halo[LANES + 8:LANES + 16, :].astype(F32)
    next_first[:, 0:LANES] = halo[0:LANES, :].T
    early = EARLY * halves // 16
    done = 0
    for g in range(PACK):
        medium_of(g)
        goal = early * (g + 1) // PACK
        for b in range(done, goal):
            gate_first(b)
        done = goal

    rate = late[RATE:RATE + 1, :]
    tails = jnp.exp(-rate * (WIDE - 1.0 - time_down)).astype(BF16)
    tails_w = jnp.concatenate([jnp.where(lane_group == g, tails, jnp.zeros_like(tails)) for g in range(PACK)], axis=0)
    sums = jnp.dot(seconds[...], tails_w, preferred_element_type=F32)
    decay = jnp.exp(-rate * float(WIDE))
    state = jnp.zeros((GROUP_CH, LANES), F32)
    states = []
    for b in range(blocks):
        states.append(state)
        state = decay * state + sums[b * GROUP_CH:(b + 1) * GROUP_CH, :]
    state_out[...] = state.astype(BF16)
    carried = jnp.concatenate(split2(jnp.concatenate(states, axis=0)), axis=1)

    down = lambda row: jnp.broadcast_to(late[row:row + 1, :], (LANES, LANES)).T
    rate_t, amp_t, skip_t = down(RATE), down(AMP), down(SKIP)
    both = lambda half: jnp.concatenate([half, half], axis=1)
    power = both(amp_t) * jnp.exp(-both(rate_t) * time_along)
    lead = (power * jnp.exp(-both(rate_t))).astype(BF16)

    def long_of(g):
        chans = pl.ds(g * GROUP_CH, GROUP_CH)
        mine = slice(g * MODES, (g + 1) * MODES)
        profile = jnp.sum(power[mine], axis=0, keepdims=True)
        turned = pltpu.roll(jnp.broadcast_to(profile, (LANES, WIDE)), 0, 1, stride=1, stride_axis=0)
        near = jnp.where(causal, turned[:, :LANES], 0.0).astype(BF16)
        pieces = [jnp.concatenate([near, turned[:, LANES:].astype(BF16)], axis=1),
                  jnp.concatenate([zero, near], axis=1)]
        lead_g = [lead[mine]]
        if g > 0:
            lead_g = [jnp.zeros((g * MODES, WIDE), BF16)] + lead_g
        if g < PACK - 1:
            lead_g = lead_g + [jnp.zeros(((PACK - 1 - g) * MODES, WIDE), BF16)]
        second = seconds[:, g * WIDE:(g + 1) * WIDE]
        y = jnp.dot(jnp.concatenate([second, carried], axis=1),
                    jnp.concatenate(pieces + lead_g + lead_g, axis=0), preferred_element_type=F32)
        gain = both(skip_t[g * GROUP_CH:(g + 1) * GROUP_CH, :])
        gain = jnp.concatenate([gain] * blocks, axis=0)
        y = (y + gain * second.astype(F32)).astype(BF16)
        for b in range(blocks):
            y_t[chans, b * WIDE:(b + 1) * WIDE] = y[b * GROUP_CH:(b + 1) * GROUP_CH, :]

    for g in range(PACK):
        long_of(g)
        goal = early + (halves - early) * (g + 1) // PACK
        for b in range(done, goal):
            gate_first(b)
        done = goal
    for begin in range(0, rows, LANES):
        y_out[pl.ds(begin, LANES), :] = y_t[:, begin:begin + LANES].T


def mix(q, k, v, halo, params, medium_taps):
    rows, chans = q.shape
    strips = chans // LANES
    ahead = lambda i: jnp.minimum(i, strips - 1)
    behind = lambda i: jnp.maximum(i - 1, 0)
    column = lambda height, of: pl.BlockSpec((height, LANES), lambda i: (0, of(i)))
    return pl.pallas_call(
        mix_kernel,
        grid=(strips + 1,),
        out_shape=(jax.ShapeDtypeStruct((rows, chans), BF16), jax.ShapeDtypeStruct((GROUP_CH, chans), BF16)),
        in_specs=[column(rows, ahead)] * 3 + [
            column(halo.shape[0], ahead), column(params.shape[0], ahead), column(params.shape[0], behind),
            pl.BlockSpec((PACK, LANES), lambda i: (behind(i), 0))],
        out_specs=(column(rows, behind), column(GROUP_CH, behind)),
        scratch_shapes=[
            pltpu.VMEM((rows + 8, LANES), F32),
            pltpu.VMEM((LANES, rows), BF16),
            pltpu.VMEM((LANES, PACK * WIDE), BF16),
        ] + [pltpu.VMEM((LANES, rows + LANES), BF16), pltpu.VMEM((LANES, rows), BF16)] * 2,
        compiler_params=pltpu.CompilerParams(vmem_limit_bytes=MIX_VMEM),
        cost_estimate=pl.CostEstimate(flops=8 * rows * chans * WIDE, bytes_accessed=8 * rows * chans, transcendentals=0),
        name="mix",
    )(q, k, v, halo, params, params, medium_taps)


def join_kernel(y, v, states, weights, params, mixed_out, energy_out, energy):
    rows, wide = y.shape
    step = pl.program_id(0)

    @pl.when(step == 0)
    def _():
        energy[...] = jnp.zeros_like(energy)

    row_i = lax.broadcasted_iota(jnp.int32, (LANES, LANES), 0)
    col_i = lax.broadcasted_iota(jnp.int32, (LANES, LANES), 1)
    own = row_i // GROUP_CH == col_i // MODES
    time = row_i.astype(F32) + 1.0
    entry = jnp.zeros((GROUP_CH, wide), F32)
    for source in range(states.shape[0]):
        entry = entry + weights[source:source + 1, :] * states[source].astype(F32)
    entries, leads = [], []
    for s in range(wide // LANES):
        here = slice(s * LANES, (s + 1) * LANES)
        spread = jnp.where(own, jnp.concatenate([entry[:, here]] * PACK, axis=0), 0.0)
        entries.append(jnp.concatenate(split2(spread), axis=1))
        leads.append(jnp.exp(-params[RATE:RATE + 1, here] * time))
    for b in range(rows // LANES):
        part = pl.ds(b * LANES, LANES)
        total = energy[part, :]
        for s in range(wide // LANES):
            here = slice(s * LANES, (s + 1) * LANES)
            lead = (leads[s] * jnp.exp(-params[RATE:RATE + 1, here] * float(b * LANES))).astype(BF16)
            carried = lax.dot_general(jnp.concatenate([lead, lead], axis=1), entries[s],
                                      (((1,), (1,)), ((), ())), preferred_element_type=F32)
            mixed = v[part, here].astype(F32) * (y[part, here].astype(F32) + carried)
            mixed_out[part, here] = mixed.astype(BF16)
            total = total + mixed * mixed
        energy[part, :] = total

    @pl.when(step == pl.num_programs(0) - 1)
    def _():
        for begin in range(0, rows, LANES):
            energy_out[:, begin:begin + LANES] = jnp.sum(energy[pl.ds(begin, LANES), :].T, axis=0, keepdims=True)


def join(y, v, states, weights, params):
    rows, chans = y.shape
    wide = math.gcd(chans, JOIN_STRIP)
    column = lambda height: pl.BlockSpec((height, wide), lambda i: (0, i))
    return pl.pallas_call(
        join_kernel,
        grid=(chans // wide,),
        out_shape=(jax.ShapeDtypeStruct((rows, chans), BF16), jax.ShapeDtypeStruct((1, rows), F32)),
        in_specs=[column(rows), column(rows), pl.BlockSpec((states.shape[0], GROUP_CH, wide), lambda i: (0, 0, i)),
                  column(weights.shape[0]), column(params.shape[0])],
        out_specs=(column(rows), pl.BlockSpec((1, rows), lambda i: (0, 0))),
        scratch_shapes=[pltpu.VMEM((rows, LANES), F32)],
        compiler_params=pltpu.CompilerParams(vmem_limit_bytes=JOIN_VMEM),
        cost_estimate=pl.CostEstimate(flops=2 * rows * chans * WIDE, bytes_accessed=6 * rows * chans, transcendentals=0),
        name="join",
    )(y, v, states, weights, params)


def scale_kernel(mixed, energy, gain, out, *, width):
    rows, chans = mixed.shape
    for begin in range(0, rows, LANES):
        part = pl.ds(begin, LANES)
        scale = lax.rsqrt(energy[:, begin:begin + LANES] / width + 1e-06)
        scale = jnp.broadcast_to(scale, (LANES, LANES)).T
        for left in range(0, chans, LANES):
            here = slice(left, left + LANES)
            out[part, here] = (mixed[part, here].astype(F32) * scale * gain[:, here]).astype(BF16)


def scaled(mixed, energy, gain, width):
    rows, chans = mixed.shape
    tall = math.gcd(rows, 256)
    block = pl.BlockSpec((tall, chans), lambda i: (i, 0))
    return pl.pallas_call(
        functools.partial(scale_kernel, width=width),
        grid=(rows // tall,),
        out_shape=jax.ShapeDtypeStruct((rows, chans), BF16),
        in_specs=[block, pl.BlockSpec((1, tall), lambda i: (0, i)), pl.BlockSpec((1, chans), lambda i: (0, 0))],
        out_specs=block,
        compiler_params=pltpu.CompilerParams(vmem_limit_bytes=JOIN_VMEM),
        name="scale",
    )(mixed, energy, gain)


def local(queries, key_rows, value_rows, short_filter, medium_filter, decays, residue, skip_gain,
          norm_gain, width):
    rows, chans = queries.shape
    amplitude = residue * jnp.sqrt(-jnp.expm1(-2.0 * decays))
    params = jnp.concatenate([
        jnp.repeat(short_filter, GROUP_CH, axis=1),
        decays.reshape(1, chans), amplitude.reshape(1, chans), skip_gain[None, :],
        jnp.zeros((16 - SHORT - 3, chans), F32)], axis=0)
    halo = passed_along(edge(queries, key_rows, value_rows, params), "context", 1)
    y, state = mix(queries, key_rows, value_rows, halo, params, medium_filter.T.astype(F32))
    states = lax.all_gather(state, "context")
    count = lax.axis_size("context")
    gap = (lax.axis_index("context") - 1 - jnp.arange(count)).astype(F32)[:, None]
    weights = jnp.where(gap >= 0.0, params[AMP:AMP + 1] * jnp.exp(-params[RATE:RATE + 1] * (jnp.maximum(gap, 0.0) * rows)), 0.0)
    mixed, energy = join(y, value_rows, states, weights, params)
    energy = lax.psum(energy, "tensor")
    return scaled(mixed, energy, norm_gain[None, :], width)


def solution(mesh):
    def whole(*args):
        return jax.shard_map(
            functools.partial(local, width=args[0].shape[1]),
            mesh=mesh,
            in_specs=(
                P("context", "tensor"),
                P("context", "tensor"),
                P("context", "tensor"),
                P(None, "tensor"),
                P(None, "tensor"),
                P("tensor", None),
                P("tensor", None),
                P("tensor"),
                P("tensor"),
            ),
            out_specs=P("context", "tensor"),
            check_vma=False,
        )(*args)

    return whole
```

time: 123 us -> 107 us (0.87)
  local copies, waits for them, and re-layouts: 27 us -> 5.37 us
  Pallas kernels: 51 us -> 63.1 us
  other arithmetic: 9.6 us -> 2.09 us
  blocking collectives: 31.5 us -> 33.2 us
    unnamed x22 -> x6, local copies, waits for them, and re-layouts: 24.6 us -> 1.72 us
    convert_element_type x1 -> x0, other arithmetic: 8.74 us -> none  [local(): (mixed.astype(F32) * scale[:, None] * norm_gain[None, :]).astype(BF16)]
    pallas_call x1 -> x2, Pallas kernels: 38.2 us -> 44.4 us  [the longest x1 34.5 us: mix(): pl.pallas_call(mix_kernel, grid=(strips + 1,), out_shape=(jax.ShapeDtypeS...]
    pallas_call x1, Pallas kernels: 10.8 us -> 14.2 us  [join(): pl.pallas_call(join_kernel, grid=(chans // wide,), out_shape=(jax.ShapeDt...]
    pallas_call x1, Pallas kernels: 1.91 us -> 4.39 us  [edge(): pl.pallas_call(edge_kernel, grid=(chans // wide,), out_shape=jax.ShapeDty...]
  transfers between devices with their start and end apart: 1 -> 1, of which waited for: 1 -> 0; matrix products, arithmetic and copies ran while one was open for 0% -> 2% of each run, Pallas kernels for 0% -> 0%
where the time goes in v3:
time: 107 us; the launch traced here: 106 us
  Pallas kernels  63.1 us (59%)
  blocking collectives  33.2 us (31%)
  local copies, waits for them, and re-layouts  5.37 us (5%)
  starting transfers between devices  2.38 us (2%)
  other arithmetic  2.09 us (2%)
    pallas_call x1, Pallas kernels, mix(): pl.pallas_call(mix_kernel, grid=(strips + 1,), out_shape=(jax.ShapeDtypeS...  34.5 us
    all_gather x1, blocking collectives, local(): states = lax.all_gather(state, 'context')  20.4 us
    pallas_call x1, Pallas kernels, join(): pl.pallas_call(join_kernel, grid=(chans // wide,), out_shape=(jax.ShapeDt...  14.2 us
    psum x1, blocking collectives, local(): energy = lax.psum(energy, 'tensor')  12.8 us
    pallas_call x1, Pallas kernels, scaled(): pl.pallas_call(functools.partial(scale_kernel, width=width), grid=(rows /...  9.96 us
    pallas_call x1, Pallas kernels, edge(): pl.pallas_call(edge_kernel, grid=(chans // wide,), out_shape=jax.ShapeDty...  4.39 us
    ppermute x1, starting transfers between devices, passed_along(): lax.ppermute(value, axis, [(source, source + steps) for source in range(c...  2.38 us
  transfers between devices with their start and end apart: 1, of which 0 were waited for; matrix products, arithmetic and copies ran while one was open for 2% of the time, Pallas kernels for 0%

profile of v3, /device:TPU:0, one launch (start us, length us, event | category | flops | bytes accessed | tf_op | source)
XLA Modules:
  0.0 106.2 jit_solution(6277571915174073657)
XLA Ops:
  0.0 0.8 copy.13
  0.8 0.7 fusion
  1.5 0.1 copy.14
  1.6 0.1 reshape.33
  1.7 0.1 reshape.32
  1.8 0.9 broadcast_in_dim.25
  2.7 0.3 reshape.31
  3.0 2.0 %concatenate.3.taps.params.late_params = f32[16,2048]{1,0:T(8,128)} concatenate(f32[7,2048]{1,0:T(8,128)S(1)} %reshape.31, f32[1,2048]{1,0:T(1,128)S(1)} %reshape.32, f32[1,2048]{1,0:T(1,128)S(1)} %reshape.33, f32[1,2048]{1,0:T(1,128)} %bitcast.7, f32[6,2048]{1,0:T(8,128)S(1)} %broadcast_in_dim.27), dimensions={0} | concatenate | bytes 262144 | tf_op jit(solution)/shard_map/concatenate | solution.py:303
  4.9 4.4 %edge.1 = bf16[144,2048]{1,0:T(8,128)(2,1)} custom-call(bf16[2048,2048]{1,0:T(8,128)(2,1)} %q.3, bf16[2048,2048]{1,0:T(8,128)(2,1)} %k.3, bf16[2048,2048]{1,0:T(8,128)(2,1)} %v.5, f32[16,2048]{1,0:T(8,128)} %concatenate.3.taps.params.late_params), custom_call_target="tpu_custom_call" | custom-call | tf_op jit(solution)/shard_map/edge/pallas_call | solution.py:56
  9.3 2.4 %collective-permute-start = (bf16[144,2048]{1,0:T(8,128)(2,1)}, bf16[144,2048]{1,0:T(8,128)(2,1)S(1)}, u32[]{:S(2)}, u32[]{:S(2)}) collective-permute-start(bf16[144,2048]{1,0:T(8,128)(2,1)} %edge.1), channel_id=1, source_target_pairs={{0,4},{4,8},{8,12},{12,16},{16,20},{20,24},{24,28},{1,5},{5,9},{9,... | collective-permute-start | bytes 1769480 | tf_op jit(solution)/shard_map/ppermute | solution.py:33
  11.7 0.0 copy-done
  11.7 0.1 copy.15
  11.9 0.6 convert_bitcast_fusion.medium_taps
  12.5 0.1 mul.43
  12.6 0.1 copy.17
  12.7 0.1 neg.16
  12.8 0.7 multiply_select_fusion.weights
  13.5 0.0 collective-permute-done.halo
  13.5 0.8 copy-done.1
  14.3 34.5 %mix.1 = (bf16[2048,2048]{1,0:T(8,128)(2,1)}, bf16[16,2048]{1,0:T(8,128)(2,1)}) custom-call(bf16[2048,2048]{1,0:T(8,128)(2,1)} %q.3, bf16[2048,2048]{1,0:T(8,128)(2,1)} %k.3, bf16[2048,2048]{1,0:T(8,128)(2,1)} %v.5, bf16[144,2048]{1,0:T(8,128)(2,1)} %copy-done.1, f32[16,2048]{1,0:T(8,128)} %concatenate.3.taps.params.late_params, ...), custom_call_target="tpu_custom_call" | custom-call | flops 8589934592 | bytes 33554432 | tf_op jit(solution)/shard_map/mix/pallas_call | solution.py:196
  48.8 20.4 %all-gather = bf16[128,2048]{1,0:T(8,128)(2,1)} all-gather(bf16[16,2048]{1,0:T(8,128)(2,1)} %get-tuple-element.10), channel_id=2, replica_groups=mesh['context'=8,'tensor'=4] {'context'}, dimensions={0}, use_global_device_ids=true | all-gather | bytes 589824 | tf_op jit(solution)/shard_map/all_gather | solution.py:309
  69.2 14.2 %join.1 = (bf16[2048,2048]{1,0:T(8,128)(2,1)}, f32[1,2048]{1,0:T(1,128)}) custom-call(bf16[2048,2048]{1,0:T(8,128)(2,1)} %get-tuple-element.9.y, bf16[2048,2048]{1,0:T(8,128)(2,1)} %v.5, bf16[8,16,2048]{2,1,0:T(8,128)(2,1)} %bitcast.5, f32[8,2048]{1,0:T(8,128)} %multiply_select_fusion.weights, f32[16,2048]{1,0:T(8,128)} %concatenate.3.taps.params.late_params), custom_call_target="tpu_custom_call" | custom-call | flops 2147483648 | bytes 25165824 | tf_op jit(solution)/shard_map/join/pallas_call | solution.py:259
  83.4 12.8 %psum.7.energy = f32[1,2048]{1,0:T(1,128)} all-reduce(f32[1,2048]{1,0:T(1,128)} %get-tuple-element.12), channel_id=1, replica_groups=mesh['context'=8,'tensor'=4] {'tensor'}, use_global_device_ids=true, to_apply=%region_0.1 | all-reduce | flops 2048 | bytes 16384 | tf_op jit(solution)/shard_map/psum | solution.py:314
  96.3 10.0 %scale.1 = bf16[2048,2048]{1,0:T(8,128)(2,1)} custom-call(bf16[2048,2048]{1,0:T(8,128)(2,1)} %get-tuple-element.11.mixed, f32[1,2048]{1,0:T(1,128)} %psum.7.energy, f32[1,2048]{1,0:T(1,128)} %bitcast.6), custom_call_target="tpu_custom_call" | custom-call | tf_op jit(solution)/shard_map/scale/pallas_call | solution.py:288
  (5 shorter events, 0.0 us)
Async XLA Ops:
  4.9 6.8 %copy-start = (bf16[128,128]{1,0:T(8,128)(2,1)S(1)}, bf16[128,128]{1,0:T(8,128)(2,1)}, u32[]{:S(2)}) copy-start(bf16[128,128]{1,0:T(8,128)(2,1)} %param.13) | copy-start | bytes 98308
  9.3 4.2 %collective-permute-start = (bf16[144,2048]{1,0:T(8,128)(2,1)}, bf16[144,2048]{1,0:T(8,128)(2,1)S(1)}, u32[]{:S(2)}, u32[]{:S(2)}) collective-permute-start(bf16[144,2048]{1,0:T(8,128)(2,1)} %edge.1), channel_id=1, source_target_pairs={{0,4},{4,8},{8,12},{12,16},{16,20},{20,24},{24,28},{1,5},{5,9},{9,... | collective-permute-start | bytes 1769480 | tf_op jit(solution)/shard_map/ppermute | solution.py:33
  13.5 0.8 copy-start.1

commit v4 on v3

--- a/solution.py
+++ b/solution.py
@@ -16,9 +16,11 @@
 SHORT = 7
 RATE, AMP, SKIP = SHORT, SHORT + 1, SHORT + 2
 EARLY = 0
-JOIN_STRIP = 256
-MIX_VMEM = 60 << 20
-JOIN_VMEM = 60 << 20
+EDGE_PARTS = 1
+JOIN_STRIP = 512
+TALL = 256
+MIX_VMEM = 24 << 20
+JOIN_VMEM = 24 << 20
 F32 = jnp.float32
 BF16 = jnp.bfloat16
 
@@ -33,9 +35,13 @@
     return lax.ppermute(value, axis, [(source, source + steps) for source in range(count - steps)])
 
 
-def edge_kernel(q, k, v, taps, halo_out, gated):
-    rows = q.shape[0]
+def edge_kernel(q, k, v, short_filter, halo_out, gated):
+    rows, wide = q.shape
     begin = rows - LANES
+    pack = wide // GROUP_CH
+    spread = (lax.broadcasted_iota(jnp.int32, (pack, wide), 1) // GROUP_CH
+              == lax.broadcasted_iota(jnp.int32, (pack, wide), 0)).astype(F32)
+    taps = jnp.dot(short_filter[...], spread, precision=lax.Precision.HIGHEST, preferred_element_type=F32)
     kv = k[begin - 16:, :].astype(F32) * v[begin - 16:, :].astype(F32)
     gated[...] = kv
     total = taps[0:1, :] * gated[16:, :]
@@ -47,22 +53,27 @@
     halo_out[LANES:LANES + 16, :] = jnp.concatenate([high, last - high], axis=0).astype(BF16)
 
 
-def edge(q, k, v, params):
+def edge(q, k, v, short_filter):
     rows, chans = q.shape
-    wide = math.gcd(chans, 512)
+    wide = chans // EDGE_PARTS
     tall = math.gcd(rows, 256)
     last = pl.BlockSpec((tall, wide), lambda i: (rows // tall - 1, i))
-    column = lambda height: pl.BlockSpec((height, wide), lambda i: (0, i))
+    column = lambda height, width: pl.BlockSpec((height, width), lambda i: (0, i))
+    if wide // GROUP_CH % LANES:
+        short_filter = short_filter.reshape(SHORT, EDGE_PARTS, wide // GROUP_CH).transpose(1, 0, 2)
+        tap_spec = pl.BlockSpec((pl.Squeezed(), SHORT, wide // GROUP_CH), lambda i: (i, 0, 0))
+    else:
+        tap_spec = column(SHORT, wide // GROUP_CH)
     return pl.pallas_call(
         edge_kernel,
-        grid=(chans // wide,),
+        grid=(EDGE_PARTS,),
         out_shape=jax.ShapeDtypeStruct((LANES + 16, chans), BF16),
-        in_specs=[last] * 3 + [column(params.shape[0])],
-        out_specs=column(LANES + 16),
+        in_specs=[last] * 3 + [tap_spec],
+        out_specs=column(LANES + 16, wide),
         scratch_shapes=[pltpu.VMEM((LANES + 16, wide), F32)],
         compiler_params=pltpu.CompilerParams(vmem_limit_bytes=MIX_VMEM),
         name="edge",
-    )(q, k, v, params)
+    )(q, k, v, short_filter)
 
 
 def mix_kernel(q, k, v, halo, params, late_params, medium_taps, y_out, state_out, gated, y_t, seconds,
@@ -220,31 +231,26 @@
     def _():
         energy[...] = jnp.zeros_like(energy)
 
-    row_i = lax.broadcasted_iota(jnp.int32, (LANES, LANES), 0)
-    col_i = lax.broadcasted_iota(jnp.int32, (LANES, LANES), 1)
-    own = row_i // GROUP_CH == col_i // MODES
-    time = row_i.astype(F32) + 1.0
+    own = (lax.broadcasted_iota(jnp.int32, (WIDE, WIDE), 0) // GROUP_CH
+           == lax.broadcasted_iota(jnp.int32, (WIDE, WIDE), 1) // MODES)
+    time = lax.broadcasted_iota(jnp.int32, (TALL, WIDE), 0).astype(F32) + 1.0
     entry = jnp.zeros((GROUP_CH, wide), F32)
     for source in range(states.shape[0]):
         entry = entry + weights[source:source + 1, :] * states[source].astype(F32)
-    entries, leads = [], []
-    for s in range(wide // LANES):
-        here = slice(s * LANES, (s + 1) * LANES)
-        spread = jnp.where(own, jnp.concatenate([entry[:, here]] * PACK, axis=0), 0.0)
-        entries.append(jnp.concatenate(split2(spread), axis=1))
-        leads.append(jnp.exp(-params[RATE:RATE + 1, here] * time))
-    for b in range(rows // LANES):
-        part = pl.ds(b * LANES, LANES)
-        total = energy[part, :]
-        for s in range(wide // LANES):
-            here = slice(s * LANES, (s + 1) * LANES)
-            lead = (leads[s] * jnp.exp(-params[RATE:RATE + 1, here] * float(b * LANES))).astype(BF16)
-            carried = lax.dot_general(jnp.concatenate([lead, lead], axis=1), entries[s],
-                                      (((1,), (1,)), ((), ())), preferred_element_type=F32)
+    for s in range(wide // WIDE):
+        here = slice(s * WIDE, (s + 1) * WIDE)
+        rate = params[RATE:RATE + 1, here]
+        spread = jnp.concatenate([entry[:, here]] * (WIDE // GROUP_CH), axis=0)
+        spread = jnp.where(own, spread, 0.0).astype(BF16)
+        lead = jnp.exp(-rate * time)
+        for b in range(rows // TALL):
+            part = pl.ds(b * TALL, TALL)
+            faded = (lead * jnp.exp(-rate * float(b * TALL))).astype(BF16)
+            carried = lax.dot_general(faded, spread, (((1,), (1,)), ((), ())), preferred_element_type=F32)
             mixed = v[part, here].astype(F32) * (y[part, here].astype(F32) + carried)
             mixed_out[part, here] = mixed.astype(BF16)
-            total = total + mixed * mixed
-        energy[part, :] = total
+            square = mixed * mixed
+            energy[part, :] += square[:, :LANES] + square[:, LANES:]
 
     @pl.when(step == pl.num_programs(0) - 1)
     def _():
@@ -274,7 +280,8 @@
     rows, chans = mixed.shape
     for begin in range(0, rows, LANES):
         part = pl.ds(begin, LANES)
-        scale = lax.rsqrt(energy[:, begin:begin + LANES] / width + 1e-06)
+        scale = jnp.sum(energy[:, begin:begin + LANES], axis=0, keepdims=True)
+        scale = lax.rsqrt(scale / width + 1e-06)
         scale = jnp.broadcast_to(scale, (LANES, LANES)).T
         for left in range(0, chans, LANES):
             here = slice(left, left + LANES)
@@ -283,13 +290,13 @@
 
 def scaled(mixed, energy, gain, width):
     rows, chans = mixed.shape
-    tall = math.gcd(rows, 256)
+    tall = math.gcd(rows, 512)
     block = pl.BlockSpec((tall, chans), lambda i: (i, 0))
     return pl.pallas_call(
         functools.partial(scale_kernel, width=width),
         grid=(rows // tall,),
         out_shape=jax.ShapeDtypeStruct((rows, chans), BF16),
-        in_specs=[block, pl.BlockSpec((1, tall), lambda i: (0, i)), pl.BlockSpec((1, chans), lambda i: (0, 0))],
+        in_specs=[block, pl.BlockSpec((energy.shape[0], tall), lambda i: (0, i)), pl.BlockSpec((1, chans), lambda i: (0, 0))],
         out_specs=block,
         compiler_params=pltpu.CompilerParams(vmem_limit_bytes=JOIN_VMEM),
         name="scale",
@@ -299,19 +306,23 @@
 def local(queries, key_rows, value_rows, short_filter, medium_filter, decays, residue, skip_gain,
           norm_gain, width):
     rows, chans = queries.shape
+    queries, key_rows, value_rows = (pltpu.with_memory_space_constraint(array, pltpu.HBM)
+                                     for array in (queries, key_rows, value_rows))
     amplitude = residue * jnp.sqrt(-jnp.expm1(-2.0 * decays))
     params = jnp.concatenate([
         jnp.repeat(short_filter, GROUP_CH, axis=1),
         decays.reshape(1, chans), amplitude.reshape(1, chans), skip_gain[None, :],
         jnp.zeros((16 - SHORT - 3, chans), F32)], axis=0)
-    halo = passed_along(edge(queries, key_rows, value_rows, params), "context", 1)
+    halo = passed_along(edge(queries, key_rows, value_rows, short_filter), "context", 1)
     y, state = mix(queries, key_rows, value_rows, halo, params, medium_filter.T.astype(F32))
     states = lax.all_gather(state, "context")
     count = lax.axis_size("context")
     gap = (lax.axis_index("context") - 1 - jnp.arange(count)).astype(F32)[:, None]
     weights = jnp.where(gap >= 0.0, params[AMP:AMP + 1] * jnp.exp(-params[RATE:RATE + 1] * (jnp.maximum(gap, 0.0) * rows)), 0.0)
+    y = pltpu.with_memory_space_constraint(y, pltpu.VMEM)
     mixed, energy = join(y, value_rows, states, weights, params)
-    energy = lax.psum(energy, "tensor")
+    energy = lax.all_gather(energy, "tensor", tiled=True)
+    mixed = pltpu.with_memory_space_constraint(mixed, pltpu.VMEM)
     return scaled(mixed, energy, norm_gain[None, :], width)
 
 

time: 107 us -> 90.2 us (0.84)
  Pallas kernels: 63.1 us -> 52.5 us
  local copies, waits for them, and re-layouts: 5.37 us -> 1.99 us
  other arithmetic: 2.09 us -> 0.13 us
    all_gather x0 -> x1, blocking collectives: none -> 13.3 us  [local(): energy = lax.all_gather(energy, 'tensor', tiled=True)]
    psum x1 -> x0, blocking collectives: 12.8 us -> none  [local(): energy = lax.psum(energy, 'tensor')]
    pallas_call x1, Pallas kernels: 14.2 us -> 8.63 us  [join(): pl.pallas_call(join_kernel, grid=(chans // wide,), out_shape=(jax.ShapeDt...]
    pallas_call x1, Pallas kernels: 9.96 us -> 4.6 us  [scaled(): pl.pallas_call(functools.partial(scale_kernel, width=width), grid=(rows /...]
    concatenate x1, local copies, waits for them, and re-layouts: 1.98 us -> 0.08 us  [local(): jnp.concatenate([jnp.repeat(short_filter, GROUP_CH, axis=1), decays.resha...]
    pallas_call x1, Pallas kernels: 34.5 us -> 35.9 us  [mix(): pl.pallas_call(mix_kernel, grid=(strips + 1,), out_shape=(jax.ShapeDtypeS...]
  transfers between devices with their start and end apart: 1 -> 1, of which waited for: 0 -> 1; matrix products, arithmetic and copies ran while one was open for 2% -> 2% of each run, Pallas kernels for 0% -> 0%
where the time goes in v4:
time: 90.2 us; the launch traced here: 90 us
  Pallas kernels  52.5 us (58%)
  blocking collectives  32.8 us (36%)
  starting transfers between devices  2.39 us (3%)
  local copies, waits for them, and re-layouts  1.99 us (2%)
    pallas_call x1, Pallas kernels, mix(): pl.pallas_call(mix_kernel, grid=(strips + 1,), out_shape=(jax.ShapeDtypeS...  35.9 us
    all_gather x1, blocking collectives, local(): states = lax.all_gather(state, 'context')  19.4 us
    all_gather x1, blocking collectives, local(): energy = lax.all_gather(energy, 'tensor', tiled=True)  13.3 us
    pallas_call x1, Pallas kernels, join(): pl.pallas_call(join_kernel, grid=(chans // wide,), out_shape=(jax.ShapeDt...  8.63 us
    pallas_call x1, Pallas kernels, scaled(): pl.pallas_call(functools.partial(scale_kernel, width=width), grid=(rows /...  4.6 us
    pallas_call x1, Pallas kernels, edge(): pl.pallas_call(edge_kernel, grid=(EDGE_PARTS,), out_shape=jax.ShapeDtypeS...  3.33 us
    ppermute x1, starting transfers between devices, passed_along(): lax.ppermute(value, axis, [(source, source + steps) for source in range(c...  2.39 us
  transfers between devices with their start and end apart: 1, of which 1 were waited for; matrix products, arithmetic and copies ran while one was open for 2% of the time, Pallas kernels for 0%

profile of v4, /device:TPU:0, one launch (start us, length us, event | category | flops | bytes accessed | tf_op | source)
XLA Modules:
  0.0 90.0 jit_solution(397480343996383032)
XLA Ops:
  0.0 0.7 copy-done
  0.7 0.0 copy-start.5
  0.7 3.3 %edge.1 = bf16[144,2048]{1,0:T(8,128)(2,1)S(1)} custom-call(bf16[2048,2048]{1,0:T(8,128)(2,1)} %q.3, bf16[2048,2048]{1,0:T(8,128)(2,1)} %k.3, bf16[2048,2048]{1,0:T(8,128)(2,1)} %v.5, f32[7,128]{1,0:T(8,128)S(1)} %copy-done), custom_call_target="tpu_custom_call" | custom-call | tf_op jit(solution)/shard_map/edge/pallas_call | solution.py:67
  4.0 2.4 %collective-permute-start = (bf16[144,2048]{1,0:T(8,128)(2,1)S(1)}, bf16[144,2048]{1,0:T(8,128)(2,1)S(1)}, u32[]{:S(2)}, u32[]{:S(2)}) collective-permute-start(bf16[144,2048]{1,0:T(8,128)(2,1)S(1)} %edge.1), channel_id=1, source_target_pairs={{0,4},{4,8},{8,12},{12,16},{16,20},{20,24},{24,28},{1,5},{5,9},{9,... | collective-permute-start | bytes 1769480 | tf_op jit(solution)/shard_map/ppermute | solution.py:35
  6.5 0.1 copy.20
  6.6 0.0 copy-done.4
  6.6 0.0 copy-done.6
  6.7 0.1 copy.19
  6.8 0.1 mul.43
  6.8 0.1 reshape.33
  6.9 0.1 copy.18
  7.0 0.1 copy.22
  7.1 0.1 neg.16
  7.2 0.1 reshape.32
  7.3 0.2 broadcast_in_dim.25
  7.5 0.3 reshape.31
  7.8 0.1 concatenate.3.params.late_params
  7.9 0.1 multiply_select_fusion.weights
  8.0 0.1 collective-permute-done.halo
  8.0 35.9 %mix.1 = (bf16[2048,2048]{1,0:T(8,128)(2,1)S(1)}, bf16[16,2048]{1,0:T(8,128)(2,1)S(1)}) custom-call(bf16[2048,2048]{1,0:T(8,128)(2,1)} %q.3, bf16[2048,2048]{1,0:T(8,128)(2,1)} %k.3, bf16[2048,2048]{1,0:T(8,128)(2,1)} %v.5, bf16[144,2048]{1,0:T(8,128)(2,1)S(1)} %collective-permute-done.halo, f32[16,2048]{1,0:T(8,128)S(1)} %concatenate.3.params.late_params, ...), custom_call_target="tpu_custom_call" | custom-call | flops 8589934592 | bytes 33554432 | tf_op jit(solution)/shard_map/mix/pallas_call | solution.py:207
  44.0 19.4 %all-gather = bf16[128,2048]{1,0:T(8,128)(2,1)S(1)} all-gather(bf16[16,2048]{1,0:T(8,128)(2,1)S(1)} %get-tuple-element.10), channel_id=2, replica_groups=mesh['context'=8,'tensor'=4] {'context'}, dimensions={0}, use_global_device_ids=true | all-gather | bytes 589824 | tf_op jit(solution)/shard_map/all_gather | solution.py:318
  63.4 8.6 %join.1 = (bf16[2048,2048]{1,0:T(8,128)(2,1)S(1)}, f32[1,2048]{1,0:T(1,128)S(1)}) custom-call(bf16[2048,2048]{1,0:T(8,128)(2,1)S(1)} %get-tuple-element.9.y, bf16[2048,2048]{1,0:T(8,128)(2,1)} %v.5, bf16[8,16,2048]{2,1,0:T(8,128)(2,1)S(1)} %bitcast.9, f32[8,2048]{1,0:T(8,128)S(1)} %multiply_select_fusion.weights, f32[16,2048]{1,0:T(8,128)S(1)} %concatenate.3.params.late_params), custom_call_target="tpu_custom_call" | custom-call | flops 2147483648 | bytes 25165824 | tf_op jit(solution)/shard_map/join/pallas_call | solution.py:265
  72.0 13.3 %all-gather.1 = f32[4,1,2048]{2,1,0:T(1,128)S(1)} all-gather(f32[1,1,2048]{2,1,0:T(1,128)S(1)} %bitcast.12), channel_id=1, replica_groups=mesh['context'=8,'tensor'=4] {'tensor'}, dimensions={0}, use_global_device_ids=true | all-gather | bytes 40960 | tf_op jit(solution)/shard_map/all_gather | solution.py:324
  85.4 4.6 %scale.1 = bf16[2048,2048]{1,0:T(8,128)(2,1)} custom-call(bf16[2048,2048]{1,0:T(8,128)(2,1)S(1)} %get-tuple-element.11.mixed, f32[4,2048]{1,0:T(4,128)S(1)} %bitcast.10, f32[1,2048]{1,0:T(1,128)S(1)} %bitcast.11), custom_call_target="tpu_custom_call" | custom-call | tf_op jit(solution)/shard_map/scale/pallas_call | solution.py:295
  (16 shorter events, 0.1 us)
Async XLA Ops:
  0.0 0.7 copy-start
  0.7 5.8 %copy-start.3 = (bf16[128,128]{1,0:T(8,128)(2,1)S(1)}, bf16[128,128]{1,0:T(8,128)(2,1)}, u32[]{:S(2)}) copy-start(bf16[128,128]{1,0:T(8,128)(2,1)} %param.13) | copy-start | bytes 98308
  0.7 5.9 %copy-start.4 = (f32[128,16]{0,1:T(8,128)S(1)}, f32[128,16]{0,1:T(8,128)}, u32[]{:S(2)}) copy-start(f32[128,16]{0,1:T(8,128)} %param.14) | copy-start | bytes 24580
  0.7 5.9 %copy-start.6 = (f32[128,16]{0,1:T(8,128)S(1)}, f32[128,16]{0,1:T(8,128)}, u32[]{:S(2)}) copy-start(f32[128,16]{0,1:T(8,128)} %param.15) | copy-start | bytes 24580
  0.7 6.6 %copy-start.1 = (f32[7,128]{1,0:T(8,128)S(1)}, f32[7,128]{1,0:T(8,128)}, u32[]{:S(2)}) copy-start(f32[7,128]{1,0:T(8,128)} %short_filter.1) | copy-start | bytes 10756
  0.7 7.1 %copy-start.5 = (f32[2048]{0:T(1024)S(1)}, f32[2048]{0:T(1024)}, u32[]{:S(2)}) copy-start(f32[2048]{0:T(1024)} %param.16) | copy-start | bytes 24580
  4.0 4.0 %collective-permute-start = (bf16[144,2048]{1,0:T(8,128)(2,1)S(1)}, bf16[144,2048]{1,0:T(8,128)(2,1)S(1)}, u32[]{:S(2)}, u32[]{:S(2)}) collective-permute-start(bf16[144,2048]{1,0:T(8,128)(2,1)S(1)} %edge.1), channel_id=1, source_target_pairs={{0,4},{4,8},{8,12},{12,16},{16,20},{20,24},{24,28},{1,5},{5,9},{9,... | collective-permute-start | bytes 1769480 | tf_op jit(solution)/shard_map/ppermute | solution.py:35
  63.4 22.0 %copy-start.2 = (f32[2048]{0:T(1024)S(1)}, f32[2048]{0:T(1024)}, u32[]{:S(2)}) copy-start(f32[2048]{0:T(1024)} %param.17) | copy-start | bytes 24580

commit v5 on v4

--- a/solution.py
+++ b/solution.py
@@ -15,10 +15,10 @@
 MODES = 16
 SHORT = 7
 RATE, AMP, SKIP = SHORT, SHORT + 1, SHORT + 2
-EARLY = 0
+GATE_STRIP = 256
+MIX_STRIP = 256
 EDGE_PARTS = 1
 JOIN_STRIP = 512
-TALL = 256
 MIX_VMEM = 24 << 20
 JOIN_VMEM = 24 << 20
 F32 = jnp.float32
@@ -76,28 +76,67 @@
     )(q, k, v, short_filter)
 
 
-def mix_kernel(q, k, v, halo, params, late_params, medium_taps, y_out, state_out, gated, y_t, seconds,
-               first_a, key_a, first_b, key_b):
-    parity = pl.program_id(0) % 2
-
-    @pl.when(parity == 0)
-    def _():
-        mix_strip(q, k, v, halo, params, late_params, medium_taps, y_out, state_out, gated, y_t, seconds,
-                  (first_a, key_a), (first_b, key_b))
-
-    @pl.when(parity == 1)
-    def _():
-        mix_strip(q, k, v, halo, params, late_params, medium_taps, y_out, state_out, gated, y_t, seconds,
-                  (first_b, key_b), (first_a, key_a))
-
-
-def mix_strip(q, k, v, halo, params, late_params, medium_taps, y_out, state_out, gated, y_t, seconds,
-              fresh_refs, ready_refs):
-    rows = q.shape[0]
+def gate_kernel(q, k, v, params, first_out, key_out, *gated_refs):
+    rows, wide = q.shape
+    for s, gated in enumerate(gated_refs):
+        here = slice(s * LANES, (s + 1) * LANES)
+        taps = params[:, here]
+        gated[0:8, :] = jnp.zeros((8, LANES), F32)
+        for begin in range(0, rows, LANES):
+            part = pl.ds(begin, LANES)
+            keys = k[part, here]
+            fresh = keys.astype(F32) * v[part, here].astype(F32)
+            gated[pl.ds(begin + 8, LANES), :] = fresh
+            total = taps[0:1, :] * fresh
+            for delay in range(1, SHORT):
+                total = total + taps[delay:delay + 1, :] * gated[pl.ds(begin + 8 - delay, LANES), :]
+            first = (q[part, here].astype(F32) * total).astype(BF16)
+            first_out[here, begin:begin + LANES] = first.T
+            key_out[here, begin:begin + LANES] = keys.T
+
+
+def gate(q, k, v, params):
+    rows, chans = q.shape
+    column = lambda height: pl.BlockSpec((height, GATE_STRIP), lambda i: (0, i))
+    down = pl.BlockSpec((GATE_STRIP, rows), lambda i: (i, 0))
+    return pl.pallas_call(
+        gate_kernel,
+        grid=(chans // GATE_STRIP,),
+        out_shape=(jax.ShapeDtypeStruct((chans, rows), BF16),) * 2,
+        in_specs=[column(rows)] * 3 + [column(params.shape[0])],
+        out_specs=(down, down),
+        scratch_shapes=[pltpu.VMEM((rows + 8, LANES), F32)] * (GATE_STRIP // LANES),
+        compiler_params=pltpu.CompilerParams(vmem_limit_bytes=MIX_VMEM),
+        cost_estimate=pl.CostEstimate(flops=64 * rows * chans, bytes_accessed=10 * rows * chans, transcendentals=0),
+        name="gate",
+    )(q, k, v, params)
+
+
+def summed(value, axis):
+    count = lax.axis_size(axis)
+    if count & (count - 1):
+        return lax.psum(value, axis)
+    step = 1
+    while step < count:
+        value = value + lax.ppermute(value, axis, [(source, source ^ step) for source in range(count)])
+        step *= 2
+    return value
+
+
+def mix_kernel(first, keys_t, halo, q, k, v, params, medium_taps, y_out, carry_out, state_out, *scratch):
+    strips = first.shape[0] // LANES
+    for s in range(strips):
+        here = slice(s * LANES, (s + 1) * LANES)
+        mix_strip(first.at[here, :], keys_t.at[here, :], halo.at[:, here], q.at[:, here], k.at[:, here], v.at[:, here],
+                  params.at[:, here], medium_taps.at[s * PACK:(s + 1) * PACK, :],
+                  y_out.at[:, here], carry_out.at[:, here], state_out.at[:, here], *scratch[4 * s:4 * s + 4])
+
+
+def mix_strip(first_t, key_t, halo, q, k, v, late_params, medium_taps, y_out, carry_out, state_out, y_t, seconds,
+              gated, start):
+    rows = first_t.shape[1]
     blocks = rows // WIDE
     halves = rows // LANES
-    next_first, next_key = fresh_refs
-    first_t, key_t = ready_refs
     row_i = lax.broadcasted_iota(jnp.int32, (LANES, LANES), 0)
     col_i = lax.broadcasted_iota(jnp.int32, (LANES, LANES), 1)
     causal = col_i >= row_i
@@ -105,21 +144,22 @@
     time_down = lax.broadcasted_iota(jnp.int32, (WIDE, LANES), 0).astype(F32)
     time_along = lax.broadcasted_iota(jnp.int32, (LANES, WIDE), 1).astype(F32)
     lane_group = lax.broadcasted_iota(jnp.int32, (WIDE, LANES), 1) // MODES
-    taps = params[...]
     late = late_params[...]
 
-    def gate_first(b):
-        begin = b * LANES
-        part = pl.ds(begin, LANES)
-        keys = k[part, :]
-        fresh = keys.astype(F32) * v[part, :].astype(F32)
-        gated[pl.ds(begin + 8, LANES), :] = fresh
-        total = taps[0:1, :] * fresh
-        for delay in range(1, SHORT):
-            total = total + taps[delay:delay + 1, :] * gated[pl.ds(begin + 8 - delay, LANES), :]
-        first = (q[part, :].astype(F32) * total).astype(BF16)
-        next_first[:, begin + LANES:begin + 2 * LANES] = first.T
-        next_key[:, begin:begin + LANES] = keys.T
+    gated[0:8, :] = halo[LANES:LANES + 8, :].astype(F32) + halo[LANES + 8:LANES + 16, :].astype(F32)
+    gated[8:24, :] = k[...].astype(F32) * v[...].astype(F32)
+    total = late[0:1, :] * gated[8:24, :]
+    for delay in range(1, SHORT):
+        total = total + late[delay:delay + 1, :] * gated[8 - delay:24 - delay, :]
+    opening = (q[...].astype(F32) * total).astype(BF16)
+    opening = jnp.concatenate([opening, jnp.zeros((LANES - 16, LANES), BF16)], axis=0).T
+    start[:, 0:LANES] = halo[0:LANES, :].T
+    start[:, LANES:2 * LANES] = jnp.where(col_i < 16, opening, first_t[:, 0:LANES])
+
+    def tile(chans, b):
+        if b < 1:
+            return start[chans, (b + 1) * LANES:(b + 2) * LANES]
+        return first_t[chans, b * LANES:(b + 1) * LANES]
 
     def medium_of(g):
         chans = pl.ds(g * GROUP_CH, GROUP_CH)
@@ -127,7 +167,7 @@
         turned = pltpu.roll(turned, 0, 1, stride=1, stride_axis=0)
         medium_w = jnp.concatenate(
             [jnp.where(causal, 0.0, turned), jnp.where(causal, turned, 0.0)], axis=0).astype(BF16)
-        window = jnp.concatenate([first_t[chans, b * LANES:(b + 2) * LANES] for b in range(halves)], axis=0)
+        window = jnp.concatenate([jnp.concatenate([tile(chans, b - 1), tile(chans, b)], axis=1) for b in range(halves)], axis=0)
         medium = jnp.dot(window, medium_w, preferred_element_type=F32)
         key = jnp.concatenate([key_t[chans, b * LANES:(b + 1) * LANES] for b in range(halves)], axis=0)
         second = (key.astype(F32) * medium).astype(BF16)
@@ -136,16 +176,8 @@
                     g * WIDE + (b % 2) * LANES:g * WIDE + (b % 2 + 1) * LANES] = (
                 second[b * GROUP_CH:(b + 1) * GROUP_CH])
 
-    gated[0:8, :] = halo[LANES:LANES + 8, :].astype(F32) + halo[LANES + 8:LANES + 16, :].astype(F32)
-    next_first[:, 0:LANES] = halo[0:LANES, :].T
-    early = EARLY * halves // 16
-    done = 0
     for g in range(PACK):
         medium_of(g)
-        goal = early * (g + 1) // PACK
-        for b in range(done, goal):
-            gate_first(b)
-        done = goal
 
     rate = late[RATE:RATE + 1, :]
     tails = jnp.exp(-rate * (WIDE - 1.0 - time_down)).astype(BF16)
@@ -153,18 +185,15 @@
     sums = jnp.dot(seconds[...], tails_w, preferred_element_type=F32)
     decay = jnp.exp(-rate * float(WIDE))
     state = jnp.zeros((GROUP_CH, LANES), F32)
-    states = []
     for b in range(blocks):
-        states.append(state)
+        carry_out[b * GROUP_CH:(b + 1) * GROUP_CH, :] = state
         state = decay * state + sums[b * GROUP_CH:(b + 1) * GROUP_CH, :]
     state_out[...] = state.astype(BF16)
-    carried = jnp.concatenate(split2(jnp.concatenate(states, axis=0)), axis=1)
 
     down = lambda row: jnp.broadcast_to(late[row:row + 1, :], (LANES, LANES)).T
     rate_t, amp_t, skip_t = down(RATE), down(AMP), down(SKIP)
     both = lambda half: jnp.concatenate([half, half], axis=1)
     power = both(amp_t) * jnp.exp(-both(rate_t) * time_along)
-    lead = (power * jnp.exp(-both(rate_t))).astype(BF16)
 
     def long_of(g):
         chans = pl.ds(g * GROUP_CH, GROUP_CH)
@@ -174,14 +203,8 @@
         near = jnp.where(causal, turned[:, :LANES], 0.0).astype(BF16)
         pieces = [jnp.concatenate([near, turned[:, LANES:].astype(BF16)], axis=1),
                   jnp.concatenate([zero, near], axis=1)]
-        lead_g = [lead[mine]]
-        if g > 0:
-            lead_g = [jnp.zeros((g * MODES, WIDE), BF16)] + lead_g
-        if g < PACK - 1:
-            lead_g = lead_g + [jnp.zeros(((PACK - 1 - g) * MODES, WIDE), BF16)]
         second = seconds[:, g * WIDE:(g + 1) * WIDE]
-        y = jnp.dot(jnp.concatenate([second, carried], axis=1),
-                    jnp.concatenate(pieces + lead_g + lead_g, axis=0), preferred_element_type=F32)
+        y = jnp.dot(second, jnp.concatenate(pieces, axis=0), preferred_element_type=F32)
         gain = both(skip_t[g * GROUP_CH:(g + 1) * GROUP_CH, :])
         gain = jnp.concatenate([gain] * blocks, axis=0)
         y = (y + gain * second.astype(F32)).astype(BF16)
@@ -190,40 +213,36 @@
 
     for g in range(PACK):
         long_of(g)
-        goal = early + (halves - early) * (g + 1) // PACK
-        for b in range(done, goal):
-            gate_first(b)
-        done = goal
     for begin in range(0, rows, LANES):
         y_out[pl.ds(begin, LANES), :] = y_t[:, begin:begin + LANES].T
 
 
-def mix(q, k, v, halo, params, medium_taps):
-    rows, chans = q.shape
-    strips = chans // LANES
-    ahead = lambda i: jnp.minimum(i, strips - 1)
-    behind = lambda i: jnp.maximum(i - 1, 0)
-    column = lambda height, of: pl.BlockSpec((height, LANES), lambda i: (0, of(i)))
+def mix(first, keys_t, halo, q, k, v, params, medium_taps):
+    chans, rows = first.shape
+    column = lambda height: pl.BlockSpec((height, MIX_STRIP), lambda i: (0, i))
+    down = lambda height, width: pl.BlockSpec((height, width), lambda i: (i, 0))
+    carried = rows // WIDE * GROUP_CH
     return pl.pallas_call(
         mix_kernel,
-        grid=(strips + 1,),
-        out_shape=(jax.ShapeDtypeStruct((rows, chans), BF16), jax.ShapeDtypeStruct((GROUP_CH, chans), BF16)),
-        in_specs=[column(rows, ahead)] * 3 + [
-            column(halo.shape[0], ahead), column(params.shape[0], ahead), column(params.shape[0], behind),
-            pl.BlockSpec((PACK, LANES), lambda i: (behind(i), 0))],
-        out_specs=(column(rows, behind), column(GROUP_CH, behind)),
+        grid=(chans // MIX_STRIP,),
+        out_shape=(jax.ShapeDtypeStruct((rows, chans), BF16), jax.ShapeDtypeStruct((carried, chans), F32),
+                   jax.ShapeDtypeStruct((GROUP_CH, chans), BF16)),
+        in_specs=[down(MIX_STRIP, rows)] * 2 + [column(halo.shape[0])] + [column(16)] * 3 + [
+            column(params.shape[0]), down(MIX_STRIP // GROUP_CH, LANES)],
+        out_specs=(column(rows), column(carried), column(GROUP_CH)),
         scratch_shapes=[
-            pltpu.VMEM((rows + 8, LANES), F32),
             pltpu.VMEM((LANES, rows), BF16),
             pltpu.VMEM((LANES, PACK * WIDE), BF16),
-        ] + [pltpu.VMEM((LANES, rows + LANES), BF16), pltpu.VMEM((LANES, rows), BF16)] * 2,
-        compiler_params=pltpu.CompilerParams(vmem_limit_bytes=MIX_VMEM),
-        cost_estimate=pl.CostEstimate(flops=8 * rows * chans * WIDE, bytes_accessed=8 * rows * chans, transcendentals=0),
+            pltpu.VMEM((24, LANES), F32),
+            pltpu.VMEM((LANES, 2 * LANES), BF16),
+        ] * (MIX_STRIP // LANES),
+        compiler_params=pltpu.CompilerParams(vmem_limit_bytes=JOIN_VMEM),
+        cost_estimate=pl.CostEstimate(flops=8 * rows * chans * WIDE, bytes_accessed=6 * rows * chans, transcendentals=0),
         name="mix",
-    )(q, k, v, halo, params, params, medium_taps)
-
-
-def join_kernel(y, v, states, weights, params, mixed_out, energy_out, energy):
+    )(first, keys_t, halo, q, k, v, params, medium_taps)
+
+
+def join_kernel(y, v, carry, states, weights, params, mixed_out, energy_out, energy):
     rows, wide = y.shape
     step = pl.program_id(0)
 
@@ -233,20 +252,21 @@
 
     own = (lax.broadcasted_iota(jnp.int32, (WIDE, WIDE), 0) // GROUP_CH
            == lax.broadcasted_iota(jnp.int32, (WIDE, WIDE), 1) // MODES)
-    time = lax.broadcasted_iota(jnp.int32, (TALL, WIDE), 0).astype(F32) + 1.0
+    time = lax.broadcasted_iota(jnp.int32, (WIDE, WIDE), 0).astype(F32) + 1.0
+    nothing = jnp.zeros((WIDE, WIDE), BF16)
     entry = jnp.zeros((GROUP_CH, wide), F32)
     for source in range(states.shape[0]):
         entry = entry + weights[source:source + 1, :] * states[source].astype(F32)
     for s in range(wide // WIDE):
         here = slice(s * WIDE, (s + 1) * WIDE)
         rate = params[RATE:RATE + 1, here]
-        spread = jnp.concatenate([entry[:, here]] * (WIDE // GROUP_CH), axis=0)
-        spread = jnp.where(own, spread, 0.0).astype(BF16)
-        lead = jnp.exp(-rate * time)
-        for b in range(rows // TALL):
-            part = pl.ds(b * TALL, TALL)
-            faded = (lead * jnp.exp(-rate * float(b * TALL))).astype(BF16)
-            carried = lax.dot_general(faded, spread, (((1,), (1,)), ((), ())), preferred_element_type=F32)
+        lead = (params[AMP:AMP + 1, here] * jnp.exp(-rate * time)).astype(BF16)
+        for b in range(rows // WIDE):
+            part = pl.ds(b * WIDE, WIDE)
+            state = carry[b * GROUP_CH:(b + 1) * GROUP_CH, here] + jnp.exp(-rate * float(b * WIDE)) * entry[:, here]
+            spread = jnp.concatenate([state.astype(BF16)] * (WIDE // GROUP_CH), axis=0)
+            carried = lax.dot_general(lead, jnp.where(own, spread, nothing), (((1,), (1,)), ((), ())),
+                                      preferred_element_type=F32)
             mixed = v[part, here].astype(F32) * (y[part, here].astype(F32) + carried)
             mixed_out[part, here] = mixed.astype(BF16)
             square = mixed * mixed
@@ -258,7 +278,7 @@
             energy_out[:, begin:begin + LANES] = jnp.sum(energy[pl.ds(begin, LANES), :].T, axis=0, keepdims=True)
 
 
-def join(y, v, states, weights, params):
+def join(y, v, carry, states, weights, params):
     rows, chans = y.shape
     wide = math.gcd(chans, JOIN_STRIP)
     column = lambda height: pl.BlockSpec((height, wide), lambda i: (0, i))
@@ -266,14 +286,14 @@
         join_kernel,
         grid=(chans // wide,),
         out_shape=(jax.ShapeDtypeStruct((rows, chans), BF16), jax.ShapeDtypeStruct((1, rows), F32)),
-        in_specs=[column(rows), column(rows), pl.BlockSpec((states.shape[0], GROUP_CH, wide), lambda i: (0, 0, i)),
+        in_specs=[column(rows), column(rows), column(carry.shape[0]), pl.BlockSpec((states.shape[0], GROUP_CH, wide), lambda i: (0, 0, i)),
                   column(weights.shape[0]), column(params.shape[0])],
         out_specs=(column(rows), pl.BlockSpec((1, rows), lambda i: (0, 0))),
         scratch_shapes=[pltpu.VMEM((rows, LANES), F32)],
         compiler_params=pltpu.CompilerParams(vmem_limit_bytes=JOIN_VMEM),
         cost_estimate=pl.CostEstimate(flops=2 * rows * chans * WIDE, bytes_accessed=6 * rows * chans, transcendentals=0),
         name="join",
-    )(y, v, states, weights, params)
+    )(y, v, carry, states, weights, params)
 
 
 def scale_kernel(mixed, energy, gain, out, *, width):
@@ -314,14 +334,16 @@
         decays.reshape(1, chans), amplitude.reshape(1, chans), skip_gain[None, :],
         jnp.zeros((16 - SHORT - 3, chans), F32)], axis=0)
     halo = passed_along(edge(queries, key_rows, value_rows, short_filter), "context", 1)
-    y, state = mix(queries, key_rows, value_rows, halo, params, medium_filter.T.astype(F32))
+    first, keys_t = (pltpu.with_memory_space_constraint(array, pltpu.VMEM)
+                     for array in gate(queries, key_rows, value_rows, params))
+    y, carry, state = mix(first, keys_t, halo, queries, key_rows, value_rows, params, medium_filter.T.astype(F32))
     states = lax.all_gather(state, "context")
     count = lax.axis_size("context")
     gap = (lax.axis_index("context") - 1 - jnp.arange(count)).astype(F32)[:, None]
-    weights = jnp.where(gap >= 0.0, params[AMP:AMP + 1] * jnp.exp(-params[RATE:RATE + 1] * (jnp.maximum(gap, 0.0) * rows)), 0.0)
+    weights = jnp.where(gap >= 0.0, jnp.exp(-params[RATE:RATE + 1] * (jnp.maximum(gap, 0.0) * rows)), 0.0)
     y = pltpu.with_memory_space_constraint(y, pltpu.VMEM)
-    mixed, energy = join(y, value_rows, states, weights, params)
-    energy = lax.all_gather(energy, "tensor", tiled=True)
+    mixed, energy = join(y, value_rows, carry, states, weights, params)
+    energy = summed(energy, "tensor")
     mixed = pltpu.with_memory_space_constraint(mixed, pltpu.VMEM)
     return scaled(mixed, energy, norm_gain[None, :], width)
 

time: 90.2 us -> 74 us (0.82)
  blocking collectives: 32.8 us -> 11.3 us
  starting transfers between devices: 2.39 us -> 6.69 us
  waiting for transfers between devices: 0.06 us -> 4.03 us
  Pallas kernels: 52.5 us -> 49.4 us
    all_gather x1 -> x0, blocking collectives: 13.3 us -> none  [local(): energy = lax.all_gather(energy, 'tensor', tiled=True)]
    all_gather x1, blocking collectives: 19.4 us -> 11.3 us  [local(): states = lax.all_gather(state, 'context')]
    ppermute x0 -> x2, starting transfers between devices: none -> 4.3 us  [summed(): lax.ppermute(value, axis, [(source, source ^ step) for source in range(co...]
    ppermute x0 -> x2, waiting for transfers between devices: none -> 4.03 us  [summed(): lax.ppermute(value, axis, [(source, source ^ step) for source in range(co...]
    pallas_call x1 -> x2, Pallas kernels: 35.9 us -> 32.9 us  [the longest x1 16.6 us: gate(): pl.pallas_call(gate_kernel, grid=(chans // GATE_STRIP,), out_shape=(jax.S...]
  transfers between devices with their start and end apart: 1 -> 3, of which waited for: 1 -> 2; matrix products, arithmetic and copies ran while one was open for 2% -> 2% of each run, Pallas kernels for 0% -> 23%
where the time goes in v5:
time: 74 us; the launch traced here: 73.7 us
  Pallas kernels  49.4 us (67%)
  blocking collectives  11.3 us (15%)
  starting transfers between devices  6.69 us (9%)
  waiting for transfers between devices  4.03 us (5%)
  local copies, waits for them, and re-layouts  1.89 us (3%)
    pallas_call x1, Pallas kernels, gate(): pl.pallas_call(gate_kernel, grid=(chans // GATE_STRIP,), out_shape=(jax.S...  16.6 us
    pallas_call x1, Pallas kernels, mix(): pl.pallas_call(mix_kernel, grid=(chans // MIX_STRIP,), out_shape=(jax.Sha...  16.3 us
    all_gather x1, blocking collectives, local(): states = lax.all_gather(state, 'context')  11.3 us
    pallas_call x1, Pallas kernels, join(): pl.pallas_call(join_kernel, grid=(chans // wide,), out_shape=(jax.ShapeDt...  8.62 us
    pallas_call x1, Pallas kernels, scaled(): pl.pallas_call(functools.partial(scale_kernel, width=width), grid=(rows /...  4.59 us
    ppermute x2, starting transfers between devices, summed(): lax.ppermute(value, axis, [(source, source ^ step) for source in range(co...  4.3 us
    ppermute x2, waiting for transfers between devices, summed(): lax.ppermute(value, axis, [(source, source ^ step) for source in range(co...  4.03 us
    pallas_call x1, Pallas kernels, edge(): pl.pallas_call(edge_kernel, grid=(EDGE_PARTS,), out_shape=jax.ShapeDtypeS...  3.33 us
  transfers between devices with their start and end apart: 3, of which 2 were waited for; matrix products, arithmetic and copies ran while one was open for 2% of the time, Pallas kernels for 23%

profile of v5, /device:TPU:0, one launch (start us, length us, event | category | flops | bytes accessed | tf_op | source)
XLA Modules:
  0.0 73.7 jit_solution(15938897581458716131)
XLA Ops:
  0.0 0.7 copy-done
  0.7 3.3 %edge.1 = bf16[144,2048]{1,0:T(8,128)(2,1)S(1)} custom-call(bf16[2048,2048]{1,0:T(8,128)(2,1)} %q.5, bf16[2048,2048]{1,0:T(8,128)(2,1)} %k.5, bf16[2048,2048]{1,0:T(8,128)(2,1)} %v.7, f32[7,128]{1,0:T(8,128)S(1)} %copy-done), custom_call_target="tpu_custom_call" | custom-call | tf_op jit(solution)/shard_map/edge/pallas_call | solution.py:67
  4.0 2.4 %collective-permute-start = (bf16[144,2048]{1,0:T(8,128)(2,1)S(1)}, bf16[144,2048]{1,0:T(8,128)(2,1)S(1)}, u32[]{:S(2)}, u32[]{:S(2)}) collective-permute-start(bf16[144,2048]{1,0:T(8,128)(2,1)S(1)} %edge.1), channel_id=1, source_target_pairs={{0,4},{4,8},{8,12},{12,16},{16,20},{20,24},{24,28},{1,5},{5,9},{9,... | collective-permute-start | bytes 1769480 | tf_op jit(solution)/shard_map/ppermute | solution.py:35
  6.5 0.1 copy.15
  6.7 0.1 copy.13
  6.8 0.1 copy.14
  6.9 0.1 reshape.32
  7.0 0.2 broadcast_in_dim.25
  7.1 0.3 reshape.30
  7.4 0.1 reshape.31
  7.5 0.1 copy.16
  7.6 0.1 neg.16
  7.7 0.1 concatenate.3.params
  7.8 16.6 %gate.1 = (bf16[2048,2048]{1,0:T(8,128)(2,1)S(1)}, bf16[2048,2048]{1,0:T(8,128)(2,1)S(1)}) custom-call(bf16[2048,2048]{1,0:T(8,128)(2,1)} %q.5, bf16[2048,2048]{1,0:T(8,128)(2,1)} %k.5, bf16[2048,2048]{1,0:T(8,128)(2,1)} %v.7, f32[16,2048]{1,0:T(8,128)S(1)} %concatenate.3.params), custom_call_target="tpu_custom_call" | custom-call | flops 268435456 | bytes 41943040 | tf_op jit(solution)/shard_map/gate/pallas_call | solution.py:102
  24.4 0.1 exponential_select_fusion.weights
  24.5 0.0 collective-permute-done.halo
  24.5 16.3 %mix.1 = (bf16[2048,2048]{1,0:T(8,128)(2,1)S(1)}, f32[128,2048]{1,0:T(8,128)S(1)}, bf16[16,2048]{1,0:T(8,128)(2,1)S(1)}) custom-call(bf16[2048,2048]{1,0:T(8,128)(2,1)S(1)} %get-tuple-element.12.first, bf16[2048,2048]{1,0:T(8,128)(2,1)S(1)} %get-tuple-element.13.keys_t, bf16[144,2048]{1,0:T(8,128)(2,1)S(1)} %collective-permute-done.halo, ...), custom_call_target="tpu_custom_call" | custom-call | flops 8589934592 | bytes 25165824 | tf_op jit(solution)/shard_map/mix/pallas_call | solution.py:225
  40.8 11.3 %all-gather = bf16[128,2048]{1,0:T(8,128)(2,1)S(1)} all-gather(bf16[16,2048]{1,0:T(8,128)(2,1)S(1)} %get-tuple-element.16), channel_id=2, replica_groups=mesh['context'=8,'tensor'=4] {'context'}, dimensions={0}, use_global_device_ids=true | all-gather | bytes 589824 | tf_op jit(solution)/shard_map/all_gather | solution.py:340
  52.1 8.6 %join.1 = (bf16[2048,2048]{1,0:T(8,128)(2,1)S(1)}, f32[1,2048]{1,0:T(1,128)S(1)}) custom-call(bf16[2048,2048]{1,0:T(8,128)(2,1)S(1)} %get-tuple-element.14.y, bf16[2048,2048]{1,0:T(8,128)(2,1)} %v.7, f32[128,2048]{1,0:T(8,128)S(1)} %get-tuple-element.15.carry, bf16[8,16,2048]{2,1,0:T(8,128)(2,1)S(1)} %bitcast.5, ...), custom_call_target="tpu_custom_call" | custom-call | flops 2147483648 | bytes 25165824 | tf_op jit(solution)/shard_map/join/pallas_call | solution.py:285
  60.7 1.6 %collective-permute-start.1 = (f32[1,2048]{1,0:T(1,128)S(1)}, f32[1,2048]{1,0:T(1,128)S(1)}, u32[]{:S(2)}, u32[]{:S(2)}) collective-permute-start(f32[1,2048]{1,0:T(1,128)S(1)} %get-tuple-element.18), channel_id=1, source_target_pairs={{0,1},{1,0},{2,3},{3,2},{4,5},{5,4},{6,7},{7,6},{8,9},{9,8},{10,11... | collective-permute-start | bytes 24584 | tf_op jit(solution)/shard_map/ppermute | solution.py:121
  62.4 2.1 %collective-permute-done.1 = f32[1,2048]{1,0:T(1,128)S(1)} collective-permute-done((f32[1,2048]{1,0:T(1,128)S(1)}, f32[1,2048]{1,0:T(1,128)S(1)}, u32[]{:S(2)}, u32[]{:S(2)}) %collective-permute-start.1) | collective-permute-done | bytes 8224 | tf_op jit(solution)/shard_map/ppermute | solution.py:121
  64.5 2.7 %collective-permute-start.2 = (f32[1,2048]{1,0:T(1,128)S(1)}, f32[1,2048]{1,0:T(1,128)S(1)}, u32[]{:S(2)}, u32[]{:S(2)}) collective-permute-start(f32[1,2048]{1,0:T(1,128)S(1)} %add.7), channel_id=1, source_target_pairs={{0,2},{1,3},{2,0},{3,1},{4,6},{5,7},{6,4},{7,5},{8,10},{9,11},{10,... | collective-permute-start | bytes 24584 | tf_op jit(solution)/shard_map/ppermute | solution.py:121
  67.1 2.0 %collective-permute-done.2 = f32[1,2048]{1,0:T(1,128)S(1)} collective-permute-done((f32[1,2048]{1,0:T(1,128)S(1)}, f32[1,2048]{1,0:T(1,128)S(1)}, u32[]{:S(2)}, u32[]{:S(2)}) %collective-permute-start.2) | collective-permute-done | bytes 8224 | tf_op jit(solution)/shard_map/ppermute | solution.py:121
  69.1 4.6 %scale.1 = bf16[2048,2048]{1,0:T(8,128)(2,1)} custom-call(bf16[2048,2048]{1,0:T(8,128)(2,1)S(1)} %get-tuple-element.17.mixed, f32[1,2048]{1,0:T(1,128)S(1)} %add.8.energy, f32[1,2048]{1,0:T(1,128)S(1)} %bitcast.6), custom_call_target="tpu_custom_call" | custom-call | tf_op jit(solution)/shard_map/scale/pallas_call | solution.py:315
  (20 shorter events, 0.1 us)
Async XLA Ops:
  0.0 0.7 copy-start
  0.7 5.8 %copy-start.3 = (bf16[128,128]{1,0:T(8,128)(2,1)S(1)}, bf16[128,128]{1,0:T(8,128)(2,1)}, u32[]{:S(2)}) copy-start(bf16[128,128]{1,0:T(8,128)(2,1)} %param.13) | copy-start | bytes 98308
  0.7 5.9 %copy-start.4 = (f32[128,16]{0,1:T(8,128)S(1)}, f32[128,16]{0,1:T(8,128)}, u32[]{:S(2)}) copy-start(f32[128,16]{0,1:T(8,128)} %param.14) | copy-start | bytes 24580
  0.7 5.9 %copy-start.6 = (f32[128,16]{0,1:T(8,128)S(1)}, f32[128,16]{0,1:T(8,128)}, u32[]{:S(2)}) copy-start(f32[128,16]{0,1:T(8,128)} %param.15) | copy-start | bytes 24580
  0.7 6.3 %copy-start.1 = (f32[7,128]{1,0:T(8,128)S(1)}, f32[7,128]{1,0:T(8,128)}, u32[]{:S(2)}) copy-start(f32[7,128]{1,0:T(8,128)} %short_filter.1) | copy-start | bytes 10756
  0.7 7.0 %copy-start.5 = (f32[2048]{0:T(1024)S(1)}, f32[2048]{0:T(1024)}, u32[]{:S(2)}) copy-start(f32[2048]{0:T(1024)} %param.16) | copy-start | bytes 24580
  4.0 20.5 %collective-permute-start = (bf16[144,2048]{1,0:T(8,128)(2,1)S(1)}, bf16[144,2048]{1,0:T(8,128)(2,1)S(1)}, u32[]{:S(2)}, u32[]{:S(2)}) collective-permute-start(bf16[144,2048]{1,0:T(8,128)(2,1)S(1)} %edge.1), channel_id=1, source_target_pairs={{0,4},{4,8},{8,12},{12,16},{16,20},{20,24},{24,28},{1,5},{5,9},{9,... | collective-permute-start | bytes 1769480 | tf_op jit(solution)/shard_map/ppermute | solution.py:35
  52.1 17.0 %copy-start.2 = (f32[2048]{0:T(1024)S(1)}, f32[2048]{0:T(1024)}, u32[]{:S(2)}) copy-start(f32[2048]{0:T(1024)} %param.17) | copy-start | bytes 24580
  60.7 3.7 %collective-permute-start.1 = (f32[1,2048]{1,0:T(1,128)S(1)}, f32[1,2048]{1,0:T(1,128)S(1)}, u32[]{:S(2)}, u32[]{:S(2)}) collective-permute-start(f32[1,2048]{1,0:T(1,128)S(1)} %get-tuple-element.18), channel_id=1, source_target_pairs={{0,1},{1,0},{2,3},{3,2},{4,5},{5,4},{6,7},{7,6},{8,9},{9,8},{10,11... | collective-permute-start | bytes 24584 | tf_op jit(solution)/shard_map/ppermute | solution.py:121
  64.5 4.6 %collective-permute-start.2 = (f32[1,2048]{1,0:T(1,128)S(1)}, f32[1,2048]{1,0:T(1,128)S(1)}, u32[]{:S(2)}, u32[]{:S(2)}) collective-permute-start(f32[1,2048]{1,0:T(1,128)S(1)} %add.7), channel_id=1, source_target_pairs={{0,2},{1,3},{2,0},{3,1},{4,6},{5,7},{6,4},{7,5},{8,10},{9,11},{10,... | collective-permute-start | bytes 24584 | tf_op jit(solution)/shard_map/ppermute | solution.py:121

commit v6 on v5

--- a/solution.py
+++ b/solution.py
@@ -17,7 +17,6 @@
 RATE, AMP, SKIP = SHORT, SHORT + 1, SHORT + 2
 GATE_STRIP = 256
 MIX_STRIP = 256
-EDGE_PARTS = 1
 JOIN_STRIP = 512
 MIX_VMEM = 24 << 20
 JOIN_VMEM = 24 << 20
@@ -35,42 +34,49 @@
     return lax.ppermute(value, axis, [(source, source + steps) for source in range(count - steps)])
 
 
-def edge_kernel(q, k, v, short_filter, halo_out, gated):
-    rows, wide = q.shape
-    begin = rows - LANES
+def edge_kernel(q, k, v, short_filter, halo_out, q_tail, k_tail, v_tail, gated, arrived):
+    rows, chans = q.shape
+    parts = arrived.shape[0]
+    wide = chans // parts
     pack = wide // GROUP_CH
+    tail = LANES + 16
+    copies = []
+    for s in range(parts):
+        here = pl.ds(s * wide, wide)
+        copies.append([pltpu.make_async_copy(source.at[pl.ds(rows - tail, tail), here], target.at[:, here], arrived.at[s, n])
+                       for n, (source, target) in enumerate(((q, q_tail), (k, k_tail), (v, v_tail)))])
+        for copy in copies[-1]:
+            copy.start()
     spread = (lax.broadcasted_iota(jnp.int32, (pack, wide), 1) // GROUP_CH
               == lax.broadcasted_iota(jnp.int32, (pack, wide), 0)).astype(F32)
-    taps = jnp.dot(short_filter[...], spread, precision=lax.Precision.HIGHEST, preferred_element_type=F32)
-    kv = k[begin - 16:, :].astype(F32) * v[begin - 16:, :].astype(F32)
-    gated[...] = kv
-    total = taps[0:1, :] * gated[16:, :]
-    for delay in range(1, SHORT):
-        total = total + taps[delay:delay + 1, :] * gated[pl.ds(16 - delay, LANES), :]
-    halo_out[0:LANES, :] = (q[begin:, :].astype(F32) * total).astype(BF16)
-    last = kv[LANES + 8:, :]
-    high = last.astype(BF16).astype(F32)
-    halo_out[LANES:LANES + 16, :] = jnp.concatenate([high, last - high], axis=0).astype(BF16)
+    for s in range(parts):
+        here = pl.ds(s * wide, wide)
+        taps = jnp.dot(short_filter[:, s * pack:(s + 1) * pack], spread, precision=lax.Precision.HIGHEST,
+                       preferred_element_type=F32)
+        for copy in copies[s]:
+            copy.wait()
+        kv = k_tail[:, here].astype(F32) * v_tail[:, here].astype(F32)
+        gated[...] = kv
+        total = taps[0:1, :] * kv[16:, :]
+        for delay in range(1, SHORT):
+            total = total + taps[delay:delay + 1, :] * gated[pl.ds(16 - delay, LANES), :]
+        halo_out[0:LANES, here] = (q_tail[16:, here].astype(F32) * total).astype(BF16)
+        last = kv[LANES + 8:, :]
+        high = last.astype(BF16).astype(F32)
+        halo_out[LANES:LANES + 16, here] = jnp.concatenate([high, last - high], axis=0).astype(BF16)
 
 
 def edge(q, k, v, short_filter):
-    rows, chans = q.shape
-    wide = chans // EDGE_PARTS
-    tall = math.gcd(rows, 256)
-    last = pl.BlockSpec((tall, wide), lambda i: (rows // tall - 1, i))
-    column = lambda height, width: pl.BlockSpec((height, width), lambda i: (0, i))
-    if wide // GROUP_CH % LANES:
-        short_filter = short_filter.reshape(SHORT, EDGE_PARTS, wide // GROUP_CH).transpose(1, 0, 2)
-        tap_spec = pl.BlockSpec((pl.Squeezed(), SHORT, wide // GROUP_CH), lambda i: (i, 0, 0))
-    else:
-        tap_spec = column(SHORT, wide // GROUP_CH)
+    chans = q.shape[1]
+    parts = chans // math.gcd(chans, 512)
+    far = pl.BlockSpec(memory_space=pltpu.HBM)
     return pl.pallas_call(
         edge_kernel,
-        grid=(EDGE_PARTS,),
         out_shape=jax.ShapeDtypeStruct((LANES + 16, chans), BF16),
-        in_specs=[last] * 3 + [tap_spec],
-        out_specs=column(LANES + 16, wide),
-        scratch_shapes=[pltpu.VMEM((LANES + 16, wide), F32)],
+        in_specs=[far] * 3 + [pl.BlockSpec(memory_space=pltpu.VMEM)],
+        out_specs=pl.BlockSpec(memory_space=pltpu.VMEM),
+        scratch_shapes=[pltpu.VMEM((LANES + 16, chans), BF16)] * 3 + [
+            pltpu.VMEM((LANES + 16, chans // parts), F32), pltpu.SemaphoreType.DMA((parts, 3))],
         compiler_params=pltpu.CompilerParams(vmem_limit_bytes=MIX_VMEM),
         name="edge",
     )(q, k, v, short_filter)
@@ -123,16 +129,16 @@
     return value
 
 
-def mix_kernel(first, keys_t, halo, q, k, v, params, medium_taps, y_out, carry_out, state_out, *scratch):
+def mix_kernel(first, keys_t, halo, q, k, v, params, medium_taps, seconds_out, carry_out, state_out, *scratch):
     strips = first.shape[0] // LANES
     for s in range(strips):
         here = slice(s * LANES, (s + 1) * LANES)
         mix_strip(first.at[here, :], keys_t.at[here, :], halo.at[:, here], q.at[:, here], k.at[:, here], v.at[:, here],
                   params.at[:, here], medium_taps.at[s * PACK:(s + 1) * PACK, :],
-                  y_out.at[:, here], carry_out.at[:, here], state_out.at[:, here], *scratch[4 * s:4 * s + 4])
-
-
-def mix_strip(first_t, key_t, halo, q, k, v, late_params, medium_taps, y_out, carry_out, state_out, y_t, seconds,
+                  seconds_out.at[here, :], carry_out.at[:, here], state_out.at[:, here], *scratch[2 * s:2 * s + 2])
+
+
+def mix_strip(first_t, key_t, halo, q, k, v, late_params, medium_taps, seconds, carry_out, state_out,
               gated, start):
     rows = first_t.shape[1]
     blocks = rows // WIDE
@@ -140,9 +146,7 @@
     row_i = lax.broadcasted_iota(jnp.int32, (LANES, LANES), 0)
     col_i = lax.broadcasted_iota(jnp.int32, (LANES, LANES), 1)
     causal = col_i >= row_i
-    zero = jnp.zeros((LANES, LANES), BF16)
     time_down = lax.broadcasted_iota(jnp.int32, (WIDE, LANES), 0).astype(F32)
-    time_along = lax.broadcasted_iota(jnp.int32, (LANES, WIDE), 1).astype(F32)
     lane_group = lax.broadcasted_iota(jnp.int32, (WIDE, LANES), 1) // MODES
     late = late_params[...]
 
@@ -189,6 +193,23 @@
         carry_out[b * GROUP_CH:(b + 1) * GROUP_CH, :] = state
         state = decay * state + sums[b * GROUP_CH:(b + 1) * GROUP_CH, :]
     state_out[...] = state.astype(BF16)
+
+
+def long_kernel(seconds, params, y_out, *scratch):
+    for s in range(seconds.shape[0] // LANES):
+        here = slice(s * LANES, (s + 1) * LANES)
+        long_strip(seconds.at[here, :], params.at[:, here], y_out.at[:, here], scratch[s])
+
+
+def long_strip(seconds, params, y_out, y_t):
+    rows = y_out.shape[0]
+    blocks = rows // WIDE
+    row_i = lax.broadcasted_iota(jnp.int32, (LANES, LANES), 0)
+    col_i = lax.broadcasted_iota(jnp.int32, (LANES, LANES), 1)
+    causal = col_i >= row_i
+    zero = jnp.zeros((LANES, LANES), BF16)
+    time_along = lax.broadcasted_iota(jnp.int32, (LANES, WIDE), 1).astype(F32)
+    late = params[...]
 
     down = lambda row: jnp.broadcast_to(late[row:row + 1, :], (LANES, LANES)).T
     rate_t, amp_t, skip_t = down(RATE), down(AMP), down(SKIP)
@@ -225,24 +246,35 @@
     return pl.pallas_call(
         mix_kernel,
         grid=(chans // MIX_STRIP,),
-        out_shape=(jax.ShapeDtypeStruct((rows, chans), BF16), jax.ShapeDtypeStruct((carried, chans), F32),
+        out_shape=(pltpu.HBM((chans, rows), BF16), jax.ShapeDtypeStruct((carried, chans), F32),
                    jax.ShapeDtypeStruct((GROUP_CH, chans), BF16)),
         in_specs=[down(MIX_STRIP, rows)] * 2 + [column(halo.shape[0])] + [column(16)] * 3 + [
             column(params.shape[0]), down(MIX_STRIP // GROUP_CH, LANES)],
-        out_specs=(column(rows), column(carried), column(GROUP_CH)),
-        scratch_shapes=[
-            pltpu.VMEM((LANES, rows), BF16),
-            pltpu.VMEM((LANES, PACK * WIDE), BF16),
-            pltpu.VMEM((24, LANES), F32),
-            pltpu.VMEM((LANES, 2 * LANES), BF16),
-        ] * (MIX_STRIP // LANES),
-        compiler_params=pltpu.CompilerParams(vmem_limit_bytes=JOIN_VMEM),
-        cost_estimate=pl.CostEstimate(flops=8 * rows * chans * WIDE, bytes_accessed=6 * rows * chans, transcendentals=0),
+        out_specs=(down(MIX_STRIP, rows), column(carried), column(GROUP_CH)),
+        scratch_shapes=[pltpu.VMEM((24, LANES), F32), pltpu.VMEM((LANES, 2 * LANES), BF16)] * (MIX_STRIP // LANES),
+        compiler_params=pltpu.CompilerParams(vmem_limit_bytes=MIX_VMEM),
+        cost_estimate=pl.CostEstimate(flops=6 * rows * chans * WIDE, bytes_accessed=6 * rows * chans, transcendentals=0),
         name="mix",
     )(first, keys_t, halo, q, k, v, params, medium_taps)
 
 
-def join_kernel(y, v, carry, states, weights, params, mixed_out, energy_out, energy):
+def long_conv(seconds, params):
+    chans, rows = seconds.shape
+    column = lambda height: pl.BlockSpec((height, MIX_STRIP), lambda i: (0, i))
+    return pl.pallas_call(
+        long_kernel,
+        grid=(chans // MIX_STRIP,),
+        out_shape=jax.ShapeDtypeStruct((rows, chans), BF16),
+        in_specs=[pl.BlockSpec((MIX_STRIP, rows), lambda i: (i, 0)), column(params.shape[0])],
+        out_specs=column(rows),
+        scratch_shapes=[pltpu.VMEM((LANES, rows), BF16)] * (MIX_STRIP // LANES),
+        compiler_params=pltpu.CompilerParams(vmem_limit_bytes=MIX_VMEM),
+        cost_estimate=pl.CostEstimate(flops=6 * rows * chans * WIDE, bytes_accessed=10 * rows * chans, transcendentals=0),
+        name="long",
+    )(seconds, params)
+
+
+def join_kernel(y, v, carry, entry, params, mixed_out, energy_out, energy):
     rows, wide = y.shape
     step = pl.program_id(0)
 
@@ -254,9 +286,6 @@
            == lax.broadcasted_iota(jnp.int32, (WIDE, WIDE), 1) // MODES)
     time = lax.broadcasted_iota(jnp.int32, (WIDE, WIDE), 0).astype(F32) + 1.0
     nothing = jnp.zeros((WIDE, WIDE), BF16)
-    entry = jnp.zeros((GROUP_CH, wide), F32)
-    for source in range(states.shape[0]):
-        entry = entry + weights[source:source + 1, :] * states[source].astype(F32)
     for s in range(wide // WIDE):
         here = slice(s * WIDE, (s + 1) * WIDE)
         rate = params[RATE:RATE + 1, here]
@@ -278,7 +307,7 @@
             energy_out[:, begin:begin + LANES] = jnp.sum(energy[pl.ds(begin, LANES), :].T, axis=0, keepdims=True)
 
 
-def join(y, v, carry, states, weights, params):
+def join(y, v, carry, entry, params):
     rows, chans = y.shape
     wide = math.gcd(chans, JOIN_STRIP)
     column = lambda height: pl.BlockSpec((height, wide), lambda i: (0, i))
@@ -286,14 +315,14 @@
         join_kernel,
         grid=(chans // wide,),
         out_shape=(jax.ShapeDtypeStruct((rows, chans), BF16), jax.ShapeDtypeStruct((1, rows), F32)),
-        in_specs=[column(rows), column(rows), column(carry.shape[0]), pl.BlockSpec((states.shape[0], GROUP_CH, wide), lambda i: (0, 0, i)),
-                  column(weights.shape[0]), column(params.shape[0])],
+        in_specs=[column(rows), column(rows), column(carry.shape[0]),
+                  column(GROUP_CH), column(params.shape[0])],
         out_specs=(column(rows), pl.BlockSpec((1, rows), lambda i: (0, 0))),
         scratch_shapes=[pltpu.VMEM((rows, LANES), F32)],
         compiler_params=pltpu.CompilerParams(vmem_limit_bytes=JOIN_VMEM),
         cost_estimate=pl.CostEstimate(flops=2 * rows * chans * WIDE, bytes_accessed=6 * rows * chans, transcendentals=0),
         name="join",
-    )(y, v, carry, states, weights, params)
+    )(y, v, carry, entry, params)
 
 
 def scale_kernel(mixed, energy, gain, out, *, width):
@@ -336,13 +365,14 @@
     halo = passed_along(edge(queries, key_rows, value_rows, short_filter), "context", 1)
     first, keys_t = (pltpu.with_memory_space_constraint(array, pltpu.VMEM)
                      for array in gate(queries, key_rows, value_rows, params))
-    y, carry, state = mix(first, keys_t, halo, queries, key_rows, value_rows, params, medium_filter.T.astype(F32))
-    states = lax.all_gather(state, "context")
-    count = lax.axis_size("context")
-    gap = (lax.axis_index("context") - 1 - jnp.arange(count)).astype(F32)[:, None]
-    weights = jnp.where(gap >= 0.0, jnp.exp(-params[RATE:RATE + 1] * (jnp.maximum(gap, 0.0) * rows)), 0.0)
+    seconds, carry, state = mix(first, keys_t, halo, queries, key_rows, value_rows, params, medium_filter.T.astype(F32))
+    entry = jnp.zeros(state.shape, F32)
+    for away in range(1, lax.axis_size("context")):
+        fade = jnp.exp(-params[RATE:RATE + 1] * float(rows * (away - 1)))
+        entry = entry + fade * passed_along(state, "context", away).astype(F32)
+    y = long_conv(pltpu.with_memory_space_constraint(seconds, pltpu.HBM), params)
     y = pltpu.with_memory_space_constraint(y, pltpu.VMEM)
-    mixed, energy = join(y, value_rows, carry, states, weights, params)
+    mixed, energy = join(y, value_rows, carry, entry, params)
     energy = summed(energy, "tensor")
     mixed = pltpu.with_memory_space_constraint(mixed, pltpu.VMEM)
     return scaled(mixed, energy, norm_gain[None, :], width)

time: 74 us -> 83.8 us (1.13)
  starting transfers between devices: 6.69 us -> 20.9 us
  blocking collectives: 11.3 us -> 0 us
  Pallas kernels: 49.4 us -> 54.8 us
  local copies, waits for them, and re-layouts: 1.89 us -> 2.99 us
    ppermute x1 -> x8, starting transfers between devices: 2.39 us -> 16.6 us  [passed_along(): lax.ppermute(value, axis, [(source, source + steps) for source in range(c...]
    all_gather x1 -> x0, blocking collectives: 11.3 us -> none  [local(): states = lax.all_gather(state, 'context')]
    pallas_call x2 -> x3, Pallas kernels: 19.6 us -> 25 us  [the longest x1 11.3 us: long_conv(): pl.pallas_call(long_kernel, grid=(chans // MIX_STRIP,), out_shape=jax.Sha...]
    exp x0 -> x14, local copies, waits for them, and re-layouts: none -> 1.28 us  [local(): fade = jnp.exp(-params[RATE:RATE + 1] * float(rows * (away - 1)))]
  transfers between devices with their start and end apart: 3 -> 10, of which waited for: 2 -> 2; matrix products, arithmetic and copies ran while one was open for 2% -> 3% of each run, Pallas kernels for 23% -> 34%
where the time goes in v6:
time: 83.8 us; the launch traced here: 83.2 us
  Pallas kernels  54.8 us (65%)
  starting transfers between devices  20.9 us (25%)
  waiting for transfers between devices  4.05 us (5%)
  local copies, waits for them, and re-layouts  2.99 us (4%)
    pallas_call x1, Pallas kernels, gate(): pl.pallas_call(gate_kernel, grid=(chans // GATE_STRIP,), out_shape=(jax.S...  16.6 us
    ppermute x8, starting transfers between devices, passed_along(): lax.ppermute(value, axis, [(source, source + steps) for source in range(c...  16.6 us
    pallas_call x1, Pallas kernels, long_conv(): pl.pallas_call(long_kernel, grid=(chans // MIX_STRIP,), out_shape=jax.Sha...  11.3 us
    pallas_call x1, Pallas kernels, mix(): pl.pallas_call(mix_kernel, grid=(chans // MIX_STRIP,), out_shape=(pltpu.H...  10.5 us
    pallas_call x1, Pallas kernels, join(): pl.pallas_call(join_kernel, grid=(chans // wide,), out_shape=(jax.ShapeDt...  8.58 us
    pallas_call x1, Pallas kernels, scaled(): pl.pallas_call(functools.partial(scale_kernel, width=width), grid=(rows /...  4.59 us
    ppermute x2, starting transfers between devices, summed(): lax.ppermute(value, axis, [(source, source ^ step) for source in range(co...  4.3 us
    ppermute x2, waiting for transfers between devices, summed(): lax.ppermute(value, axis, [(source, source ^ step) for source in range(co...  4.03 us
  transfers between devices with their start and end apart: 10, of which 2 were waited for; matrix products, arithmetic and copies ran while one was open for 3% of the time, Pallas kernels for 34%

profile of v6, /device:TPU:0, one launch (start us, length us, event | category | flops | bytes accessed | tf_op | source)
XLA Modules:
  0.0 83.2 jit_solution(12932147299288842795)
XLA Ops:
  0.0 0.7 copy-done
  0.7 3.3 %edge.1 = bf16[144,2048]{1,0:T(8,128)(2,1)S(1)} custom-call(bf16[2048,2048]{1,0:T(8,128)(2,1)} %q.5, bf16[2048,2048]{1,0:T(8,128)(2,1)} %k.5, bf16[2048,2048]{1,0:T(8,128)(2,1)} %v.7, f32[7,128]{1,0:T(8,128)S(1)} %copy-done), custom_call_target="tpu_custom_call" | custom-call | tf_op jit(solution)/shard_map/edge/pallas_call | solution.py:73
  4.0 2.4 %collective-permute-start = (bf16[144,2048]{1,0:T(8,128)(2,1)S(1)}, bf16[144,2048]{1,0:T(8,128)(2,1)S(1)}, u32[]{:S(2)}, u32[]{:S(2)}) collective-permute-start(bf16[144,2048]{1,0:T(8,128)(2,1)S(1)} %edge.1), channel_id=1, source_target_pairs={{0,4},{4,8},{8,12},{12,16},{16,20},{20,24},{24,28},{1,5},{5,9},{9,... | collective-permute-start | bytes 1769480 | tf_op jit(solution)/shard_map/ppermute | solution.py:34
  6.4 0.1 copy.15
  6.5 0.1 copy.13
  7.0 0.2 broadcast_in_dim.12
  7.2 0.3 reshape.84
  7.5 16.6 %gate.1 = (bf16[2048,2048]{1,0:T(8,128)(2,1)S(1)}, bf16[2048,2048]{1,0:T(8,128)(2,1)S(1)}) custom-call(bf16[2048,2048]{1,0:T(8,128)(2,1)} %q.5, bf16[2048,2048]{1,0:T(8,128)(2,1)} %k.5, bf16[2048,2048]{1,0:T(8,128)(2,1)} %v.7, f32[16,2048]{1,0:T(8,128)S(1)} %concatenate.3.params), custom_call_target="tpu_custom_call" | custom-call | flops 268435456 | bytes 41943040 | tf_op jit(solution)/shard_map/gate/pallas_call | solution.py:108
  24.2 10.5 %mix.1 = (bf16[2048,2048]{1,0:T(8,128)(2,1)}, f32[128,2048]{1,0:T(8,128)S(1)}, bf16[16,2048]{1,0:T(8,128)(2,1)S(1)}) custom-call(bf16[2048,2048]{1,0:T(8,128)(2,1)S(1)} %get-tuple-element.12.first, bf16[2048,2048]{1,0:T(8,128)(2,1)S(1)} %get-tuple-element.13.keys_t, bf16[144,2048]{1,0:T(8,128)(2,1)S(1)} %collective-permute-done.halo, bf16[2048,2048]{1,0:T(8,128)(2,1)} %q.5, ...), custom_call_target="tpu_custom_call" | custom-call | flops 6442450944 | bytes 25165824 | tf_op jit(solution)/shard_map/mix/pallas_call | solution.py:246
  34.7 4.1 %collective-permute-start.7 = (bf16[16,2048]{1,0:T(8,128)(2,1)S(1)}, bf16[16,2048]{1,0:T(8,128)(2,1)S(1)}, u32[]{:S(2)}, u32[]{:S(2)}) collective-permute-start(bf16[16,2048]{1,0:T(8,128)(2,1)S(1)} %get-tuple-element.16), channel_id=1, source_target_pairs={{0,28},{1,29},{2,30},{3,31}} | collective-permute-start | bytes 196616 | tf_op jit(solution)/shard_map/ppermute | solution.py:34
  38.8 1.9 %collective-permute-start.6 = (bf16[16,2048]{1,0:T(8,128)(2,1)S(1)}, bf16[16,2048]{1,0:T(8,128)(2,1)S(1)}, u32[]{:S(2)}, u32[]{:S(2)}) collective-permute-start(bf16[16,2048]{1,0:T(8,128)(2,1)S(1)} %get-tuple-element.16), channel_id=1, source_target_pairs={{0,24},{4,28},{1,25},{5,29},{2,26},{6,30},{3,27},{7,31}} | collective-permute-start | bytes 196616 | tf_op jit(solution)/shard_map/ppermute | solution.py:34
  42.0 1.3 %collective-permute-start.5 = (bf16[16,2048]{1,0:T(8,128)(2,1)S(1)}, bf16[16,2048]{1,0:T(8,128)(2,1)S(1)}, u32[]{:S(2)}, u32[]{:S(2)}) collective-permute-start(bf16[16,2048]{1,0:T(8,128)(2,1)S(1)} %get-tuple-element.16), channel_id=1, source_target_pairs={{0,20},{4,24},{8,28},{1,21},{5,25},{9,29},{2,22},{6,26},{10,30},{3... | collective-permute-start | bytes 196616 | tf_op jit(solution)/shard_map/ppermute | solution.py:34
  43.3 1.3 %collective-permute-start.4 = (bf16[16,2048]{1,0:T(8,128)(2,1)S(1)}, bf16[16,2048]{1,0:T(8,128)(2,1)S(1)}, u32[]{:S(2)}, u32[]{:S(2)}) collective-permute-start(bf16[16,2048]{1,0:T(8,128)(2,1)S(1)} %get-tuple-element.16), channel_id=1, source_target_pairs={{0,16},{4,20},{8,24},{12,28},{1,17},{5,21},{9,25},{13,29},{2,18},{... | collective-permute-start | bytes 196616 | tf_op jit(solution)/shard_map/ppermute | solution.py:34
  44.6 1.6 %collective-permute-start.3 = (bf16[16,2048]{1,0:T(8,128)(2,1)S(1)}, bf16[16,2048]{1,0:T(8,128)(2,1)S(1)}, u32[]{:S(2)}, u32[]{:S(2)}) collective-permute-start(bf16[16,2048]{1,0:T(8,128)(2,1)S(1)} %get-tuple-element.16), channel_id=1, source_target_pairs={{0,12},{4,16},{8,20},{12,24},{16,28},{1,13},{5,17},{9,21},{13,25},... | collective-permute-start | bytes 196616 | tf_op jit(solution)/shard_map/ppermute | solution.py:34
  46.2 2.7 %collective-permute-start.2 = (bf16[16,2048]{1,0:T(8,128)(2,1)S(1)}, bf16[16,2048]{1,0:T(8,128)(2,1)S(1)}, u32[]{:S(2)}, u32[]{:S(2)}) collective-permute-start(bf16[16,2048]{1,0:T(8,128)(2,1)S(1)} %get-tuple-element.16), channel_id=1, source_target_pairs={{0,8},{4,12},{8,16},{12,20},{16,24},{20,28},{1,9},{5,13},{9,17},{1... | collective-permute-start | bytes 196616 | tf_op jit(solution)/shard_map/ppermute | solution.py:34
  48.9 1.3 %collective-permute-start.1 = (bf16[16,2048]{1,0:T(8,128)(2,1)S(1)}, bf16[16,2048]{1,0:T(8,128)(2,1)S(1)}, u32[]{:S(2)}, u32[]{:S(2)}) collective-permute-start(bf16[16,2048]{1,0:T(8,128)(2,1)S(1)} %get-tuple-element.16), channel_id=1, source_target_pairs={{0,4},{4,8},{8,12},{12,16},{16,20},{20,24},{24,28},{1,5},{5,9},{9,... | collective-permute-start | bytes 196616 | tf_op jit(solution)/shard_map/ppermute | solution.py:34
  50.2 11.3 %long.1.y = bf16[2048,2048]{1,0:T(8,128)(2,1)S(1)} custom-call(bf16[2048,2048]{1,0:T(8,128)(2,1)} %get-tuple-element.14.seconds, f32[16,2048]{1,0:T(8,128)S(1)} %concatenate.3.params), custom_call_target="tpu_custom_call" | custom-call | flops 6442450944 | bytes 41943040 | tf_op jit(solution)/shard_map/long/pallas_call | solution.py:264
  61.5 0.1 multiply_add_fusion.entry
  61.6 8.6 %join.1 = (bf16[2048,2048]{1,0:T(8,128)(2,1)S(1)}, f32[1,2048]{1,0:T(1,128)S(1)}) custom-call(bf16[2048,2048]{1,0:T(8,128)(2,1)S(1)} %long.1.y, bf16[2048,2048]{1,0:T(8,128)(2,1)} %v.7, f32[128,2048]{1,0:T(8,128)S(1)} %get-tuple-element.15.carry, f32[16,2048]{1,0:T(8,128)S(1)} %multiply_add_fusion.entry, f32[16,2048]{1,0:T(8,128)S(1)} %concatenate.3.params), custom_call_target="tpu_custom_call" | custom-call | flops 2147483648 | bytes 25165824 | tf_op jit(solution)/shard_map/join/pallas_call | solution.py:314
  70.2 1.6 %collective-permute-start.8 = (f32[1,2048]{1,0:T(1,128)S(1)}, f32[1,2048]{1,0:T(1,128)S(1)}, u32[]{:S(2)}, u32[]{:S(2)}) collective-permute-start(f32[1,2048]{1,0:T(1,128)S(1)} %get-tuple-element.18), channel_id=1, source_target_pairs={{0,1},{1,0},{2,3},{3,2},{4,5},{5,4},{6,7},{7,6},{8,9},{9,8},{10,11... | collective-permute-start | bytes 24584 | tf_op jit(solution)/shard_map/ppermute | solution.py:127
  71.9 2.1 %collective-permute-done.8 = f32[1,2048]{1,0:T(1,128)S(1)} collective-permute-done((f32[1,2048]{1,0:T(1,128)S(1)}, f32[1,2048]{1,0:T(1,128)S(1)}, u32[]{:S(2)}, u32[]{:S(2)}) %collective-permute-start.8) | collective-permute-done | bytes 8224 | tf_op jit(solution)/shard_map/ppermute | solution.py:127
  74.0 2.7 %collective-permute-start.9 = (f32[1,2048]{1,0:T(1,128)S(1)}, f32[1,2048]{1,0:T(1,128)S(1)}, u32[]{:S(2)}, u32[]{:S(2)}) collective-permute-start(f32[1,2048]{1,0:T(1,128)S(1)} %add.30), channel_id=1, source_target_pairs={{0,2},{1,3},{2,0},{3,1},{4,6},{5,7},{6,4},{7,5},{8,10},{9,11},{10,... | collective-permute-start | bytes 24584 | tf_op jit(solution)/shard_map/ppermute | solution.py:127
  76.6 2.0 %collective-permute-done.9 = f32[1,2048]{1,0:T(1,128)S(1)} collective-permute-done((f32[1,2048]{1,0:T(1,128)S(1)}, f32[1,2048]{1,0:T(1,128)S(1)}, u32[]{:S(2)}, u32[]{:S(2)}) %collective-permute-start.9) | collective-permute-done | bytes 8224 | tf_op jit(solution)/shard_map/ppermute | solution.py:127
  78.6 4.6 %scale.1 = bf16[2048,2048]{1,0:T(8,128)(2,1)} custom-call(bf16[2048,2048]{1,0:T(8,128)(2,1)S(1)} %get-tuple-element.17.mixed, f32[1,2048]{1,0:T(1,128)S(1)} %add.31.energy, f32[1,2048]{1,0:T(1,128)S(1)} %bitcast.4), custom_call_target="tpu_custom_call" | custom-call | tf_op jit(solution)/shard_map/scale/pallas_call | solution.py:344
  (44 shorter events, 1.8 us)
Async XLA Ops:
  0.0 0.7 copy-start
  0.7 5.7 %copy-start.4 = (bf16[128,128]{1,0:T(8,128)(2,1)S(1)}, bf16[128,128]{1,0:T(8,128)(2,1)}, u32[]{:S(2)}) copy-start(bf16[128,128]{1,0:T(8,128)(2,1)} %param.13) | copy-start | bytes 98308
  0.7 5.8 %copy-start.3 = (f32[128,16]{0,1:T(8,128)S(1)}, f32[128,16]{0,1:T(8,128)}, u32[]{:S(2)}) copy-start(f32[128,16]{0,1:T(8,128)} %param.14) | copy-start | bytes 24580
  0.7 6.0 %copy-start.5 = (f32[128,16]{0,1:T(8,128)S(1)}, f32[128,16]{0,1:T(8,128)}, u32[]{:S(2)}) copy-start(f32[128,16]{0,1:T(8,128)} %param.15) | copy-start | bytes 24580
  0.7 6.3 %copy-start.1 = (f32[7,128]{1,0:T(8,128)S(1)}, f32[7,128]{1,0:T(8,128)}, u32[]{:S(2)}) copy-start(f32[7,128]{1,0:T(8,128)} %short_filter.1) | copy-start | bytes 10756
  0.7 6.7 %copy-start.6 = (f32[2048]{0:T(1024)S(1)}, f32[2048]{0:T(1024)}, u32[]{:S(2)}) copy-start(f32[2048]{0:T(1024)} %param.16) | copy-start | bytes 24580
  4.0 20.2 %collective-permute-start = (bf16[144,2048]{1,0:T(8,128)(2,1)S(1)}, bf16[144,2048]{1,0:T(8,128)(2,1)S(1)}, u32[]{:S(2)}, u32[]{:S(2)}) collective-permute-start(bf16[144,2048]{1,0:T(8,128)(2,1)S(1)} %edge.1), channel_id=1, source_target_pairs={{0,4},{4,8},{8,12},{12,16},{16,20},{20,24},{24,28},{1,5},{5,9},{9,... | collective-permute-start | bytes 1769480 | tf_op jit(solution)/shard_map/ppermute | solution.py:34
  34.7 11.5 %collective-permute-start.7 = (bf16[16,2048]{1,0:T(8,128)(2,1)S(1)}, bf16[16,2048]{1,0:T(8,128)(2,1)S(1)}, u32[]{:S(2)}, u32[]{:S(2)}) collective-permute-start(bf16[16,2048]{1,0:T(8,128)(2,1)S(1)} %get-tuple-element.16), channel_id=1, source_target_pairs={{0,28},{1,29},{2,30},{3,31}} | collective-permute-start | bytes 196616 | tf_op jit(solution)/shard_map/ppermute | solution.py:34
  38.8 10.1 %collective-permute-start.6 = (bf16[16,2048]{1,0:T(8,128)(2,1)S(1)}, bf16[16,2048]{1,0:T(8,128)(2,1)S(1)}, u32[]{:S(2)}, u32[]{:S(2)}) collective-permute-start(bf16[16,2048]{1,0:T(8,128)(2,1)S(1)} %get-tuple-element.16), channel_id=1, source_target_pairs={{0,24},{4,28},{1,25},{5,29},{2,26},{6,30},{3,27},{7,31}} | collective-permute-start | bytes 196616 | tf_op jit(solution)/shard_map/ppermute | solution.py:34
  42.0 19.5 %collective-permute-start.5 = (bf16[16,2048]{1,0:T(8,128)(2,1)S(1)}, bf16[16,2048]{1,0:T(8,128)(2,1)S(1)}, u32[]{:S(2)}, u32[]{:S(2)}) collective-permute-start(bf16[16,2048]{1,0:T(8,128)(2,1)S(1)} %get-tuple-element.16), channel_id=1, source_target_pairs={{0,20},{4,24},{8,28},{1,21},{5,25},{9,29},{2,22},{6,26},{10,30},{3... | collective-permute-start | bytes 196616 | tf_op jit(solution)/shard_map/ppermute | solution.py:34
  43.3 18.2 %collective-permute-start.4 = (bf16[16,2048]{1,0:T(8,128)(2,1)S(1)}, bf16[16,2048]{1,0:T(8,128)(2,1)S(1)}, u32[]{:S(2)}, u32[]{:S(2)}) collective-permute-start(bf16[16,2048]{1,0:T(8,128)(2,1)S(1)} %get-tuple-element.16), channel_id=1, source_target_pairs={{0,16},{4,20},{8,24},{12,28},{1,17},{5,21},{9,25},{13,29},{2,18},{... | collective-permute-start | bytes 196616 | tf_op jit(solution)/shard_map/ppermute | solution.py:34
  44.6 16.9 %collective-permute-start.3 = (bf16[16,2048]{1,0:T(8,128)(2,1)S(1)}, bf16[16,2048]{1,0:T(8,128)(2,1)S(1)}, u32[]{:S(2)}, u32[]{:S(2)}) collective-permute-start(bf16[16,2048]{1,0:T(8,128)(2,1)S(1)} %get-tuple-element.16), channel_id=1, source_target_pairs={{0,12},{4,16},{8,20},{12,24},{16,28},{1,13},{5,17},{9,21},{13,25},... | collective-permute-start | bytes 196616 | tf_op jit(solution)/shard_map/ppermute | solution.py:34
  46.2 15.3 %collective-permute-start.2 = (bf16[16,2048]{1,0:T(8,128)(2,1)S(1)}, bf16[16,2048]{1,0:T(8,128)(2,1)S(1)}, u32[]{:S(2)}, u32[]{:S(2)}) collective-permute-start(bf16[16,2048]{1,0:T(8,128)(2,1)S(1)} %get-tuple-element.16), channel_id=1, source_target_pairs={{0,8},{4,12},{8,16},{12,20},{16,24},{20,28},{1,9},{5,13},{9,17},{1... | collective-permute-start | bytes 196616 | tf_op jit(solution)/shard_map/ppermute | solution.py:34
  48.9 12.6 %collective-permute-start.1 = (bf16[16,2048]{1,0:T(8,128)(2,1)S(1)}, bf16[16,2048]{1,0:T(8,128)(2,1)S(1)}, u32[]{:S(2)}, u32[]{:S(2)}) collective-permute-start(bf16[16,2048]{1,0:T(8,128)(2,1)S(1)} %get-tuple-element.16), channel_id=1, source_target_pairs={{0,4},{4,8},{8,12},{12,16},{16,20},{20,24},{24,28},{1,5},{5,9},{9,... | collective-permute-start | bytes 196616 | tf_op jit(solution)/shard_map/ppermute | solution.py:34
  61.6 17.0 %copy-start.2 = (f32[2048]{0:T(1024)S(1)}, f32[2048]{0:T(1024)}, u32[]{:S(2)}) copy-start(f32[2048]{0:T(1024)} %param.17) | copy-start | bytes 24580
  70.2 3.7 %collective-permute-start.8 = (f32[1,2048]{1,0:T(1,128)S(1)}, f32[1,2048]{1,0:T(1,128)S(1)}, u32[]{:S(2)}, u32[]{:S(2)}) collective-permute-start(f32[1,2048]{1,0:T(1,128)S(1)} %get-tuple-element.18), channel_id=1, source_target_pairs={{0,1},{1,0},{2,3},{3,2},{4,5},{5,4},{6,7},{7,6},{8,9},{9,8},{10,11... | collective-permute-start | bytes 24584 | tf_op jit(solution)/shard_map/ppermute | solution.py:127
  74.0 4.6 %collective-permute-start.9 = (f32[1,2048]{1,0:T(1,128)S(1)}, f32[1,2048]{1,0:T(1,128)S(1)}, u32[]{:S(2)}, u32[]{:S(2)}) collective-permute-start(f32[1,2048]{1,0:T(1,128)S(1)} %add.30), channel_id=1, source_target_pairs={{0,2},{1,3},{2,0},{3,1},{4,6},{5,7},{6,4},{7,5},{8,10},{9,11},{10,... | collective-permute-start | bytes 24584 | tf_op jit(solution)/shard_map/ppermute | solution.py:127

commit v7 on v5

--- a/solution.py
+++ b/solution.py
@@ -16,7 +16,7 @@
 SHORT = 7
 RATE, AMP, SKIP = SHORT, SHORT + 1, SHORT + 2
 GATE_STRIP = 256
-MIX_STRIP = 256
+MIX_STRIP = 512
 EDGE_PARTS = 1
 JOIN_STRIP = 512
 MIX_VMEM = 24 << 20
@@ -59,7 +59,7 @@
     tall = math.gcd(rows, 256)
     last = pl.BlockSpec((tall, wide), lambda i: (rows // tall - 1, i))
     column = lambda height, width: pl.BlockSpec((height, width), lambda i: (0, i))
-    if wide // GROUP_CH % LANES:
+    if EDGE_PARTS > 1 and wide // GROUP_CH % LANES:
         short_filter = short_filter.reshape(SHORT, EDGE_PARTS, wide // GROUP_CH).transpose(1, 0, 2)
         tap_spec = pl.BlockSpec((pl.Squeezed(), SHORT, wide // GROUP_CH), lambda i: (i, 0, 0))
     else:
@@ -199,10 +199,12 @@
         chans = pl.ds(g * GROUP_CH, GROUP_CH)
         mine = slice(g * MODES, (g + 1) * MODES)
         profile = jnp.sum(power[mine], axis=0, keepdims=True)
-        turned = pltpu.roll(jnp.broadcast_to(profile, (LANES, WIDE)), 0, 1, stride=1, stride_axis=0)
-        near = jnp.where(causal, turned[:, :LANES], 0.0).astype(BF16)
-        pieces = [jnp.concatenate([near, turned[:, LANES:].astype(BF16)], axis=1),
-                  jnp.concatenate([zero, near], axis=1)]
+        soon, late_part = (
+            pltpu.roll(jnp.broadcast_to(profile[:, half * LANES:(half + 1) * LANES], (LANES, LANES)),
+                       0, 1, stride=1, stride_axis=0) for half in range(2))
+        near = jnp.where(causal, soon, 0.0).astype(BF16)
+        far = jnp.where(causal, late_part, soon).astype(BF16)
+        pieces = [jnp.concatenate([near, far], axis=1), jnp.concatenate([zero, near], axis=1)]
         second = seconds[:, g * WIDE:(g + 1) * WIDE]
         y = jnp.dot(second, jnp.concatenate(pieces, axis=0), preferred_element_type=F32)
         gain = both(skip_t[g * GROUP_CH:(g + 1) * GROUP_CH, :])
@@ -333,7 +335,7 @@
         jnp.repeat(short_filter, GROUP_CH, axis=1),
         decays.reshape(1, chans), amplitude.reshape(1, chans), skip_gain[None, :],
         jnp.zeros((16 - SHORT - 3, chans), F32)], axis=0)
-    halo = passed_along(edge(queries, key_rows, value_rows, short_filter), "context", 1)
+    halo = passed_along(edge(queries, key_rows, value_rows, pltpu.with_memory_space_constraint(short_filter, pltpu.HBM)), "context", 1)
     first, keys_t = (pltpu.with_memory_space_constraint(array, pltpu.VMEM)
                      for array in gate(queries, key_rows, value_rows, params))
     y, carry, state = mix(first, keys_t, halo, queries, key_rows, value_rows, params, medium_filter.T.astype(F32))

time: 74 us -> 71.4 us (0.965)
  Pallas kernels: 49.4 us -> 47.5 us
    pallas_call x1, Pallas kernels: 16.3 us -> 14.3 us  [mix(): pl.pallas_call(mix_kernel, grid=(chans // MIX_STRIP,), out_shape=(jax.Sha...]
where the time goes in v7:
time: 71.4 us; the launch traced here: 71 us
  Pallas kernels  47.5 us (67%)
  blocking collectives  11.3 us (16%)
  starting transfers between devices  6.69 us (9%)
  waiting for transfers between devices  4.03 us (6%)
  local copies, waits for them, and re-layouts  1.2 us (2%)
    pallas_call x1, Pallas kernels, gate(): pl.pallas_call(gate_kernel, grid=(chans // GATE_STRIP,), out_shape=(jax.S...  16.6 us
    pallas_call x1, Pallas kernels, mix(): pl.pallas_call(mix_kernel, grid=(chans // MIX_STRIP,), out_shape=(jax.Sha...  14.3 us
    all_gather x1, blocking collectives, local(): states = lax.all_gather(state, 'context')  11.3 us
    pallas_call x1, Pallas kernels, join(): pl.pallas_call(join_kernel, grid=(chans // wide,), out_shape=(jax.ShapeDt...  8.62 us
    pallas_call x1, Pallas kernels, scaled(): pl.pallas_call(functools.partial(scale_kernel, width=width), grid=(rows /...  4.59 us
    ppermute x2, starting transfers between devices, summed(): lax.ppermute(value, axis, [(source, source ^ step) for source in range(co...  4.3 us
    ppermute x2, waiting for transfers between devices, summed(): lax.ppermute(value, axis, [(source, source ^ step) for source in range(co...  4.03 us
    pallas_call x1, Pallas kernels, edge(): pl.pallas_call(edge_kernel, grid=(EDGE_PARTS,), out_shape=jax.ShapeDtypeS...  3.32 us
  transfers between devices with their start and end apart: 3, of which 2 were waited for; matrix products, arithmetic and copies ran while one was open for 2% of the time, Pallas kernels for 23%

profile of v7, /device:TPU:0, one launch (start us, length us, event | category | flops | bytes accessed | tf_op | source)
XLA Modules:
  0.0 71.0 jit_solution(13543700321991115544)
XLA Ops:
  0.0 3.3 %edge.1 = bf16[144,2048]{1,0:T(8,128)(2,1)S(1)} custom-call(bf16[2048,2048]{1,0:T(8,128)(2,1)} %q.5, bf16[2048,2048]{1,0:T(8,128)(2,1)} %k.5, bf16[2048,2048]{1,0:T(8,128)(2,1)} %v.7, f32[7,128]{1,0:T(8,128)} %short_filter.1), custom_call_target="tpu_custom_call" | custom-call | tf_op jit(solution)/shard_map/edge/pallas_call | solution.py:67
  3.3 2.4 %collective-permute-start = (bf16[144,2048]{1,0:T(8,128)(2,1)S(1)}, bf16[144,2048]{1,0:T(8,128)(2,1)S(1)}, u32[]{:S(2)}, u32[]{:S(2)}) collective-permute-start(bf16[144,2048]{1,0:T(8,128)(2,1)S(1)} %edge.1), channel_id=1, source_target_pairs={{0,4},{4,8},{8,12},{12,16},{16,20},{20,24},{24,28},{1,5},{5,9},{9,... | collective-permute-start | bytes 1769480 | tf_op jit(solution)/shard_map/ppermute | solution.py:35
  5.8 0.1 copy.15
  5.9 0.0 copy-done.2
  5.9 0.1 copy.13
  6.0 0.1 copy.14
  6.1 0.1 reshape.32
  6.3 0.2 broadcast_in_dim.25
  6.4 0.3 reshape.30
  6.7 0.1 reshape.31
  6.8 0.1 copy.16
  6.9 0.1 neg.16
  7.0 0.1 concatenate.3.params
  7.1 16.6 %gate.1 = (bf16[2048,2048]{1,0:T(8,128)(2,1)S(1)}, bf16[2048,2048]{1,0:T(8,128)(2,1)S(1)}) custom-call(bf16[2048,2048]{1,0:T(8,128)(2,1)} %q.5, bf16[2048,2048]{1,0:T(8,128)(2,1)} %k.5, bf16[2048,2048]{1,0:T(8,128)(2,1)} %v.7, f32[16,2048]{1,0:T(8,128)S(1)} %concatenate.3.params), custom_call_target="tpu_custom_call" | custom-call | flops 268435456 | bytes 41943040 | tf_op jit(solution)/shard_map/gate/pallas_call | solution.py:102
  23.7 0.1 exponential_select_fusion.weights
  23.8 0.0 collective-permute-done.halo
  23.8 14.3 %mix.1 = (bf16[2048,2048]{1,0:T(8,128)(2,1)S(1)}, f32[128,2048]{1,0:T(8,128)S(1)}, bf16[16,2048]{1,0:T(8,128)(2,1)S(1)}) custom-call(bf16[2048,2048]{1,0:T(8,128)(2,1)S(1)} %get-tuple-element.12.first, bf16[2048,2048]{1,0:T(8,128)(2,1)S(1)} %get-tuple-element.13.keys_t, bf16[144,2048]{1,0:T(8,128)(2,1)S(1)} %collective-permute-done.halo, ...), custom_call_target="tpu_custom_call" | custom-call | flops 8589934592 | bytes 25165824 | tf_op jit(solution)/shard_map/mix/pallas_call | solution.py:227
  38.1 11.3 %all-gather = bf16[128,2048]{1,0:T(8,128)(2,1)S(1)} all-gather(bf16[16,2048]{1,0:T(8,128)(2,1)S(1)} %get-tuple-element.16), channel_id=2, replica_groups=mesh['context'=8,'tensor'=4] {'context'}, dimensions={0}, use_global_device_ids=true | all-gather | bytes 589824 | tf_op jit(solution)/shard_map/all_gather | solution.py:342
  49.4 8.6 %join.1 = (bf16[2048,2048]{1,0:T(8,128)(2,1)S(1)}, f32[1,2048]{1,0:T(1,128)S(1)}) custom-call(bf16[2048,2048]{1,0:T(8,128)(2,1)S(1)} %get-tuple-element.14.y, bf16[2048,2048]{1,0:T(8,128)(2,1)} %v.7, f32[128,2048]{1,0:T(8,128)S(1)} %get-tuple-element.15.carry, bf16[8,16,2048]{2,1,0:T(8,128)(2,1)S(1)} %bitcast.5, ...), custom_call_target="tpu_custom_call" | custom-call | flops 2147483648 | bytes 25165824 | tf_op jit(solution)/shard_map/join/pallas_call | solution.py:287
  58.1 1.6 %collective-permute-start.1 = (f32[1,2048]{1,0:T(1,128)S(1)}, f32[1,2048]{1,0:T(1,128)S(1)}, u32[]{:S(2)}, u32[]{:S(2)}) collective-permute-start(f32[1,2048]{1,0:T(1,128)S(1)} %get-tuple-element.18), channel_id=1, source_target_pairs={{0,1},{1,0},{2,3},{3,2},{4,5},{5,4},{6,7},{7,6},{8,9},{9,8},{10,11... | collective-permute-start | bytes 24584 | tf_op jit(solution)/shard_map/ppermute | solution.py:121
  59.7 2.1 %collective-permute-done.1 = f32[1,2048]{1,0:T(1,128)S(1)} collective-permute-done((f32[1,2048]{1,0:T(1,128)S(1)}, f32[1,2048]{1,0:T(1,128)S(1)}, u32[]{:S(2)}, u32[]{:S(2)}) %collective-permute-start.1) | collective-permute-done | bytes 8224 | tf_op jit(solution)/shard_map/ppermute | solution.py:121
  61.8 2.7 %collective-permute-start.2 = (f32[1,2048]{1,0:T(1,128)S(1)}, f32[1,2048]{1,0:T(1,128)S(1)}, u32[]{:S(2)}, u32[]{:S(2)}) collective-permute-start(f32[1,2048]{1,0:T(1,128)S(1)} %add.7), channel_id=1, source_target_pairs={{0,2},{1,3},{2,0},{3,1},{4,6},{5,7},{6,4},{7,5},{8,10},{9,11},{10,... | collective-permute-start | bytes 24584 | tf_op jit(solution)/shard_map/ppermute | solution.py:121
  64.5 2.0 %collective-permute-done.2 = f32[1,2048]{1,0:T(1,128)S(1)} collective-permute-done((f32[1,2048]{1,0:T(1,128)S(1)}, f32[1,2048]{1,0:T(1,128)S(1)}, u32[]{:S(2)}, u32[]{:S(2)}) %collective-permute-start.2) | collective-permute-done | bytes 8224 | tf_op jit(solution)/shard_map/ppermute | solution.py:121
  66.4 4.6 %scale.1 = bf16[2048,2048]{1,0:T(8,128)(2,1)} custom-call(bf16[2048,2048]{1,0:T(8,128)(2,1)S(1)} %get-tuple-element.17.mixed, f32[1,2048]{1,0:T(1,128)S(1)} %add.8.energy, f32[1,2048]{1,0:T(1,128)S(1)} %bitcast.6), custom_call_target="tpu_custom_call" | custom-call | tf_op jit(solution)/shard_map/scale/pallas_call | solution.py:317
  (18 shorter events, 0.1 us)
Async XLA Ops:
  0.0 6.2 %copy-start.3 = (f32[7,128]{1,0:T(8,128)S(1)}, f32[7,128]{1,0:T(8,128)}, u32[]{:S(2)}) copy-start(f32[7,128]{1,0:T(8,128)} %short_filter.1) | copy-start | bytes 10756
  0.0 5.7 %copy-start.1 = (bf16[128,128]{1,0:T(8,128)(2,1)S(1)}, bf16[128,128]{1,0:T(8,128)(2,1)}, u32[]{:S(2)}) copy-start(bf16[128,128]{1,0:T(8,128)(2,1)} %param.13) | copy-start | bytes 98308
  0.0 5.9 %copy-start.2 = (f32[128,16]{0,1:T(8,128)S(1)}, f32[128,16]{0,1:T(8,128)}, u32[]{:S(2)}) copy-start(f32[128,16]{0,1:T(8,128)} %param.14) | copy-start | bytes 24580
  0.0 5.9 %copy-start.5 = (f32[128,16]{0,1:T(8,128)S(1)}, f32[128,16]{0,1:T(8,128)}, u32[]{:S(2)}) copy-start(f32[128,16]{0,1:T(8,128)} %param.15) | copy-start | bytes 24580
  0.0 7.0 %copy-start.4 = (f32[2048]{0:T(1024)S(1)}, f32[2048]{0:T(1024)}, u32[]{:S(2)}) copy-start(f32[2048]{0:T(1024)} %param.16) | copy-start | bytes 24580
  3.3 20.5 %collective-permute-start = (bf16[144,2048]{1,0:T(8,128)(2,1)S(1)}, bf16[144,2048]{1,0:T(8,128)(2,1)S(1)}, u32[]{:S(2)}, u32[]{:S(2)}) collective-permute-start(bf16[144,2048]{1,0:T(8,128)(2,1)S(1)} %edge.1), channel_id=1, source_target_pairs={{0,4},{4,8},{8,12},{12,16},{16,20},{20,24},{24,28},{1,5},{5,9},{9,... | collective-permute-start | bytes 1769480 | tf_op jit(solution)/shard_map/ppermute | solution.py:35
  49.4 17.0 %copy-start = (f32[2048]{0:T(1024)S(1)}, f32[2048]{0:T(1024)}, u32[]{:S(2)}) copy-start(f32[2048]{0:T(1024)} %param.17) | copy-start | bytes 24580
  58.1 3.7 %collective-permute-start.1 = (f32[1,2048]{1,0:T(1,128)S(1)}, f32[1,2048]{1,0:T(1,128)S(1)}, u32[]{:S(2)}, u32[]{:S(2)}) collective-permute-start(f32[1,2048]{1,0:T(1,128)S(1)} %get-tuple-element.18), channel_id=1, source_target_pairs={{0,1},{1,0},{2,3},{3,2},{4,5},{5,4},{6,7},{7,6},{8,9},{9,8},{10,11... | collective-permute-start | bytes 24584 | tf_op jit(solution)/shard_map/ppermute | solution.py:121
  61.8 4.6 %collective-permute-start.2 = (f32[1,2048]{1,0:T(1,128)S(1)}, f32[1,2048]{1,0:T(1,128)S(1)}, u32[]{:S(2)}, u32[]{:S(2)}) collective-permute-start(f32[1,2048]{1,0:T(1,128)S(1)} %add.7), channel_id=1, source_target_pairs={{0,2},{1,3},{2,0},{3,1},{4,6},{5,7},{6,4},{7,5},{8,10},{9,11},{10,... | collective-permute-start | bytes 24584 | tf_op jit(solution)/shard_map/ppermute | solution.py:121

commit v8 on v7

--- a/solution.py
+++ b/solution.py
@@ -244,7 +244,7 @@
     )(first, keys_t, halo, q, k, v, params, medium_taps)
 
 
-def join_kernel(y, v, carry, states, weights, params, mixed_out, energy_out, energy):
+def join_kernel(y, v, carry, states, weights, params, mixed_out, energy_out, energy, *leads):
     rows, wide = y.shape
     step = pl.program_id(0)
 
@@ -259,20 +259,23 @@
     entry = jnp.zeros((GROUP_CH, wide), F32)
     for source in range(states.shape[0]):
         entry = entry + weights[source:source + 1, :] * states[source].astype(F32)
-    for s in range(wide // WIDE):
-        here = slice(s * WIDE, (s + 1) * WIDE)
-        rate = params[RATE:RATE + 1, here]
-        lead = (params[AMP:AMP + 1, here] * jnp.exp(-rate * time)).astype(BF16)
-        for b in range(rows // WIDE):
-            part = pl.ds(b * WIDE, WIDE)
+    pieces = [slice(s * WIDE, (s + 1) * WIDE) for s in range(wide // WIDE)]
+    rates = [params[RATE:RATE + 1, here] for here in pieces]
+    for here, rate, lead in zip(pieces, rates, leads):
+        lead[...] = (params[AMP:AMP + 1, here] * jnp.exp(-rate * time)).astype(BF16)
+    for b in range(rows // WIDE):
+        part = pl.ds(b * WIDE, WIDE)
+        total = energy[part, :]
+        for here, rate, lead in zip(pieces, rates, leads):
             state = carry[b * GROUP_CH:(b + 1) * GROUP_CH, here] + jnp.exp(-rate * float(b * WIDE)) * entry[:, here]
             spread = jnp.concatenate([state.astype(BF16)] * (WIDE // GROUP_CH), axis=0)
-            carried = lax.dot_general(lead, jnp.where(own, spread, nothing), (((1,), (1,)), ((), ())),
+            carried = lax.dot_general(lead[...], jnp.where(own, spread, nothing), (((1,), (1,)), ((), ())),
                                       preferred_element_type=F32)
             mixed = v[part, here].astype(F32) * (y[part, here].astype(F32) + carried)
             mixed_out[part, here] = mixed.astype(BF16)
             square = mixed * mixed
-            energy[part, :] += square[:, :LANES] + square[:, LANES:]
+            total = total + square[:, :LANES] + square[:, LANES:]
+        energy[part, :] = total
 
     @pl.when(step == pl.num_programs(0) - 1)
     def _():
@@ -291,7 +294,7 @@
         in_specs=[column(rows), column(rows), column(carry.shape[0]), pl.BlockSpec((states.shape[0], GROUP_CH, wide), lambda i: (0, 0, i)),
                   column(weights.shape[0]), column(params.shape[0])],
         out_specs=(column(rows), pl.BlockSpec((1, rows), lambda i: (0, 0))),
-        scratch_shapes=[pltpu.VMEM((rows, LANES), F32)],
+        scratch_shapes=[pltpu.VMEM((rows, LANES), F32)] + [pltpu.VMEM((WIDE, WIDE), BF16)] * (wide // WIDE),
         compiler_params=pltpu.CompilerParams(vmem_limit_bytes=JOIN_VMEM),
         cost_estimate=pl.CostEstimate(flops=2 * rows * chans * WIDE, bytes_accessed=6 * rows * chans, transcendentals=0),
         name="join",

time: 71.4 us -> 71.3 us (level)
  no operation moved by 1% of the time
where the time goes in v8:
time: 71.3 us; the launch traced here: 71 us
  Pallas kernels  47.4 us (66%)
  blocking collectives  11.3 us (16%)
  starting transfers between devices  6.71 us (9%)
  waiting for transfers between devices  4.03 us (6%)
  local copies, waits for them, and re-layouts  1.2 us (2%)
    pallas_call x1, Pallas kernels, gate(): pl.pallas_call(gate_kernel, grid=(chans // GATE_STRIP,), out_shape=(jax.S...  16.6 us
    pallas_call x1, Pallas kernels, mix(): pl.pallas_call(mix_kernel, grid=(chans // MIX_STRIP,), out_shape=(jax.Sha...  14.3 us
    all_gather x1, blocking collectives, local(): states = lax.all_gather(state, 'context')  11.3 us
    pallas_call x1, Pallas kernels, join(): pl.pallas_call(join_kernel, grid=(chans // wide,), out_shape=(jax.ShapeDt...  8.56 us
    pallas_call x1, Pallas kernels, scaled(): pl.pallas_call(functools.partial(scale_kernel, width=width), grid=(rows /...  4.59 us
    ppermute x2, starting transfers between devices, summed(): lax.ppermute(value, axis, [(source, source ^ step) for source in range(co...  4.31 us
    ppermute x2, waiting for transfers between devices, summed(): lax.ppermute(value, axis, [(source, source ^ step) for source in range(co...  4.03 us
    pallas_call x1, Pallas kernels, edge(): pl.pallas_call(edge_kernel, grid=(EDGE_PARTS,), out_shape=jax.ShapeDtypeS...  3.32 us
  transfers between devices with their start and end apart: 3, of which 2 were waited for; matrix products, arithmetic and copies ran while one was open for 2% of the time, Pallas kernels for 23%

profile of v8, /device:TPU:0, one launch (start us, length us, event | category | flops | bytes accessed | tf_op | source)
XLA Modules:
  0.0 71.0 jit_solution(6046102315961290965)
XLA Ops:
  0.0 3.3 %edge.1 = bf16[144,2048]{1,0:T(8,128)(2,1)S(1)} custom-call(bf16[2048,2048]{1,0:T(8,128)(2,1)} %q.5, bf16[2048,2048]{1,0:T(8,128)(2,1)} %k.5, bf16[2048,2048]{1,0:T(8,128)(2,1)} %v.7, f32[7,128]{1,0:T(8,128)} %short_filter.1), custom_call_target="tpu_custom_call" | custom-call | tf_op jit(solution)/shard_map/edge/pallas_call | solution.py:67
  3.3 2.4 %collective-permute-start = (bf16[144,2048]{1,0:T(8,128)(2,1)S(1)}, bf16[144,2048]{1,0:T(8,128)(2,1)S(1)}, u32[]{:S(2)}, u32[]{:S(2)}) collective-permute-start(bf16[144,2048]{1,0:T(8,128)(2,1)S(1)} %edge.1), channel_id=1, source_target_pairs={{0,4},{4,8},{8,12},{12,16},{16,20},{20,24},{24,28},{1,5},{5,9},{9,... | collective-permute-start | bytes 1769480 | tf_op jit(solution)/shard_map/ppermute | solution.py:35
  5.8 0.1 copy.15
  5.9 0.1 copy.13
  6.0 0.1 copy.14
  6.1 0.1 reshape.32
  6.2 0.0 copy-done.3
  6.3 0.2 broadcast_in_dim.25
  6.4 0.3 reshape.30
  6.7 0.1 reshape.31
  6.8 0.1 copy.16
  6.9 0.1 neg.16
  7.0 0.1 concatenate.3.params
  7.1 16.6 %gate.1 = (bf16[2048,2048]{1,0:T(8,128)(2,1)S(1)}, bf16[2048,2048]{1,0:T(8,128)(2,1)S(1)}) custom-call(bf16[2048,2048]{1,0:T(8,128)(2,1)} %q.5, bf16[2048,2048]{1,0:T(8,128)(2,1)} %k.5, bf16[2048,2048]{1,0:T(8,128)(2,1)} %v.7, f32[16,2048]{1,0:T(8,128)S(1)} %concatenate.3.params), custom_call_target="tpu_custom_call" | custom-call | flops 268435456 | bytes 41943040 | tf_op jit(solution)/shard_map/gate/pallas_call | solution.py:102
  23.7 0.1 exponential_select_fusion.weights
  23.8 0.0 collective-permute-done.halo
  23.8 14.3 %mix.1 = (bf16[2048,2048]{1,0:T(8,128)(2,1)S(1)}, f32[128,2048]{1,0:T(8,128)S(1)}, bf16[16,2048]{1,0:T(8,128)(2,1)S(1)}) custom-call(bf16[2048,2048]{1,0:T(8,128)(2,1)S(1)} %get-tuple-element.12.first, bf16[2048,2048]{1,0:T(8,128)(2,1)S(1)} %get-tuple-element.13.keys_t, bf16[144,2048]{1,0:T(8,128)(2,1)S(1)} %collective-permute-done.halo, ...), custom_call_target="tpu_custom_call" | custom-call | flops 8589934592 | bytes 25165824 | tf_op jit(solution)/shard_map/mix/pallas_call | solution.py:227
  38.1 11.3 %all-gather = bf16[128,2048]{1,0:T(8,128)(2,1)S(1)} all-gather(bf16[16,2048]{1,0:T(8,128)(2,1)S(1)} %get-tuple-element.16), channel_id=2, replica_groups=mesh['context'=8,'tensor'=4] {'context'}, dimensions={0}, use_global_device_ids=true | all-gather | bytes 589824 | tf_op jit(solution)/shard_map/all_gather | solution.py:345
  49.4 8.6 %join.1 = (bf16[2048,2048]{1,0:T(8,128)(2,1)S(1)}, f32[1,2048]{1,0:T(1,128)S(1)}) custom-call(bf16[2048,2048]{1,0:T(8,128)(2,1)S(1)} %get-tuple-element.14.y, bf16[2048,2048]{1,0:T(8,128)(2,1)} %v.7, f32[128,2048]{1,0:T(8,128)S(1)} %get-tuple-element.15.carry, bf16[8,16,2048]{2,1,0:T(8,128)(2,1)S(1)} %bitcast.5, ...), custom_call_target="tpu_custom_call" | custom-call | flops 2147483648 | bytes 25165824 | tf_op jit(solution)/shard_map/join/pallas_call | solution.py:290
  58.0 1.7 %collective-permute-start.1 = (f32[1,2048]{1,0:T(1,128)S(1)}, f32[1,2048]{1,0:T(1,128)S(1)}, u32[]{:S(2)}, u32[]{:S(2)}) collective-permute-start(f32[1,2048]{1,0:T(1,128)S(1)} %get-tuple-element.18), channel_id=1, source_target_pairs={{0,1},{1,0},{2,3},{3,2},{4,5},{5,4},{6,7},{7,6},{8,9},{9,8},{10,11... | collective-permute-start | bytes 24584 | tf_op jit(solution)/shard_map/ppermute | solution.py:121
  59.7 2.1 %collective-permute-done.1 = f32[1,2048]{1,0:T(1,128)S(1)} collective-permute-done((f32[1,2048]{1,0:T(1,128)S(1)}, f32[1,2048]{1,0:T(1,128)S(1)}, u32[]{:S(2)}, u32[]{:S(2)}) %collective-permute-start.1) | collective-permute-done | bytes 8224 | tf_op jit(solution)/shard_map/ppermute | solution.py:121
  61.8 2.7 %collective-permute-start.2 = (f32[1,2048]{1,0:T(1,128)S(1)}, f32[1,2048]{1,0:T(1,128)S(1)}, u32[]{:S(2)}, u32[]{:S(2)}) collective-permute-start(f32[1,2048]{1,0:T(1,128)S(1)} %add.7), channel_id=1, source_target_pairs={{0,2},{1,3},{2,0},{3,1},{4,6},{5,7},{6,4},{7,5},{8,10},{9,11},{10,... | collective-permute-start | bytes 24584 | tf_op jit(solution)/shard_map/ppermute | solution.py:121
  64.4 2.0 %collective-permute-done.2 = f32[1,2048]{1,0:T(1,128)S(1)} collective-permute-done((f32[1,2048]{1,0:T(1,128)S(1)}, f32[1,2048]{1,0:T(1,128)S(1)}, u32[]{:S(2)}, u32[]{:S(2)}) %collective-permute-start.2) | collective-permute-done | bytes 8224 | tf_op jit(solution)/shard_map/ppermute | solution.py:121
  66.4 4.6 %scale.1 = bf16[2048,2048]{1,0:T(8,128)(2,1)} custom-call(bf16[2048,2048]{1,0:T(8,128)(2,1)S(1)} %get-tuple-element.17.mixed, f32[1,2048]{1,0:T(1,128)S(1)} %add.8.energy, f32[1,2048]{1,0:T(1,128)S(1)} %bitcast.6), custom_call_target="tpu_custom_call" | custom-call | tf_op jit(solution)/shard_map/scale/pallas_call | solution.py:320
  (18 shorter events, 0.1 us)
Async XLA Ops:
  0.0 6.2 %copy-start.3 = (f32[7,128]{1,0:T(8,128)S(1)}, f32[7,128]{1,0:T(8,128)}, u32[]{:S(2)}) copy-start(f32[7,128]{1,0:T(8,128)} %short_filter.1) | copy-start | bytes 10756
  0.0 5.7 %copy-start.1 = (bf16[128,128]{1,0:T(8,128)(2,1)S(1)}, bf16[128,128]{1,0:T(8,128)(2,1)}, u32[]{:S(2)}) copy-start(bf16[128,128]{1,0:T(8,128)(2,1)} %param.13) | copy-start | bytes 98308
  0.0 5.9 %copy-start.2 = (f32[128,16]{0,1:T(8,128)S(1)}, f32[128,16]{0,1:T(8,128)}, u32[]{:S(2)}) copy-start(f32[128,16]{0,1:T(8,128)} %param.14) | copy-start | bytes 24580
  0.0 5.9 %copy-start.5 = (f32[128,16]{0,1:T(8,128)S(1)}, f32[128,16]{0,1:T(8,128)}, u32[]{:S(2)}) copy-start(f32[128,16]{0,1:T(8,128)} %param.15) | copy-start | bytes 24580
  0.0 7.0 %copy-start.4 = (f32[2048]{0:T(1024)S(1)}, f32[2048]{0:T(1024)}, u32[]{:S(2)}) copy-start(f32[2048]{0:T(1024)} %param.16) | copy-start | bytes 24580
  3.3 20.5 %collective-permute-start = (bf16[144,2048]{1,0:T(8,128)(2,1)S(1)}, bf16[144,2048]{1,0:T(8,128)(2,1)S(1)}, u32[]{:S(2)}, u32[]{:S(2)}) collective-permute-start(bf16[144,2048]{1,0:T(8,128)(2,1)S(1)} %edge.1), channel_id=1, source_target_pairs={{0,4},{4,8},{8,12},{12,16},{16,20},{20,24},{24,28},{1,5},{5,9},{9,... | collective-permute-start | bytes 1769480 | tf_op jit(solution)/shard_map/ppermute | solution.py:35
  49.4 16.9 %copy-start = (f32[2048]{0:T(1024)S(1)}, f32[2048]{0:T(1024)}, u32[]{:S(2)}) copy-start(f32[2048]{0:T(1024)} %param.17) | copy-start | bytes 24580
  58.0 3.7 %collective-permute-start.1 = (f32[1,2048]{1,0:T(1,128)S(1)}, f32[1,2048]{1,0:T(1,128)S(1)}, u32[]{:S(2)}, u32[]{:S(2)}) collective-permute-start(f32[1,2048]{1,0:T(1,128)S(1)} %get-tuple-element.18), channel_id=1, source_target_pairs={{0,1},{1,0},{2,3},{3,2},{4,5},{5,4},{6,7},{7,6},{8,9},{9,8},{10,11... | collective-permute-start | bytes 24584 | tf_op jit(solution)/shard_map/ppermute | solution.py:121
  61.8 4.6 %collective-permute-start.2 = (f32[1,2048]{1,0:T(1,128)S(1)}, f32[1,2048]{1,0:T(1,128)S(1)}, u32[]{:S(2)}, u32[]{:S(2)}) collective-permute-start(f32[1,2048]{1,0:T(1,128)S(1)} %add.7), channel_id=1, source_target_pairs={{0,2},{1,3},{2,0},{3,1},{4,6},{5,7},{6,4},{7,5},{8,10},{9,11},{10,... | collective-permute-start | bytes 24584 | tf_op jit(solution)/shard_map/ppermute | solution.py:121
